TPU v7x, 256 devices: a whole 4x4x8 slice. The times are simulated.
256 devices in a mesh: dp: 64 (over x_hi, z, y), tensor: 4 (over x_lo, core).
Axes of the slice: x: 4 (x_hi: 2, x_lo: 2; x = x_hi * 2 + x_lo), y: 4, z: 8, core: 2. Of those that a mesh axis runs over, the one named last changes fastest.
Arguments:
- queries: bfloat16 [2048, 128, 576], P('dp', 'tensor')
- latent_cache: bfloat16 [2048, 128, 576], P('dp')
- lengths: int32 [2048], P('dp'), may hold values from 2 to 128, as said below
- value_up: bfloat16 [128, 512, 128], P('tensor'), may hold values from -0.25 to 0.25
- out_proj: bfloat16 [16384, 3584], P('tensor', 'dp'), may hold values from -0.046875 to 0.046875
- norm_gain: float32 [3584], replicated, may hold values from 0.25 to 1.75
- routes: int32 [2048, 8], P('dp'), may hold values from 0 to 255, all different within a row; in each aligned block of 32 rows (0 to 31, 32 to 63, ...) at most 4 rows name the same one
- route_weight: float32 [2048, 8], P('dp'), may hold values from 0.2 to 1
- expert_home: int32 [256], replicated, may hold values from -1 to 63, as said below
- w_gate: bfloat16 [64, 3584, 1024], P('dp', None, 'tensor'), may hold values from -0.09375 to 0.09375
- w_up: bfloat16 [64, 3584, 1024], P('dp', None, 'tensor'), may hold values from -0.09375 to 0.09375
- w_down: bfloat16 [64, 1024, 3584], P('dp', 'tensor'), may hold values from -0.1875 to 0.1875
Outputs:
- attended: bfloat16 [2048, 3584], P('dp')
- experts_out: bfloat16 [2048, 3584], P('dp', 'tensor')
Inputs may be any that keep to these rules, and one draw needn't show every extreme that they name: `lengths`: every row has length 2 or more; some row reaches 128. `routes`: the 8 experts of a row differ; in the 32 rows of one index of dp no expert is named more than 4 times, a bound that some block reaches. `expert_home`: each of 0 to 63 is the value of exactly one expert; all other experts hold -1.
All inputs are finite; a program needn't handle non-finite values.
Results may differ from a plain program's by a relative error of at most 0.03.
Values may be sent and summed in bfloat16 or wider, within the bound.
No kernel may reach another device: no remote copies, remote signals or barrier semaphores. Data moves between devices by JAX's collectives and lax.ppermute only.
A program may use at most 128 MiB of HBM per device.

v0:
```python
import jax
import jax.numpy as jnp
from jax import lax
from jax.sharding import PartitionSpec as P

LATENT = 512
MOST = 4


softmax_scale = 192.0 ** (-0.5)
norm_eps = 1e-06


def shards(
    queries,
    latent_cache,
    lengths,
    value_up,
    out_proj,
    norm_gain,
    routes,
    route_weight,
    expert_home,
    w_gate,
    w_up,
    w_down,
):
    rows_here = queries.shape[0]
    owners = lax.axis_size("dp")
    scores = (
        jnp.einsum("rhc,rjc->rhj", queries, latent_cache, preferred_element_type=jnp.float32)
        * softmax_scale
    )
    visible = (
        lax.broadcasted_iota(jnp.int32, (1, 1, latent_cache.shape[1]), 2) < lengths[:, None, None]
    )
    scores = jnp.where(visible, scores, -jnp.inf)
    row_max = jnp.max(scores, axis=2, keepdims=True)
    exponent = jnp.exp(scores - row_max)
    weights = (exponent / jnp.sum(exponent, axis=2, keepdims=True)).astype(jnp.bfloat16)
    latent_out = jnp.einsum(
        "rhj,rjc->rhc", weights, latent_cache[:, :, :LATENT], preferred_element_type=jnp.float32
    ).astype(jnp.bfloat16)
    values = jnp.einsum(
        "rhc,hcv->rhv", latent_out, value_up, preferred_element_type=jnp.float32
    ).astype(jnp.bfloat16)
    values = values.reshape(rows_here, -1)
    partial_out = jnp.dot(
        lax.all_gather(values, "dp", axis=0, tiled=True),
        out_proj,
        preferred_element_type=jnp.float32,
    )
    summed = lax.psum(partial_out.astype(jnp.bfloat16), "tensor")
    attended = lax.all_to_all(summed, "dp", split_axis=0, concat_axis=1, tiled=True)
    attended_f = attended.astype(jnp.float32)
    mean_square = jnp.mean(attended_f * attended_f, axis=1, keepdims=True)
    normed = (attended_f * lax.rsqrt(mean_square + norm_eps) * norm_gain).astype(jnp.bfloat16)
    catalog = jnp.arange(expert_home.shape[0], dtype=jnp.int32)
    matches = routes[:, :, None] == catalog[None, None, :]
    home_of = jnp.sum(jnp.where(matches, expert_home[None, None, :], 0), axis=2)
    owner_ids = jnp.arange(owners, dtype=jnp.int32)
    on_owner = home_of[:, :, None] == owner_ids[None, None, :]
    chosen = jnp.any(on_owner, axis=1)
    share_weight = jnp.sum(jnp.where(on_owner, route_weight[:, :, None], 0.0), axis=1)
    order_in = jnp.cumsum(chosen.astype(jnp.int32), axis=0) - 1
    slot_ids = jnp.arange(MOST, dtype=jnp.int32)
    slot_map = chosen[:, :, None] & (order_in[:, :, None] == slot_ids[None, None, :])
    outgoing = jnp.einsum(
        "roc,rd->ocd", slot_map.astype(jnp.bfloat16), normed, preferred_element_type=jnp.float32
    ).astype(jnp.bfloat16)
    incoming = lax.all_to_all(outgoing, "dp", split_axis=0, concat_axis=0, tiled=True)
    stacked = incoming.reshape(-1, incoming.shape[2])
    gate_out = jnp.dot(stacked, w_gate[0], preferred_element_type=jnp.float32)
    up_out = jnp.dot(stacked, w_up[0], preferred_element_type=jnp.float32)
    hidden = (jax.nn.silu(gate_out) * up_out).astype(jnp.bfloat16)
    partial_term = jnp.dot(hidden, w_down[0], preferred_element_type=jnp.float32).reshape(
        incoming.shape
    )
    result = lax.psum_scatter(
        partial_term.astype(jnp.bfloat16), "tensor", scatter_dimension=2, tiled=True
    )
    returned = lax.all_to_all(result, "dp", split_axis=0, concat_axis=0, tiled=True)
    combine_weight = slot_map.astype(jnp.float32) * share_weight[:, :, None]
    experts_out = jnp.einsum("roc,ocd->rd", combine_weight, returned.astype(jnp.float32)).astype(
        jnp.bfloat16
    )
    return (attended, experts_out)


def solution(mesh):
    return jax.shard_map(
        shards,
        mesh=mesh,
        in_specs=(
            P("dp", "tensor", None),
            P("dp", None, None),
            P("dp"),
            P("tensor", None, None),
            P("tensor", "dp"),
            P(),
            P("dp", None),
            P("dp", None),
            P(),
            P("dp", None, "tensor"),
            P("dp", None, "tensor"),
            P("dp", "tensor", None),
        ),
        out_specs=(P("dp", None), P("dp", "tensor")),
        check_vma=False,
    )
```

profile of v0, /device:TPU:32, one launch (start us, length us, event | category | flops | bytes accessed | tf_op | source)
XLA Modules:
  0.0 457.1 jit_solution(15358132041718438465)
XLA Ops:
  7.2 0.0 copy-start
  7.2 0.0 all-gather.2.cloned.1.call-start
  7.2 0.9 iota_compare_fusion.3
  8.1 3.6 fusion.13
  11.7 0.3 fusion.43
  12.1 4.0 fusion.8
  16.1 3.3 fusion.14
  19.3 0.7 copy.57
  20.1 0.0 all-gather.2.cloned.1.call-update
  20.1 0.0 copy-start.4
  20.1 0.0 all-reduce.2.cloned.1.call-start
  20.2 210.1 %all-gather.2.cloned.1.call-done = bf16[2048,4096]{1,0:T(8,128)(2,1)} async-done(((bf16[32,4096]{1,0:T(8,128)(2,1)}), bf16[2048,4096]{1,0:T(8,128)(2,1)}) %all-gather.2.cloned.1.call-update) | async-done | bytes 16777232 | tf_op jit(solution)/shard_map/all_gather | solution.py:49
  230.3 11.0 %convolution_convert_fusion.2 = bf16[2048,56]{0,1:T(8,128)(2,1)S(1)} fusion(bf16[2048,4096]{1,0:T(8,128)(2,1)} %all-gather.2.cloned.1.call-done, bf16[4096,56]{0,1:T(8,128)(2,1)} %param.16), kind=kOutput, calls=%fused_computation.5 | convolution fusion | flops 939638784 | bytes 17465344 | tf_op jit(solution)/shard_map/dot_general | solution.py:48
  241.3 1.0 copy.37
  242.3 0.0 all-reduce.2.cloned.1.call-update
  242.3 0.1 copy.39
  242.4 41.4 %all-reduce.2.cloned.1.call-done = bf16[64,32,56]{2,1,0:T(8,128)(2,1)} async-done(((bf16[64,32,56]{2,1,0:T(8,128)(2,1)}), bf16[64,32,56]{2,1,0:T(8,128)(2,1)}) %all-reduce.2.cloned.1.call-update) | async-done | bytes 229392 | tf_op jit(solution)/shard_map/psum | solution.py:53
  283.8 2.6 reshape.69
  286.3 12.7 %all-to-all-start = ((bf16[64,2,896]{2,1,0:T(2,128)(2,1)}), bf16[64,2,896]{2,1,0:T(2,128)(2,1)S(1)}, u32[]{:S(2)}, u32[]{:S(2)}) async-start(bf16[64,2,896]{2,1,0:T(2,128)(2,1)} %reshape.69), calls=%async_computation | async-start | bytes 458752 | tf_op jit(solution)/shard_map/all_to_all | solution.py:54
  299.1 0.2 reduce-scatter.4.cloned.1.call-start
  299.3 0.7 select_reduce_fusion
  300.0 0.1 fusion.30
  300.1 0.1 reduce_window_sum.11
  300.2 13.3 %all-to-all-done = bf16[64,2,896]{2,1,0:T(2,128)(2,1)S(1)} async-done(((bf16[64,2,896]{2,1,0:T(2,128)(2,1)}), bf16[64,2,896]{2,1,0:T(2,128)(2,1)S(1)}, u32[]{:S(2)}, u32[]{:S(2)}) %all-to-all-start) | async-done | bytes 229408 | tf_op jit(solution)/shard_map/all_to_all | solution.py:54
  313.5 0.9 reshape.70
  314.4 0.3 multiply_reduce_fusion
  314.7 0.2 copy.38
  314.9 0.7 all_to_all.23
  315.6 0.0 copy-start.2
  315.7 0.7 convolution_convert_fusion.1
  316.4 1.4 copy.41
  317.8 50.9 %all_to_all.29 = bf16[64,4,3584]{2,1,0:T(4,128)(2,1)} all-to-all(bf16[64,4,3584]{2,1,0:T(4,128)(2,1)S(1)} %copy.41), channel_id=1, replica_groups=mesh['dp'=64,'tensor'=4] {'dp'}, dimensions={0} | all-to-all | bytes 3670016 | tf_op jit(solution)/shard_map/all_to_all | solution.py:71
  368.8 3.9 reshape.63
  372.7 2.8 fusion.6
  375.5 0.3 copy-done.7
  375.8 0.6 fusion.18
  376.5 1.9 convolution_convert_fusion
  378.4 6.3 %copy.45 = bf16[64,4,3584]{0,1,2:T(4,128)(2,1)} copy(bf16[64,4,3584]{2,0,1:T(8,128)(2,1)} %convolution_convert_fusion) | data formatting | bytes 3670016
  384.7 6.3 %reshape.67 = bf16[3584,256]{1,0:T(8,128)(2,1)} reshape(bf16[3584,4,64]{2,1,0:T(4,128)(2,1)} %bitcast.42) | data formatting | bytes 3670016
  391.0 0.0 reduce-scatter.4.cloned.1.call-update
  391.0 23.5 %reduce-scatter.4.cloned.1.call-done = bf16[896,256]{1,0:T(8,128)(2,1)} async-done(((bf16[3584,256]{1,0:T(8,128)(2,1)}), bf16[896,256]{1,0:T(8,128)(2,1)}) %reduce-scatter.4.cloned.1.call-update) | async-done | bytes 458768
  414.5 1.9 reshape.68
  416.4 1.8 copy.43
  418.2 12.6 %all-to-all-start.2 = ((bf16[64,4,896]{2,1,0:T(4,128)(2,1)}), bf16[64,4,896]{2,1,0:T(4,128)(2,1)S(1)}, u32[]{:S(2)}, u32[]{:S(2)}) async-start(bf16[64,4,896]{2,1,0:T(4,128)(2,1)} %copy.43), calls=%async_computation.2 | async-start | bytes 917504 | tf_op jit(solution)/shard_map/all_to_all | solution.py:82
  430.9 0.1 copy.40
  431.0 0.2 select_reduce_fusion.1
  431.1 18.6 %all-to-all-done.2 = bf16[64,4,896]{2,1,0:T(4,128)(2,1)S(1)} async-done(((bf16[64,4,896]{2,1,0:T(4,128)(2,1)}), bf16[64,4,896]{2,1,0:T(4,128)(2,1)S(1)}, u32[]{:S(2)}, u32[]{:S(2)}) %all-to-all-start.2) | async-done | bytes 458784 | tf_op jit(solution)/shard_map/all_to_all | solution.py:82
  449.7 0.9 fusion.21
  (16 shorter events, 0.1 us)
Async XLA Ops:
  7.2 369.3 %copy-start = (bf16[1,256,3584]{2,1,0:T(8,128)(2,1)S(1)}, bf16[1,256,3584]{2,1,0:T(8,128)(2,1)}, u32[]{:S(2)}) copy-start(bf16[1,256,3584]{2,1,0:T(8,128)(2,1)} %param.23) | copy-start | bytes 5505028
  7.2 223.1 %all-gather.2.cloned.1.call-start = ((), (), s32[]{:S(2)}) async-start(), calls=%async_computation.4 | async-start | bytes 17039360 | tf_op jit(solution)/shard_map/all_gather | solution.py:49
  20.1 222.2 %copy-start.4 = (s32[32,8]{0,1:T(8,128)S(1)}, s32[32,8]{0,1:T(8,128)}, u32[]{:S(2)}) copy-start(s32[32,8]{0,1:T(8,128)} %param.18) | copy-start | bytes 3076
  20.1 263.6 %all-reduce.2.cloned.1.call-start = ((), (), s32[]{:S(2)}) async-start(), calls=%async_computation.5 | async-start | bytes 1048576 | tf_op jit(solution)/shard_map/psum | solution.py:53
  241.3 58.0 %copy-start.6 = (s32[256]{0:T(256)S(1)}, s32[256]{0:T(256)}, u32[]{:S(2)}) copy-start(s32[256]{0:T(256)} %param.20) | copy-start | bytes 3076
  286.3 29.3 %copy-start.3 = (f32[3584]{0:T(1024)S(1)}, f32[3584]{0:T(1024)}, u32[]{:S(2)}) copy-start(f32[3584]{0:T(1024)} %param.17) | copy-start | bytes 43012
  286.3 27.2 %all-to-all-start = ((bf16[64,2,896]{2,1,0:T(2,128)(2,1)}), bf16[64,2,896]{2,1,0:T(2,128)(2,1)S(1)}, u32[]{:S(2)}, u32[]{:S(2)}) async-start(bf16[64,2,896]{2,1,0:T(2,128)(2,1)} %reshape.69), calls=%async_computation | async-start | bytes 458752 | tf_op jit(solution)/shard_map/all_to_all | solution.py:54
  299.1 115.4 %reduce-scatter.4.cloned.1.call-start = ((), (), s32[]{:S(2)}) async-start(), calls=%async_computation.6 | async-start | bytes 2293760
  315.6 2.2 copy-start.2
  372.7 2.9 copy-start.1
  372.7 3.2 copy-start.7
  391.0 39.9 %copy-start.5 = (f32[32,8]{0,1:T(8,128)S(1)}, f32[32,8]{0,1:T(8,128)}, u32[]{:S(2)}) copy-start(f32[32,8]{0,1:T(8,128)} %param.19) | copy-start | bytes 3076
  418.2 31.5 %all-to-all-start.2 = ((bf16[64,4,896]{2,1,0:T(4,128)(2,1)}), bf16[64,4,896]{2,1,0:T(4,128)(2,1)S(1)}, u32[]{:S(2)}, u32[]{:S(2)}) async-start(bf16[64,4,896]{2,1,0:T(4,128)(2,1)} %copy.43), calls=%async_computation.2 | async-start | bytes 917504 | tf_op jit(solution)/shard_map/all_to_all | solution.py:82
Sparse Core Ops, SparseCore 0:
  20.2 210.0 all-gather.1
  242.4 41.2 all-reduce.1
  391.1 23.3 reduce-scatter.3
where the time goes:
time: 458 us; the launch traced here: 457 us
  waiting for transfers between devices  307 us (67%)
  blocking collectives  50.9 us (11%)
  matrix products  28.8 us (6%)
  local copies, waits for them, and re-layouts  28.3 us (6%)
  starting transfers between devices  25.7 us (6%)
  between operations  14 us (3%)
    all_gather x1, waiting for transfers between devices, shards(): lax.all_gather(values, 'dp', axis=0, tiled=True)  210 us
    all_to_all x1, blocking collectives, shards(): lax.all_to_all(outgoing, 'dp', split_axis=0, concat_axis=0, tiled=True)  50.9 us
    psum x1, waiting for transfers between devices, shards(): summed = lax.psum(partial_out.astype(jnp.bfloat16), 'tensor')  41.4 us
    unnamed x4, waiting for transfers between devices  23.5 us
    all_to_all x1, waiting for transfers between devices, shards(): lax.all_to_all(result, 'dp', split_axis=0, concat_axis=0, tiled=True)  18.6 us
    unnamed x23, local copies, waits for them, and re-layouts  18.4 us
    all_to_all x1, waiting for transfers between devices, shards(): lax.all_to_all(summed, 'dp', split_axis=0, concat_axis=1, tiled=True)  13.3 us
    all_to_all x1, starting transfers between devices, shards(): lax.all_to_all(summed, 'dp', split_axis=0, concat_axis=1, tiled=True)  12.7 us
  transfers between devices with their start and end apart: 5, of which 5 were waited for; matrix products, arithmetic and copies ran while one was open for 0% of the time, Pallas kernels for 0%

commit v1 on v0

v1 whole, which is shorter than its diff:
```python
import jax
import jax.numpy as jnp
from jax import lax
from jax.sharding import Mesh, PartitionSpec as P

LATENT = 512
MOST = 4

softmax_scale = 192.0 ** (-0.5)
norm_eps = 1e-06

AXES = ("xh", "z", "y", "xl", "core")
DP = ("xh", "z", "y")
TENSOR = ("xl", "core")
bf16 = jnp.bfloat16
f32 = jnp.float32


def flip(value, axis, mask=1):
    count = lax.axis_size(axis)
    return lax.ppermute(value, axis, [(i, i ^ mask) for i in range(count)])


def exchange(value, axis):
    return lax.all_to_all(value, axis, split_axis=0, concat_axis=0, tiled=True)


def dot_t(left, right):
    return lax.dot_general(left, right, (((1,), (1,)), ((), ())), preferred_element_type=f32)


def pair(where_zero, mine, other):
    return jnp.where(where_zero, mine, other), jnp.where(where_zero, other, mine)


def attention(queries, latent_cache, lengths, value_up):
    scores = (
        jnp.einsum("rhc,rjc->rhj", queries, latent_cache, preferred_element_type=f32)
        * softmax_scale
    )
    visible = (
        lax.broadcasted_iota(jnp.int32, (1, 1, latent_cache.shape[1]), 2) < lengths[:, None, None]
    )
    scores = jnp.where(visible, scores, -jnp.inf)
    row_max = jnp.max(scores, axis=2, keepdims=True)
    exponent = jnp.exp(scores - row_max)
    weights = (exponent / jnp.sum(exponent, axis=2, keepdims=True)).astype(bf16)
    latent_out = jnp.einsum(
        "rhj,rjc->rhc", weights, latent_cache[:, :, :LATENT], preferred_element_type=f32
    ).astype(bf16)
    values = jnp.einsum("rhc,hcv->rhv", latent_out, value_up, preferred_element_type=f32)
    return values.astype(bf16).reshape(queries.shape[0], -1)


def placing(routes, expert_home, owners):
    catalog = jnp.arange(expert_home.shape[0], dtype=jnp.int32)
    matches = routes[:, :, None] == catalog[None, None, :]
    home_of = jnp.sum(jnp.where(matches, expert_home[None, None, :], 0), axis=2)
    owner_ids = jnp.arange(owners, dtype=jnp.int32)
    on_owner = home_of[:, :, None] == owner_ids[None, None, :]
    chosen = jnp.any(on_owner, axis=1)
    order_in = jnp.cumsum(chosen.astype(jnp.int32), axis=0) - 1
    slot_ids = jnp.arange(MOST, dtype=jnp.int32)
    slot_map = chosen[:, :, None] & (order_in[:, :, None] == slot_ids[None, None, :])
    return on_owner, slot_map


def shards(
    queries,
    latent_cache,
    lengths,
    value_up,
    out_proj,
    norm_gain,
    routes,
    route_weight,
    expert_home,
    w_gate,
    w_up,
    w_down,
):
    rows_here = queries.shape[0]
    xh, y, xl, core = (lax.axis_index(name) for name in ("xh", "y", "xl", "core"))
    n_z, n_y = lax.axis_size("z"), lax.axis_size("y")
    owners = lax.axis_size(DP)
    tensor_at = lax.axis_index(TENSOR)
    n_tensor = lax.axis_size(TENSOR)
    width = norm_gain.shape[0]
    quarter = width // n_tensor

    cols = out_proj.shape[1]
    depth = out_proj.shape[0] // n_z
    proj = out_proj.T.reshape(cols, n_z, depth).transpose(1, 0, 2)
    proj = exchange(proj, "z")
    half = n_z // 2
    proj_mine = lax.dynamic_slice_in_dim(proj, xl * half, half, 0)
    proj_other = flip(lax.dynamic_slice_in_dim(proj, (1 - xl) * half, half, 0), "xl")
    proj_both = jnp.stack([proj_mine, proj_other])
    over_y = jnp.stack([proj_both] + [flip(proj_both, "y", s) for s in range(1, n_y)])
    over_y = jnp.stack(
        [lax.dynamic_index_in_dim(over_y, y ^ s, 0, keepdims=False) for s in range(n_y)], axis=2
    )
    proj_own = over_y[0].reshape(quarter, depth)
    proj_oth = over_y[1].reshape(quarter, depth)

    down = []
    for s in range(n_tensor):
        piece = lax.dynamic_slice_in_dim(w_down[0], (tensor_at ^ s) * quarter, quarter, 1)
        down.append(flip(piece, TENSOR, s) if s else piece)

    swap = [(i, (i % 2) * 2 + i // 2) for i in range(4)]
    routes_sent = lax.ppermute(routes, ("xh", "core"), swap)

    values = attention(queries, latent_cache, lengths, value_up)
    values = values.reshape(rows_here, n_z, depth).transpose(1, 0, 2)
    values = exchange(values, "z").reshape(n_z * rows_here, depth)
    from_xl = flip(values, "xl")
    from_xh = flip(values, "xh")
    from_both = flip(values, ("xh", "xl"), 3)
    here = xh == core
    keep_own, send_own = pair(here, values, from_xh)
    keep_oth, send_oth = pair(here, from_xl, from_both)
    partial_send = (dot_t(send_own, proj_own) + dot_t(send_oth, proj_oth)).astype(bf16)
    partial_got = flip(partial_send, "core")
    partial = dot_t(keep_own, proj_own) + dot_t(keep_oth, proj_oth) + partial_got.astype(f32)
    partial = partial.astype(bf16).reshape(n_z, rows_here, quarter)
    partial = exchange(partial, "z")
    part_rows = jnp.sum(partial.astype(f32), axis=0).astype(bf16)

    _, slots_sent = placing(routes_sent, expert_home, owners)
    outgoing = jnp.einsum(
        "roc,rd->ocd", slots_sent.astype(bf16), part_rows, preferred_element_type=f32
    ).astype(bf16)
    incoming = exchange(outgoing, DP).reshape(2, -1, quarter)

    in_xl = flip(incoming, "xl")
    in_core = flip(incoming, "core")
    in_both = flip(in_xl, "core")
    own_xl = jnp.concatenate(pair(core == 0, incoming, in_core), axis=1)
    oth_xl = jnp.concatenate(pair(core == 0, in_xl, in_both), axis=1)
    xl_zero, xl_one = pair(xl == 0, own_xl, oth_xl)
    stacked = [xl_zero[0], xl_one[0], xl_zero[1], xl_one[1]]
    stacked_f = [piece.astype(f32) for piece in stacked]
    mean_square = sum(jnp.sum(p * p, axis=1, keepdims=True) for p in stacked_f) / width
    scale = lax.rsqrt(mean_square + norm_eps)
    gate_out, up_out = 0.0, 0.0
    for q in range(n_tensor):
        span = slice(q * quarter, (q + 1) * quarter)
        normed = (stacked_f[q] * scale * norm_gain[span]).astype(bf16)
        gate_out += jnp.dot(normed, w_gate[0, span], preferred_element_type=f32)
        up_out += jnp.dot(normed, w_up[0, span], preferred_element_type=f32)
    hidden = (jax.nn.silu(gate_out) * up_out).astype(bf16)
    hid_xl = flip(hidden, "xl")
    hid_core = flip(hidden, "core")
    hid_both = flip(hid_xl, "core")
    result = 0.0
    for piece, weight in zip((hidden, hid_core, hid_xl, hid_both), down):
        result += jnp.dot(piece, weight, preferred_element_type=f32)
    returned = exchange(result.astype(bf16).reshape(owners, MOST, quarter), DP)

    on_owner, slot_map = placing(routes, expert_home, owners)
    share_weight = jnp.sum(jnp.where(on_owner, route_weight[:, :, None], 0.0), axis=1)
    combine_weight = slot_map.astype(f32) * share_weight[:, :, None]
    experts_out = jnp.einsum("roc,ocd->rd", combine_weight, returned.astype(f32)).astype(bf16)

    row_xl = flip(part_rows, "xl")
    lower, upper = pair(xl == 0, part_rows, row_xl)
    mine = jnp.concatenate([lower, upper], axis=1)
    row_xh = flip(mine, "xh")
    lower, upper = pair(xh == 0, mine, row_xh)
    whole = jnp.concatenate([lower, upper], axis=1)
    attended = jnp.where(here, whole, flip(whole, "core"))
    return (attended, experts_out)


def solution(mesh):
    fine = Mesh(mesh.devices.reshape(2, 8, 4, 2, 2), AXES)
    return jax.shard_map(
        shards,
        mesh=fine,
        in_specs=(
            P(DP, TENSOR, None),
            P(DP, None, None),
            P(DP),
            P(TENSOR, None, None),
            P(TENSOR, DP),
            P(),
            P(DP, None),
            P(DP, None),
            P(),
            P(DP, None, TENSOR),
            P(DP, None, TENSOR),
            P(DP, TENSOR, None),
        ),
        out_specs=(P(DP, None), P(DP, TENSOR)),
        check_vma=False,
    )
```

time: 458 us -> 175 us (0.38)
  waiting for transfers between devices: 307 us -> 76.9 us
  blocking collectives: 50.9 us -> 0 us
  starting transfers between devices: 25.7 us -> 57.7 us
  local copies, waits for them, and re-layouts: 28.3 us -> 10.1 us
  between operations: 14 us -> 1.13 us
  matrix products: 28.8 us -> 20.5 us
  other arithmetic: 2.5 us -> 7.89 us
    all_gather x1 -> x0, waiting for transfers between devices: 210 us -> none  [shards(): lax.all_gather(values, 'dp', axis=0, tiled=True)]
    all_to_all x1 -> x0, blocking collectives: 50.9 us -> none  [shards(): lax.all_to_all(outgoing, 'dp', split_axis=0, concat_axis=0, tiled=True)]
    psum x1 -> x0, waiting for transfers between devices: 41.4 us -> none  [shards(): summed = lax.psum(partial_out.astype(jnp.bfloat16), 'tensor')]
    ppermute x0 -> x21, waiting for transfers between devices: none -> 35.1 us  [the longest x20 35.1 us: flip(): return lax.ppermute(value, axis, [(i, i ^ mask) for i in range(count)])]
    unnamed x4 -> x0, waiting for transfers between devices: 23.5 us -> none
    ppermute x0 -> x21, starting transfers between devices: none -> 20.2 us  [the longest x20 19.5 us: flip(): return lax.ppermute(value, axis, [(i, i ^ mask) for i in range(count)])]
    unnamed x23 -> x20, local copies, waits for them, and re-layouts: 18.4 us -> 1.42 us
    all_to_all x2 -> x5, starting transfers between devices: 25.4 us -> 37.5 us  [exchange(): return lax.all_to_all(value, axis, split_axis=0, concat_axis=0, tiled=True)]
  transfers between devices with their start and end apart: 5 -> 26, of which waited for: 5 -> 13; matrix products, arithmetic and copies ran while one was open for 0% -> 18% of each run, Pallas kernels for 0% -> 0%
where the time goes in v1:
time: 175 us; the launch traced here: 174 us
  waiting for transfers between devices  76.9 us (44%)
  starting transfers between devices  57.7 us (33%)
  matrix products  20.5 us (12%)
  local copies, waits for them, and re-layouts  10.1 us (6%)
  other arithmetic  7.89 us (5%)
    all_to_all x5, waiting for transfers between devices, exchange(): return lax.all_to_all(value, axis, split_axis=0, concat_axis=0, tiled=True)  41.8 us
    all_to_all x5, starting transfers between devices, exchange(): return lax.all_to_all(value, axis, split_axis=0, concat_axis=0, tiled=True)  37.5 us
    ppermute x20, waiting for transfers between devices, flip(): return lax.ppermute(value, axis, [(i, i ^ mask) for i in range(count)])  35.1 us
    ppermute x20, starting transfers between devices, flip(): return lax.ppermute(value, axis, [(i, i ^ mask) for i in range(count)])  19.5 us
    dot_general x1, matrix products, attention(): jnp.einsum('rhj,rjc->rhc', weights, latent_cache[:, :, :LATENT], preferre...  4.02 us
  transfers between devices with their start and end apart: 26, of which 13 were waited for; matrix products, arithmetic and copies ran while one was open for 18% of the time, Pallas kernels for 0%

profile of v1, /device:TPU:32, one launch (start us, length us, event | category | flops | bytes accessed | tf_op | source)
XLA Modules:
  0.0 174.2 jit_solution(16582316541776168668)
XLA Ops:
  0.7 1.9 %copy.62 = bf16[7,8,8,512]{3,2,0,1:T(8,128)(2,1)} copy(bf16[7,8,8,512]{3,2,1,0:T(8,128)(2,1)} %bitcast.116) | data formatting | bytes 917504 | tf_op jit(solution)/shard_map/reshape | solution.py:93
  2.6 8.6 %all-to-all-start.1 = ((bf16[8,56,512]{2,1,0:T(8,128)(2,1)}), bf16[8,56,512]{2,1,0:T(8,128)(2,1)S(1)}, u32[]{:S(2)}, u32[]{:S(2)}) async-start(bf16[8,56,512]{2,1,0:T(8,128)(2,1)} %bitcast.102), calls=%async_computation.1 | async-start | bytes 917504 | tf_op jit(solution)/shard_map/all_to_all | solution.py:25
  11.2 3.2 %fusion.12 = f32[32,32,128]{2,1,0:T(8,128)S(1)} fusion(bf16[32,32,576]{2,1,0:T(8,128)(2,1)S(1)} %copy-done, bf16[32,128,576]{1,2,0:T(8,128)(2,1)} %param.13, pred[32,128]{1,0:T(8,128)(4,1)S(1)} %iota_compare_fusion.6), kind=kOutput, calls=%fused_computation.19 | convolution fusion | flops 151257088 | bytes 6426624 | tf_op jit(solution)/shard_map/rhc,rjc->rhj/dot_general | solution.py:38
  14.8 4.0 %fusion.3 = bf16[32,32,512]{2,1,0:T(8,128)(2,1)S(1)} fusion(bf16[32,128,576]{1,2,0:T(8,128)(2,1)} %param.13, f32[32,32]{1,0:T(8,128)S(1)} %fusion.95, f32[32,32,128]{2,1,0:T(8,128)S(1)} %fusion.12), kind=kOutput, calls=%fused_computation.5 | convolution fusion | flops 135136384 | bytes 6307840 | tf_op jit(solution)/shard_map/rhj,rjc->rhc/dot_general | solution.py:48
  18.8 7.0 %all-to-all-done.1 = bf16[8,56,512]{2,1,0:T(8,128)(2,1)S(1)} async-done(((bf16[8,56,512]{2,1,0:T(8,128)(2,1)}), bf16[8,56,512]{2,1,0:T(8,128)(2,1)S(1)}, u32[]{:S(2)}, u32[]{:S(2)}) %all-to-all-start.1) | async-done | bytes 458784 | tf_op jit(solution)/shard_map/all_to_all | solution.py:25
  25.8 0.8 dynamic-slice_bitcast_fusion.7
  26.6 1.5 collective-permute-start.1
  28.1 3.2 %fusion.13 = bf16[32,32,128]{2,0,1:T(8,128)(2,1)S(1)} fusion(bf16[32,512,128]{2,1,0:T(8,128)(2,1)} %param.15, bf16[32,32,512]{2,1,0:T(8,128)(2,1)S(1)} %fusion.3), kind=kOutput, calls=%fused_computation.21 | convolution fusion | flops 134348800 | bytes 5505024 | tf_op jit(solution)/shard_map/rhc,hcv->rhv/dot_general | solution.py:51
  31.6 0.8 copy.48
  32.4 4.8 %all-to-all-start = ((bf16[8,32,512]{2,1,0:T(8,128)(2,1)}), bf16[8,32,512]{2,1,0:T(8,128)(2,1)S(1)}, u32[]{:S(2)}, u32[]{:S(2)}) async-start(bf16[8,32,512]{2,1,0:T(8,128)(2,1)} %copy.48), calls=%async_computation | async-start | bytes 524288 | tf_op jit(solution)/shard_map/all_to_all | solution.py:25
  37.2 1.8 %fusion.92 = (bf16[1,2,4,56,512]{4,3,2,1,0:T(8,128)(2,1)S(1)}, bf16[2,4,56,512]{3,2,1,0:T(8,128)(2,1)}) fusion(bf16[1,4,56,512]{3,2,1,0:T(8,128)(2,1)} %bitcast.6, bf16[1,4,56,512]{3,2,1,0:T(8,128)(2,1)S(1)} %copy-done.1), kind=kLoop, calls=%fused_computation.145 | loop fusion | flops 229376 | bytes 1376256 | tf_op jit(solution)/shard_map/stack | solution.py:99
  39.0 3.0 %collective-permute-start.4 = (bf16[2,4,56,512]{3,2,1,0:T(8,128)(2,1)}, bf16[2,4,56,512]{3,2,1,0:T(8,128)(2,1)S(1)}, u32[]{:S(2)}, u32[]{:S(2)}) collective-permute-start(bf16[2,4,56,512]{3,2,1,0:T(8,128)(2,1)} %get-tuple-element.24), channel_id=1, source_target_pairs={{0,12},{4,8},{8,4},{12,0},{1,13},{5,9},{9,5},{13,1},{2,14},{6,10},... | collective-permute-start | bytes 1376264 | tf_op jit(solution)/shard_map/ppermute | solution.py:21
  42.1 1.5 collective-permute-start.3
  43.7 4.1 %all-to-all-done = bf16[8,32,512]{2,1,0:T(8,128)(2,1)S(1)} async-done(((bf16[8,32,512]{2,1,0:T(8,128)(2,1)}), bf16[8,32,512]{2,1,0:T(8,128)(2,1)S(1)}, u32[]{:S(2)}, u32[]{:S(2)}) %all-to-all-start) | async-done | bytes 262176 | tf_op jit(solution)/shard_map/all_to_all | solution.py:25
  47.7 0.5 collective-permute-start.5
  48.2 2.8 %collective-permute-start.6 = (bf16[256,512]{1,0:T(8,128)(2,1)S(1)}, bf16[256,512]{1,0:T(8,128)(2,1)S(1)}, u32[]{:S(2)}, u32[]{:S(2)}) collective-permute-start(bf16[256,512]{1,0:T(8,128)(2,1)S(1)} %bitcast.108), channel_id=1, source_target_pairs={{0,130},{2,128},{128,2},{130,0},{1,131},{3,129},{129,3},{131,1},{4... | collective-permute-start | bytes 786440 | tf_op jit(solution)/shard_map/ppermute | solution.py:21
  51.0 1.9 %collective-permute-done.4 = bf16[2,4,56,512]{3,2,1,0:T(8,128)(2,1)S(1)} collective-permute-done((bf16[2,4,56,512]{3,2,1,0:T(8,128)(2,1)}, bf16[2,4,56,512]{3,2,1,0:T(8,128)(2,1)S(1)}, u32[]{:S(2)}, u32[]{:S(2)}) %collective-permute-start.4) | collective-permute-done | bytes 458784 | tf_op jit(solution)/shard_map/ppermute | solution.py:21
  52.9 2.7 %collective-permute-start = (bf16[256,512]{1,0:T(8,128)(2,1)S(1)}, bf16[256,512]{1,0:T(8,128)(2,1)S(1)}, u32[]{:S(2)}, u32[]{:S(2)}) collective-permute-start(bf16[256,512]{1,0:T(8,128)(2,1)S(1)} %bitcast.109), channel_id=1, source_target_pairs={{0,128},{128,0},{1,129},{129,1},{2,130},{130,2},{3,131},{131,3},{4... | collective-permute-start | bytes 786440 | tf_op jit(solution)/shard_map/ppermute | solution.py:21
  55.7 7.6 %collective-permute-done.3 = bf16[2,4,56,512]{3,2,1,0:T(8,128)(2,1)S(1)} collective-permute-done((bf16[2,4,56,512]{3,2,1,0:T(8,128)(2,1)}, bf16[2,4,56,512]{3,2,1,0:T(8,128)(2,1)S(1)}, u32[]{:S(2)}, u32[]{:S(2)}) %collective-permute-start.3) | collective-permute-done | bytes 458784 | tf_op jit(solution)/shard_map/ppermute | solution.py:21
  64.5 0.5 fusion.10
  65.1 0.5 fusion.59
  65.6 1.3 collective-permute-done.7
  66.9 1.3 fusion.8
  68.2 7.4 %all-to-all-start.2 = ((bf16[8,32,896]{2,1,0:T(8,128)(2,1)}), bf16[8,32,896]{2,1,0:T(8,128)(2,1)S(1)}, u32[]{:S(2)}, u32[]{:S(2)}) async-start(bf16[8,32,896]{2,1,0:T(8,128)(2,1)} %bitcast.17), calls=%async_computation.2 | async-start | bytes 917504 | tf_op jit(solution)/shard_map/all_to_all | solution.py:25
  75.5 0.7 collective-permute-start.11
  76.2 2.4 %dynamic-slice_bitcast_fusion = (bf16[256,896]{1,0:T(8,128)(2,1)}, bf16[256,896]{1,0:T(8,128)(2,1)}, bf16[256,896]{1,0:T(8,128)(2,1)}) fusion(bf16[1,256,3584]{2,1,0:T(8,128)(2,1)} %param.23, s32[]{:T(128)S(6)} %select_n.164, s32[]{:T(128)S(6)} %select_n.162, s32[]{:T(128)S(6)} %select_n.163), kind=kLoop, calls=%fused_computation.77 | loop fusion | bytes 2752524 | tf_op jit(solution)/shard_map/dynamic_slice | solution.py:108
  78.7 4.1 %collective-permute-start.16 = (bf16[256,896]{1,0:T(8,128)(2,1)}, bf16[256,896]{1,0:T(8,128)(2,1)S(1)}, u32[]{:S(2)}, u32[]{:S(2)}) collective-permute-start(bf16[256,896]{1,0:T(8,128)(2,1)} %get-tuple-element.9), channel_id=1, source_target_pairs={{0,1},{1,0},{2,3},{3,2},{4,5},{5,4},{6,7},{7,6},{8,9},{9,8},{10,11... | collective-permute-start | bytes 1376264 | tf_op jit(solution)/shard_map/ppermute | solution.py:21
  83.0 1.4 collective-permute-start.20
  84.5 1.2 select_reduce_fusion.1
  86.0 4.5 %all-to-all-done.2 = bf16[8,32,896]{2,1,0:T(8,128)(2,1)S(1)} async-done(((bf16[8,32,896]{2,1,0:T(8,128)(2,1)}), bf16[8,32,896]{2,1,0:T(8,128)(2,1)S(1)}, u32[]{:S(2)}, u32[]{:S(2)}) %all-to-all-start.2) | async-done | bytes 458784 | tf_op jit(solution)/shard_map/all_to_all | solution.py:25
  90.9 1.2 copy.53
  92.0 8.4 %all-to-all-start.3 = ((bf16[64,4,896]{2,1,0:T(4,128)(2,1)}), bf16[64,4,896]{2,1,0:T(4,128)(2,1)S(1)}, u32[]{:S(2)}, u32[]{:S(2)}) async-start(bf16[64,4,896]{2,1,0:T(4,128)(2,1)} %copy.53), calls=%async_computation.3 | async-start | bytes 917504 | tf_op jit(solution)/shard_map/all_to_all | solution.py:25
  101.1 9.9 %collective-permute-done.8 = bf16[32,896]{1,0:T(8,128)(2,1)S(1)} collective-permute-done((bf16[32,896]{1,0:T(8,128)(2,1)S(1)}, bf16[32,896]{1,0:T(8,128)(2,1)S(1)}, u32[]{:S(2)}, u32[]{:S(2)}) %collective-permute-start.8) | collective-permute-done | bytes 57376 | tf_op jit(solution)/shard_map/ppermute | solution.py:21
  111.1 8.1 %all-to-all-done.3 = bf16[64,4,896]{2,1,0:T(4,128)(2,1)S(1)} async-done(((bf16[64,4,896]{2,1,0:T(4,128)(2,1)}), bf16[64,4,896]{2,1,0:T(4,128)(2,1)S(1)}, u32[]{:S(2)}, u32[]{:S(2)}) %all-to-all-start.3) | async-done | bytes 458784 | tf_op jit(solution)/shard_map/all_to_all | solution.py:25
  119.9 0.9 broadcast_select_fusion.8
  120.9 8.7 %collective-permute-done.13 = bf16[2,128,896]{2,1,0:T(8,128)(2,1)S(1)} collective-permute-done((bf16[2,128,896]{2,1,0:T(8,128)(2,1)S(1)}, bf16[2,128,896]{2,1,0:T(8,128)(2,1)S(1)}, u32[]{:S(2)}, u32[]{:S(2)}) %collective-permute-start.13) | collective-permute-done | bytes 458784 | tf_op jit(solution)/shard_map/ppermute | solution.py:21
  129.6 0.7 pad_maximum_fusion.5
  130.4 1.0 collective-permute-done.14
  132.3 1.2 copy-done.7
  137.0 1.3 fusion.34
  138.5 4.0 %collective-permute-done.17 = bf16[256,256]{1,0:T(8,128)(2,1)S(1)} collective-permute-done((bf16[256,256]{1,0:T(8,128)(2,1)S(1)}, bf16[256,256]{1,0:T(8,128)(2,1)S(1)}, u32[]{:S(2)}, u32[]{:S(2)}) %collective-permute-start.17) | collective-permute-done | bytes 131104 | tf_op jit(solution)/shard_map/ppermute | solution.py:21
  143.1 0.7 collective-permute-done.19
  143.8 1.3 fusion.9
  145.2 0.9 reshape.221
  146.0 8.4 %all-to-all-start.4 = ((bf16[64,4,896]{2,1,0:T(4,128)(2,1)}), bf16[64,4,896]{2,1,0:T(4,128)(2,1)S(1)}, u32[]{:S(2)}, u32[]{:S(2)}) async-start(bf16[64,4,896]{2,1,0:T(4,128)(2,1)} %reshape.221), calls=%async_computation.4 | async-start | bytes 917504 | tf_op jit(solution)/shard_map/all_to_all | solution.py:25
  154.4 0.7 broadcast_select_fusion.6
  155.2 18.2 %all-to-all-done.4 = bf16[64,4,896]{2,1,0:T(4,128)(2,1)S(1)} async-done(((bf16[64,4,896]{2,1,0:T(4,128)(2,1)}), bf16[64,4,896]{2,1,0:T(4,128)(2,1)S(1)}, u32[]{:S(2)}, u32[]{:S(2)}) %all-to-all-start.4) | async-done | bytes 458784 | tf_op jit(solution)/shard_map/all_to_all | solution.py:25
  173.3 0.9 fusion.16
  (84 shorter events, 9.7 us)
Async XLA Ops:
  0.6 10.6 %copy-start = (bf16[32,32,576]{2,1,0:T(8,128)(2,1)S(1)}, bf16[32,32,576]{2,1,0:T(8,128)(2,1)}, u32[]{:S(2)}) copy-start(bf16[32,32,576]{2,1,0:T(8,128)(2,1)} %param.12) | copy-start | bytes 3538948
  0.6 10.5 %copy-start.6 = (s32[32]{0:T(128)S(1)}, s32[32]{0:T(128)}, u32[]{:S(2)}) copy-start(s32[32]{0:T(128)} %param.14) | copy-start | bytes 388
  2.6 23.2 %all-to-all-start.1 = ((bf16[8,56,512]{2,1,0:T(8,128)(2,1)}), bf16[8,56,512]{2,1,0:T(8,128)(2,1)S(1)}, u32[]{:S(2)}, u32[]{:S(2)}) async-start(bf16[8,56,512]{2,1,0:T(8,128)(2,1)} %bitcast.102), calls=%async_computation.1 | async-start | bytes 917504 | tf_op jit(solution)/shard_map/all_to_all | solution.py:25
  26.6 10.6 %collective-permute-start.1 = (bf16[4,56,512]{2,1,0:T(8,128)(2,1)}, bf16[4,56,512]{2,1,0:T(8,128)(2,1)}, u32[]{:S(2)}, u32[]{:S(2)}) collective-permute-start(bf16[4,56,512]{2,1,0:T(8,128)(2,1)} %get-tuple-element.26), channel_id=1, source_target_pairs={{0,2},{2,0},{1,3},{3,1},{4,6},{6,4},{5,7},{7,5},{8,10},{10,8},{9,1... | collective-permute-start | bytes 688136 | tf_op jit(solution)/shard_map/ppermute | solution.py:21
  31.3 5.8 %copy-start.1 = (bf16[1,4,56,512]{3,2,1,0:T(8,128)(2,1)S(1)}, bf16[1,4,56,512]{3,2,1,0:T(8,128)(2,1)}, u32[]{:S(2)}) copy-start(bf16[1,4,56,512]{3,2,1,0:T(8,128)(2,1)} %get-tuple-element.25) | copy-start | bytes 688132
  32.4 15.3 %all-to-all-start = ((bf16[8,32,512]{2,1,0:T(8,128)(2,1)}), bf16[8,32,512]{2,1,0:T(8,128)(2,1)S(1)}, u32[]{:S(2)}, u32[]{:S(2)}) async-start(bf16[8,32,512]{2,1,0:T(8,128)(2,1)} %copy.48), calls=%async_computation | async-start | bytes 524288 | tf_op jit(solution)/shard_map/all_to_all | solution.py:25
  39.0 14.0 %collective-permute-start.4 = (bf16[2,4,56,512]{3,2,1,0:T(8,128)(2,1)}, bf16[2,4,56,512]{3,2,1,0:T(8,128)(2,1)S(1)}, u32[]{:S(2)}, u32[]{:S(2)}) collective-permute-start(bf16[2,4,56,512]{3,2,1,0:T(8,128)(2,1)} %get-tuple-element.24), channel_id=1, source_target_pairs={{0,12},{4,8},{8,4},{12,0},{1,13},{5,9},{9,5},{13,1},{2,14},{6,10},... | collective-permute-start | bytes 1376264 | tf_op jit(solution)/shard_map/ppermute | solution.py:21
  42.0 13.7 %collective-permute-start.2 = (bf16[2,4,56,512]{3,2,1,0:T(8,128)(2,1)}, bf16[2,4,56,512]{3,2,1,0:T(8,128)(2,1)S(1)}, u32[]{:S(2)}, u32[]{:S(2)}) collective-permute-start(bf16[2,4,56,512]{3,2,1,0:T(8,128)(2,1)} %get-tuple-element.24), channel_id=1, source_target_pairs={{0,4},{4,0},{8,12},{12,8},{1,5},{5,1},{9,13},{13,9},{2,6},{6,2},{1... | collective-permute-start | bytes 1376264 | tf_op jit(solution)/shard_map/ppermute | solution.py:21
  42.1 21.1 %collective-permute-start.3 = (bf16[2,4,56,512]{3,2,1,0:T(8,128)(2,1)}, bf16[2,4,56,512]{3,2,1,0:T(8,128)(2,1)S(1)}, u32[]{:S(2)}, u32[]{:S(2)}) collective-permute-start(bf16[2,4,56,512]{3,2,1,0:T(8,128)(2,1)} %get-tuple-element.24), channel_id=1, source_target_pairs={{0,8},{4,12},{8,0},{12,4},{1,9},{5,13},{9,1},{13,5},{2,10},{6,14},... | collective-permute-start | bytes 1376264 | tf_op jit(solution)/shard_map/ppermute | solution.py:21
  47.7 16.3 %collective-permute-start.5 = (bf16[256,512]{1,0:T(8,128)(2,1)S(1)}, bf16[256,512]{1,0:T(8,128)(2,1)S(1)}, u32[]{:S(2)}, u32[]{:S(2)}) collective-permute-start(bf16[256,512]{1,0:T(8,128)(2,1)S(1)} %bitcast.107), channel_id=1, source_target_pairs={{0,2},{2,0},{1,3},{3,1},{4,6},{6,4},{5,7},{7,5},{8,10},{10,8},{9,1... | collective-permute-start | bytes 786440 | tf_op jit(solution)/shard_map/ppermute | solution.py:21
  48.2 15.8 %collective-permute-start.6 = (bf16[256,512]{1,0:T(8,128)(2,1)S(1)}, bf16[256,512]{1,0:T(8,128)(2,1)S(1)}, u32[]{:S(2)}, u32[]{:S(2)}) collective-permute-start(bf16[256,512]{1,0:T(8,128)(2,1)S(1)} %bitcast.108), channel_id=1, source_target_pairs={{0,130},{2,128},{128,2},{130,0},{1,131},{3,129},{129,3},{131,1},{4... | collective-permute-start | bytes 786440 | tf_op jit(solution)/shard_map/ppermute | solution.py:21
  52.9 11.6 %collective-permute-start = (bf16[256,512]{1,0:T(8,128)(2,1)S(1)}, bf16[256,512]{1,0:T(8,128)(2,1)S(1)}, u32[]{:S(2)}, u32[]{:S(2)}) collective-permute-start(bf16[256,512]{1,0:T(8,128)(2,1)S(1)} %bitcast.109), channel_id=1, source_target_pairs={{0,128},{128,0},{1,129},{129,1},{2,130},{130,2},{3,131},{131,3},{4... | collective-permute-start | bytes 786440 | tf_op jit(solution)/shard_map/ppermute | solution.py:21
  65.0 1.9 %collective-permute-start.7 = (bf16[256,896]{1,0:T(8,128)(2,1)S(1)}, bf16[256,896]{1,0:T(8,128)(2,1)S(1)}, u32[]{:S(2)}, u32[]{:S(2)}) collective-permute-start(bf16[256,896]{1,0:T(8,128)(2,1)S(1)} %fusion.10), channel_id=1, source_target_pairs={{0,1},{1,0},{2,3},{3,2},{4,5},{5,4},{6,7},{7,6},{8,9},{9,8},{10,11... | collective-permute-start | bytes 1376264 | tf_op jit(solution)/shard_map/ppermute | solution.py:21
  65.6 10.0 %copy-start.3 = (s32[32,8]{0,1:T(8,128)S(1)}, s32[32,8]{0,1:T(8,128)}, u32[]{:S(2)}) copy-start(s32[32,8]{0,1:T(8,128)} %param.18) | copy-start | bytes 3076
  68.2 16.4 %copy-start.5 = (s32[256]{0:T(256)S(1)}, s32[256]{0:T(256)}, u32[]{:S(2)}) copy-start(s32[256]{0:T(256)} %param.20) | copy-start | bytes 3076
  68.2 22.3 %all-to-all-start.2 = ((bf16[8,32,896]{2,1,0:T(8,128)(2,1)}), bf16[8,32,896]{2,1,0:T(8,128)(2,1)S(1)}, u32[]{:S(2)}, u32[]{:S(2)}) async-start(bf16[8,32,896]{2,1,0:T(8,128)(2,1)} %bitcast.17), calls=%async_computation.2 | async-start | bytes 917504 | tf_op jit(solution)/shard_map/all_to_all | solution.py:25
  75.5 8.9 %collective-permute-start.11 = (s32[32,8]{0,1:T(8,128)S(1)}, s32[32,8]{0,1:T(8,128)S(1)}, u32[]{:S(2)}, u32[]{:S(2)}) collective-permute-start(s32[32,8]{0,1:T(8,128)S(1)} %copy-done.3), channel_id=1, source_target_pairs={{0,0},{1,128},{128,1},{129,129},{2,2},{3,130},{130,3},{131,131},{4... | collective-permute-start | bytes 3080 | tf_op jit(solution)/shard_map/ppermute | solution.py:112
  78.7 21.8 %copy-start.2 = (f32[3584]{0:T(1024)S(1)}, f32[3584]{0:T(1024)}, u32[]{:S(2)}) copy-start(f32[3584]{0:T(1024)} %param.17) | copy-start | bytes 43012
  78.7 21.8 %copy-start.4 = (f32[32,8]{0,1:T(8,128)S(1)}, f32[32,8]{0,1:T(8,128)}, u32[]{:S(2)}) copy-start(f32[32,8]{0,1:T(8,128)} %param.19) | copy-start | bytes 3076
  78.7 59.7 %collective-permute-start.16 = (bf16[256,896]{1,0:T(8,128)(2,1)}, bf16[256,896]{1,0:T(8,128)(2,1)S(1)}, u32[]{:S(2)}, u32[]{:S(2)}) collective-permute-start(bf16[256,896]{1,0:T(8,128)(2,1)} %get-tuple-element.9), channel_id=1, source_target_pairs={{0,1},{1,0},{2,3},{3,2},{4,5},{5,4},{6,7},{7,6},{8,9},{9,8},{10,11... | collective-permute-start | bytes 1376264 | tf_op jit(solution)/shard_map/ppermute | solution.py:21
  82.8 60.0 %collective-permute-start.18 = (bf16[256,896]{1,0:T(8,128)(2,1)}, bf16[256,896]{1,0:T(8,128)(2,1)S(1)}, u32[]{:S(2)}, u32[]{:S(2)}) collective-permute-start(bf16[256,896]{1,0:T(8,128)(2,1)} %get-tuple-element.10), channel_id=1, source_target_pairs={{0,2},{1,3},{2,0},{3,1},{4,6},{5,7},{6,4},{7,5},{8,10},{9,11},{10,... | collective-permute-start | bytes 1376264 | tf_op jit(solution)/shard_map/ppermute | solution.py:21
  83.0 60.1 %collective-permute-start.20 = (bf16[256,896]{1,0:T(8,128)(2,1)}, bf16[256,896]{1,0:T(8,128)(2,1)}, u32[]{:S(2)}, u32[]{:S(2)}) collective-permute-start(bf16[256,896]{1,0:T(8,128)(2,1)} %get-tuple-element.8), channel_id=1, source_target_pairs={{0,3},{1,2},{2,1},{3,0},{4,7},{5,6},{6,5},{7,4},{8,11},{9,10},{10,... | collective-permute-start | bytes 1376264 | tf_op jit(solution)/shard_map/ppermute | solution.py:21
  92.0 27.2 %all-to-all-start.3 = ((bf16[64,4,896]{2,1,0:T(4,128)(2,1)}), bf16[64,4,896]{2,1,0:T(4,128)(2,1)S(1)}, u32[]{:S(2)}, u32[]{:S(2)}) async-start(bf16[64,4,896]{2,1,0:T(4,128)(2,1)} %copy.53), calls=%async_computation.3 | async-start | bytes 917504 | tf_op jit(solution)/shard_map/all_to_all | solution.py:25
  100.8 10.2 %collective-permute-start.8 = (bf16[32,896]{1,0:T(8,128)(2,1)S(1)}, bf16[32,896]{1,0:T(8,128)(2,1)S(1)}, u32[]{:S(2)}, u32[]{:S(2)}) collective-permute-start(bf16[32,896]{1,0:T(8,128)(2,1)S(1)} %reduce_sum.85), channel_id=1, source_target_pairs={{0,2},{2,0},{1,3},{3,1},{4,6},{6,4},{5,7},{7,5},{8,10},{10,8},{9,1... | collective-permute-start | bytes 172040 | tf_op jit(solution)/shard_map/ppermute | solution.py:21
  111.0 8.8 %collective-permute-start.9 = (bf16[32,1792]{1,0:T(8,128)(2,1)S(1)}, bf16[32,1792]{1,0:T(8,128)(2,1)}, u32[]{:S(2)}, u32[]{:S(2)}) collective-permute-start(bf16[32,1792]{1,0:T(8,128)(2,1)S(1)} %pad_maximum_fusion.6), channel_id=1, source_target_pairs={{0,128},{128,0},{1,129},{129,1},{2,130},{130,2},{3,131},{131,3},{4... | collective-permute-start | bytes 344072 | tf_op jit(solution)/shard_map/ppermute | solution.py:21
  119.4 10.2 %collective-permute-start.13 = (bf16[2,128,896]{2,1,0:T(8,128)(2,1)S(1)}, bf16[2,128,896]{2,1,0:T(8,128)(2,1)S(1)}, u32[]{:S(2)}, u32[]{:S(2)}) collective-permute-start(bf16[2,128,896]{2,1,0:T(8,128)(2,1)S(1)} %reshape.220), channel_id=1, source_target_pairs={{0,2},{2,0},{1,3},{3,1},{4,6},{6,4},{5,7},{7,5},{8,10},{10,8},{9,1... | collective-permute-start | bytes 1376264 | tf_op jit(solution)/shard_map/ppermute | solution.py:21
  119.8 10.4 %collective-permute-start.12 = (bf16[2,128,896]{2,1,0:T(8,128)(2,1)S(1)}, bf16[2,128,896]{2,1,0:T(8,128)(2,1)S(1)}, u32[]{:S(2)}, u32[]{:S(2)}) collective-permute-start(bf16[2,128,896]{2,1,0:T(8,128)(2,1)S(1)} %reshape.220), channel_id=1, source_target_pairs={{0,1},{1,0},{2,3},{3,2},{4,5},{5,4},{6,7},{7,6},{8,9},{9,8},{10,11... | collective-permute-start | bytes 1376264 | tf_op jit(solution)/shard_map/ppermute | solution.py:21
  129.6 1.8 %collective-permute-start.14 = (bf16[2,128,896]{2,1,0:T(8,128)(2,1)S(1)}, bf16[2,128,896]{2,1,0:T(8,128)(2,1)S(1)}, u32[]{:S(2)}, u32[]{:S(2)}) collective-permute-start(bf16[2,128,896]{2,1,0:T(8,128)(2,1)S(1)} %collective-permute-done.13), channel_id=1, source_target_pairs={{0,1},{1,0},{2,3},{3,2},{4,5},{5,4},{6,7},{7,6},{8,9},{9,8},{10,11... | collective-permute-start | bytes 1376264 | tf_op jit(solution)/shard_map/ppermute | solution.py:21
  131.5 2.4 %copy-start.8 = (bf16[1,3584,256]{2,1,0:T(8,128)(2,1)S(1)}, bf16[1,3584,256]{2,1,0:T(8,128)(2,1)}, u32[]{:S(2)}) copy-start(bf16[1,3584,256]{2,1,0:T(8,128)(2,1)} %param.22) | copy-start | bytes 5505028
  131.9 1.7 copy-start.7
  136.5 6.0 %collective-permute-start.15 = (bf16[256,256]{1,0:T(8,128)(2,1)S(1)}, bf16[256,256]{1,0:T(8,128)(2,1)S(1)}, u32[]{:S(2)}, u32[]{:S(2)}) collective-permute-start(bf16[256,256]{1,0:T(8,128)(2,1)S(1)} %fusion.15), channel_id=1, source_target_pairs={{0,1},{1,0},{2,3},{3,2},{4,5},{5,4},{6,7},{7,6},{8,9},{9,8},{10,11... | collective-permute-start | bytes 393224 | tf_op jit(solution)/shard_map/ppermute | solution.py:21
  136.7 5.8 %collective-permute-start.17 = (bf16[256,256]{1,0:T(8,128)(2,1)S(1)}, bf16[256,256]{1,0:T(8,128)(2,1)S(1)}, u32[]{:S(2)}, u32[]{:S(2)}) collective-permute-start(bf16[256,256]{1,0:T(8,128)(2,1)S(1)} %fusion.15), channel_id=1, source_target_pairs={{0,2},{2,0},{1,3},{3,1},{4,6},{6,4},{5,7},{7,5},{8,10},{10,8},{9,1... | collective-permute-start | bytes 393224 | tf_op jit(solution)/shard_map/ppermute | solution.py:21
  138.3 16.1 %collective-permute-start.10 = (bf16[32,3584]{1,0:T(8,128)(2,1)}, bf16[32,3584]{1,0:T(8,128)(2,1)S(1)}, u32[]{:S(2)}, u32[]{:S(2)}) collective-permute-start(bf16[32,3584]{1,0:T(8,128)(2,1)} %pad_maximum_fusion.5), channel_id=1, source_target_pairs={{0,1},{1,0},{2,3},{3,2},{4,5},{5,4},{6,7},{7,6},{8,9},{9,8},{10,11... | collective-permute-start | bytes 688136 | tf_op jit(solution)/shard_map/ppermute | solution.py:21
  142.5 1.3 collective-permute-start.19
  146.0 27.3 %all-to-all-start.4 = ((bf16[64,4,896]{2,1,0:T(4,128)(2,1)}), bf16[64,4,896]{2,1,0:T(4,128)(2,1)S(1)}, u32[]{:S(2)}, u32[]{:S(2)}) async-start(bf16[64,4,896]{2,1,0:T(4,128)(2,1)} %reshape.221), calls=%async_computation.4 | async-start | bytes 917504 | tf_op jit(solution)/shard_map/all_to_all | solution.py:25

commit v2 on v1

--- a/solution.py
+++ b/solution.py
@@ -92,11 +92,15 @@
     depth = out_proj.shape[0] // n_z
     proj = out_proj.T.reshape(cols, n_z, depth).transpose(1, 0, 2)
     proj = exchange(proj, "z")
+    values = attention(queries, latent_cache, lengths, value_up)
+    proj, values = lax.optimization_barrier((proj, values))
     half = n_z // 2
+    proj_leaving = lax.dynamic_slice_in_dim(proj, (1 - xl) * half, half, 0)
+    proj_other = flip(proj_leaving, "xl")
     proj_mine = lax.dynamic_slice_in_dim(proj, xl * half, half, 0)
-    proj_other = flip(lax.dynamic_slice_in_dim(proj, (1 - xl) * half, half, 0), "xl")
-    proj_both = jnp.stack([proj_mine, proj_other])
-    over_y = jnp.stack([proj_both] + [flip(proj_both, "y", s) for s in range(1, n_y)])
+    over_y = jnp.concatenate([proj_mine, proj_other], axis=0)
+    over_y = jnp.stack([over_y] + [flip(over_y, "y", s) for s in range(1, n_y)])
+    over_y = over_y.reshape(n_y, 2, half, cols, depth)
     over_y = jnp.stack(
         [lax.dynamic_index_in_dim(over_y, y ^ s, 0, keepdims=False) for s in range(n_y)], axis=2
     )
@@ -111,7 +115,6 @@
     swap = [(i, (i % 2) * 2 + i // 2) for i in range(4)]
     routes_sent = lax.ppermute(routes, ("xh", "core"), swap)
 
-    values = attention(queries, latent_cache, lengths, value_up)
     values = values.reshape(rows_here, n_z, depth).transpose(1, 0, 2)
     values = exchange(values, "z").reshape(n_z * rows_here, depth)
     from_xl = flip(values, "xl")

time: 175 us -> 170 us (0.971)
    all_to_all x5, waiting for transfers between devices: 41.8 us -> 37.2 us  [exchange(): return lax.all_to_all(value, axis, split_axis=0, concat_axis=0, tiled=True)]
    ppermute x20, waiting for transfers between devices: 35.1 us -> 38.3 us  [flip(): return lax.ppermute(value, axis, [(i, i ^ mask) for i in range(count)])]
    all_to_all x5, starting transfers between devices: 37.5 us -> 35.4 us  [exchange(): return lax.all_to_all(value, axis, split_axis=0, concat_axis=0, tiled=True)]
    reshape x1, local copies, waits for them, and re-layouts: 1.93 us -> 0.05 us  [attention(): return values.astype(bf16).reshape(queries.shape[0], -1)]
    another operation x2 -> x1, other arithmetic: 2 us -> 0.23 us  [shards(): over_y = jnp.stack([over_y] + [flip(over_y, 'y', s) for s in range(1, n_y)])]
  transfers between devices with their start and end apart: 26 -> 26, of which waited for: 13 -> 14; matrix products, arithmetic and copies ran while one was open for 18% -> 18% of each run, Pallas kernels for 0% -> 0%
where the time goes in v2:
time: 170 us; the launch traced here: 169 us
  waiting for transfers between devices  75.5 us (44%)
  starting transfers between devices  56.2 us (33%)
  matrix products  20.5 us (12%)
  local copies, waits for them, and re-layouts  9.53 us (6%)
  other arithmetic  6.16 us (4%)
    ppermute x20, waiting for transfers between devices, flip(): return lax.ppermute(value, axis, [(i, i ^ mask) for i in range(count)])  38.3 us
    all_to_all x5, waiting for transfers between devices, exchange(): return lax.all_to_all(value, axis, split_axis=0, concat_axis=0, tiled=True)  37.2 us
    all_to_all x5, starting transfers between devices, exchange(): return lax.all_to_all(value, axis, split_axis=0, concat_axis=0, tiled=True)  35.4 us
    ppermute x20, starting transfers between devices, flip(): return lax.ppermute(value, axis, [(i, i ^ mask) for i in range(count)])  20.2 us
    dot_general x1, matrix products, attention(): jnp.einsum('rhj,rjc->rhc', weights, latent_cache[:, :, :LATENT], preferre...  4.02 us
  transfers between devices with their start and end apart: 26, of which 14 were waited for; matrix products, arithmetic and copies ran while one was open for 18% of the time, Pallas kernels for 0%

profile of v2, /device:TPU:32, one launch (start us, length us, event | category | flops | bytes accessed | tf_op | source)
XLA Modules:
  0.0 169.0 jit_solution(9929879932223619748)
XLA Ops:
  0.7 1.3 copy.72
  1.9 0.9 copy.60
  2.8 8.6 %all-to-all-start = ((bf16[8,56,512]{2,1,0:T(8,128)(2,1)}), bf16[8,56,512]{2,1,0:T(8,128)(2,1)S(1)}, u32[]{:S(2)}, u32[]{:S(2)}) async-start(bf16[8,56,512]{2,1,0:T(8,128)(2,1)} %copy.60), calls=%async_computation | async-start | bytes 917504 | tf_op jit(solution)/shard_map/all_to_all | solution.py:25
  11.5 3.2 %fusion.12 = f32[32,32,128]{2,1,0:T(8,128)S(1)} fusion(bf16[32,32,576]{2,1,0:T(8,128)(2,1)S(1)} %copy-done, bf16[32,128,576]{1,2,0:T(8,128)(2,1)} %param.13, pred[32,128]{1,0:T(8,128)(4,1)S(1)} %iota_compare_fusion.6), kind=kOutput, calls=%fused_computation.19 | convolution fusion | flops 151257088 | bytes 6426624 | tf_op jit(solution)/shard_map/rhc,rjc->rhj/dot_general | solution.py:38
  15.1 4.0 %fusion.3 = bf16[32,32,512]{2,1,0:T(8,128)(2,1)S(1)} fusion(bf16[32,128,576]{1,2,0:T(8,128)(2,1)} %param.13, f32[32,32]{1,0:T(8,128)S(1)} %fusion.94, f32[32,32,128]{2,1,0:T(8,128)S(1)} %fusion.12), kind=kOutput, calls=%fused_computation.5 | convolution fusion | flops 135136384 | bytes 6307840 | tf_op jit(solution)/shard_map/rhj,rjc->rhc/dot_general | solution.py:48
  19.1 3.3 %fusion.13 = bf16[32,4,8,128]{3,2,1,0:T(8,128)(2,1)S(1)} fusion(bf16[32,512,128]{2,1,0:T(8,128)(2,1)} %param.15, bf16[32,32,512]{2,1,0:T(8,128)(2,1)S(1)} %fusion.3), kind=kOutput, calls=%fused_computation.21 | convolution fusion | flops 134348800 | bytes 5505024 | tf_op jit(solution)/shard_map/rhc,hcv->rhv/dot_general | solution.py:51
  22.4 3.6 %all-to-all-done = bf16[8,56,512]{2,1,0:T(8,128)(2,1)S(1)} async-done(((bf16[8,56,512]{2,1,0:T(8,128)(2,1)}), bf16[8,56,512]{2,1,0:T(8,128)(2,1)S(1)}, u32[]{:S(2)}, u32[]{:S(2)}) %all-to-all-start) | async-done | bytes 458784 | tf_op jit(solution)/shard_map/all_to_all | solution.py:25
  26.1 1.6 collective-permute-start.1
  27.7 0.8 copy.64
  28.5 4.8 %all-to-all-start.1 = ((bf16[8,32,512]{2,1,0:T(8,128)(2,1)}), bf16[8,32,512]{2,1,0:T(8,128)(2,1)S(1)}, u32[]{:S(2)}, u32[]{:S(2)}) async-start(bf16[8,32,512]{2,1,0:T(8,128)(2,1)} %copy.64), calls=%async_computation.1 | async-start | bytes 524288 | tf_op jit(solution)/shard_map/all_to_all | solution.py:25
  33.4 1.7 collective-permute-start.2
  35.0 2.9 %collective-permute-start.3 = (bf16[8,56,512]{2,1,0:T(8,128)(2,1)S(1)}, bf16[8,56,512]{2,1,0:T(8,128)(2,1)S(1)}, u32[]{:S(2)}, u32[]{:S(2)}) collective-permute-start(bf16[8,56,512]{2,1,0:T(8,128)(2,1)S(1)} %pad_maximum_fusion.4), channel_id=1, source_target_pairs={{0,8},{4,12},{8,0},{12,4},{1,9},{5,13},{9,1},{13,5},{2,10},{6,14},... | collective-permute-start | bytes 1376264 | tf_op jit(solution)/shard_map/ppermute | solution.py:21
  38.1 5.7 %all-to-all-done.1 = bf16[8,32,512]{2,1,0:T(8,128)(2,1)S(1)} async-done(((bf16[8,32,512]{2,1,0:T(8,128)(2,1)}), bf16[8,32,512]{2,1,0:T(8,128)(2,1)S(1)}, u32[]{:S(2)}, u32[]{:S(2)}) %all-to-all-start.1) | async-done | bytes 262176 | tf_op jit(solution)/shard_map/all_to_all | solution.py:25
  43.8 0.5 collective-permute-start.5
  44.4 2.8 %collective-permute-start.6 = (bf16[256,512]{1,0:T(8,128)(2,1)S(1)}, bf16[256,512]{1,0:T(8,128)(2,1)S(1)}, u32[]{:S(2)}, u32[]{:S(2)}) collective-permute-start(bf16[256,512]{1,0:T(8,128)(2,1)S(1)} %bitcast.108), channel_id=1, source_target_pairs={{0,130},{2,128},{128,2},{130,0},{1,131},{3,129},{129,3},{131,1},{4... | collective-permute-start | bytes 786440 | tf_op jit(solution)/shard_map/ppermute | solution.py:21
  47.1 2.5 %collective-permute-start = (bf16[256,512]{1,0:T(8,128)(2,1)S(1)}, bf16[256,512]{1,0:T(8,128)(2,1)S(1)}, u32[]{:S(2)}, u32[]{:S(2)}) collective-permute-start(bf16[256,512]{1,0:T(8,128)(2,1)S(1)} %bitcast.109), channel_id=1, source_target_pairs={{0,128},{128,0},{1,129},{129,1},{2,130},{130,2},{3,131},{131,3},{4... | collective-permute-start | bytes 786440 | tf_op jit(solution)/shard_map/ppermute | solution.py:21
  49.6 8.0 %collective-permute-done.3 = bf16[8,56,512]{2,1,0:T(8,128)(2,1)S(1)} collective-permute-done((bf16[8,56,512]{2,1,0:T(8,128)(2,1)S(1)}, bf16[8,56,512]{2,1,0:T(8,128)(2,1)S(1)}, u32[]{:S(2)}, u32[]{:S(2)}) %collective-permute-start.3) | collective-permute-done | bytes 458784 | tf_op jit(solution)/shard_map/ppermute | solution.py:21
  57.6 2.6 %collective-permute-done.4 = bf16[8,56,512]{2,1,0:T(8,128)(2,1)S(1)} collective-permute-done((bf16[8,56,512]{2,1,0:T(8,128)(2,1)S(1)}, bf16[8,56,512]{2,1,0:T(8,128)(2,1)S(1)}, u32[]{:S(2)}, u32[]{:S(2)}) %collective-permute-start.4) | collective-permute-done | bytes 458784 | tf_op jit(solution)/shard_map/ppermute | solution.py:21
  62.5 1.3 collective-permute-done.7
  63.8 1.3 fusion.8
  65.1 7.4 %all-to-all-start.2 = ((bf16[8,32,896]{2,1,0:T(8,128)(2,1)}), bf16[8,32,896]{2,1,0:T(8,128)(2,1)S(1)}, u32[]{:S(2)}, u32[]{:S(2)}) async-start(bf16[8,32,896]{2,1,0:T(8,128)(2,1)} %bitcast.15), calls=%async_computation.2 | async-start | bytes 917504 | tf_op jit(solution)/shard_map/all_to_all | solution.py:25
  72.5 0.7 collective-permute-start.11
  73.2 2.5 %dynamic-slice_bitcast_fusion = (bf16[256,896]{1,0:T(8,128)(2,1)}, bf16[256,896]{1,0:T(8,128)(2,1)}, bf16[256,896]{1,0:T(8,128)(2,1)}) fusion(bf16[1,256,3584]{2,1,0:T(8,128)(2,1)} %param.23, s32[]{:T(128)S(6)} %select_n.164, s32[]{:T(128)S(6)} %select_n.162, s32[]{:T(128)S(6)} %select_n.163), kind=kLoop, calls=%fused_computation.76 | loop fusion | bytes 2752524 | tf_op jit(solution)/shard_map/dynamic_slice | solution.py:112
  75.6 4.1 %collective-permute-start.16 = (bf16[256,896]{1,0:T(8,128)(2,1)}, bf16[256,896]{1,0:T(8,128)(2,1)S(1)}, u32[]{:S(2)}, u32[]{:S(2)}) collective-permute-start(bf16[256,896]{1,0:T(8,128)(2,1)} %get-tuple-element.13), channel_id=1, source_target_pairs={{0,1},{1,0},{2,3},{3,2},{4,5},{5,4},{6,7},{7,6},{8,9},{9,8},{10,11... | collective-permute-start | bytes 1376264 | tf_op jit(solution)/shard_map/ppermute | solution.py:21
  80.0 1.4 collective-permute-start.20
  81.5 1.2 select_reduce_fusion.1
  83.0 4.5 %all-to-all-done.2 = bf16[8,32,896]{2,1,0:T(8,128)(2,1)S(1)} async-done(((bf16[8,32,896]{2,1,0:T(8,128)(2,1)}), bf16[8,32,896]{2,1,0:T(8,128)(2,1)S(1)}, u32[]{:S(2)}, u32[]{:S(2)}) %all-to-all-start.2) | async-done | bytes 458784 | tf_op jit(solution)/shard_map/all_to_all | solution.py:25
  87.8 1.2 copy.68
  89.0 6.0 %all-to-all-start.3 = ((bf16[64,4,896]{2,1,0:T(4,128)(2,1)}), bf16[64,4,896]{2,1,0:T(4,128)(2,1)S(1)}, u32[]{:S(2)}, u32[]{:S(2)}) async-start(bf16[64,4,896]{2,1,0:T(4,128)(2,1)} %copy.68), calls=%async_computation.3 | async-start | bytes 917504 | tf_op jit(solution)/shard_map/all_to_all | solution.py:25
  95.6 12.8 %collective-permute-done.8 = bf16[32,896]{1,0:T(8,128)(2,1)S(1)} collective-permute-done((bf16[32,896]{1,0:T(8,128)(2,1)S(1)}, bf16[32,896]{1,0:T(8,128)(2,1)S(1)}, u32[]{:S(2)}, u32[]{:S(2)}) %collective-permute-start.8) | collective-permute-done | bytes 57376 | tf_op jit(solution)/shard_map/ppermute | solution.py:21
  108.6 5.2 %all-to-all-done.3 = bf16[64,4,896]{2,1,0:T(4,128)(2,1)S(1)} async-done(((bf16[64,4,896]{2,1,0:T(4,128)(2,1)}), bf16[64,4,896]{2,1,0:T(4,128)(2,1)S(1)}, u32[]{:S(2)}, u32[]{:S(2)}) %all-to-all-start.3) | async-done | bytes 458784 | tf_op jit(solution)/shard_map/all_to_all | solution.py:25
  113.9 0.5 collective-permute-start.13
  114.6 1.2 collective-permute-done.9
  115.8 0.9 broadcast_select_fusion.8
  116.8 7.4 %collective-permute-done.13 = bf16[2,128,896]{2,1,0:T(8,128)(2,1)S(1)} collective-permute-done((bf16[2,128,896]{2,1,0:T(8,128)(2,1)S(1)}, bf16[2,128,896]{2,1,0:T(8,128)(2,1)S(1)}, u32[]{:S(2)}, u32[]{:S(2)}) %collective-permute-start.13) | collective-permute-done | bytes 458784 | tf_op jit(solution)/shard_map/ppermute | solution.py:21
  124.1 0.7 pad_maximum_fusion.5
  124.9 1.0 collective-permute-done.14
  126.9 1.2 copy-done.6
  131.2 0.9 collective-permute-start.17
  132.2 1.3 fusion.34
  133.7 3.4 %collective-permute-done.17 = bf16[256,256]{1,0:T(8,128)(2,1)S(1)} collective-permute-done((bf16[256,256]{1,0:T(8,128)(2,1)S(1)}, bf16[256,256]{1,0:T(8,128)(2,1)S(1)}, u32[]{:S(2)}, u32[]{:S(2)}) %collective-permute-start.17) | collective-permute-done | bytes 131104 | tf_op jit(solution)/shard_map/ppermute | solution.py:21
  137.7 0.7 collective-permute-done.19
  138.4 1.3 fusion.9
  139.7 0.9 reshape.238
  140.6 8.6 %all-to-all-start.4 = ((bf16[64,4,896]{2,1,0:T(4,128)(2,1)}), bf16[64,4,896]{2,1,0:T(4,128)(2,1)S(1)}, u32[]{:S(2)}, u32[]{:S(2)}) async-start(bf16[64,4,896]{2,1,0:T(4,128)(2,1)} %reshape.238), calls=%async_computation.4 | async-start | bytes 917504 | tf_op jit(solution)/shard_map/all_to_all | solution.py:25
  149.2 0.7 broadcast_select_fusion.6
  150.0 18.2 %all-to-all-done.4 = bf16[64,4,896]{2,1,0:T(4,128)(2,1)S(1)} async-done(((bf16[64,4,896]{2,1,0:T(4,128)(2,1)}), bf16[64,4,896]{2,1,0:T(4,128)(2,1)S(1)}, u32[]{:S(2)}, u32[]{:S(2)}) %all-to-all-start.4) | async-done | bytes 458784 | tf_op jit(solution)/shard_map/all_to_all | solution.py:25
  168.2 0.9 fusion.16
  (83 shorter events, 9.9 us)
Async XLA Ops:
  0.6 10.9 %copy-start = (bf16[32,32,576]{2,1,0:T(8,128)(2,1)S(1)}, bf16[32,32,576]{2,1,0:T(8,128)(2,1)}, u32[]{:S(2)}) copy-start(bf16[32,32,576]{2,1,0:T(8,128)(2,1)} %param.12) | copy-start | bytes 3538948
  0.6 10.8 %copy-start.5 = (s32[32]{0:T(128)S(1)}, s32[32]{0:T(128)}, u32[]{:S(2)}) copy-start(s32[32]{0:T(128)} %param.14) | copy-start | bytes 388
  2.8 23.2 %all-to-all-start = ((bf16[8,56,512]{2,1,0:T(8,128)(2,1)}), bf16[8,56,512]{2,1,0:T(8,128)(2,1)S(1)}, u32[]{:S(2)}, u32[]{:S(2)}) async-start(bf16[8,56,512]{2,1,0:T(8,128)(2,1)} %copy.60), calls=%async_computation | async-start | bytes 917504 | tf_op jit(solution)/shard_map/all_to_all | solution.py:25
  26.1 7.2 %collective-permute-start.1 = (bf16[4,56,512]{2,1,0:T(8,128)(2,1)S(1)}, bf16[4,56,512]{2,1,0:T(8,128)(2,1)S(1)}, u32[]{:S(2)}, u32[]{:S(2)}) collective-permute-start(bf16[4,56,512]{2,1,0:T(8,128)(2,1)S(1)} %get-tuple-element.28), channel_id=1, source_target_pairs={{0,2},{2,0},{1,3},{3,1},{4,6},{6,4},{5,7},{7,5},{8,10},{10,8},{9,1... | collective-permute-start | bytes 688136 | tf_op jit(solution)/shard_map/ppermute | solution.py:21
  28.5 15.3 %all-to-all-start.1 = ((bf16[8,32,512]{2,1,0:T(8,128)(2,1)}), bf16[8,32,512]{2,1,0:T(8,128)(2,1)S(1)}, u32[]{:S(2)}, u32[]{:S(2)}) async-start(bf16[8,32,512]{2,1,0:T(8,128)(2,1)} %copy.64), calls=%async_computation.1 | async-start | bytes 524288 | tf_op jit(solution)/shard_map/all_to_all | solution.py:25
  33.4 13.8 %collective-permute-start.2 = (bf16[8,56,512]{2,1,0:T(8,128)(2,1)S(1)}, bf16[8,56,512]{2,1,0:T(8,128)(2,1)S(1)}, u32[]{:S(2)}, u32[]{:S(2)}) collective-permute-start(bf16[8,56,512]{2,1,0:T(8,128)(2,1)S(1)} %pad_maximum_fusion.4), channel_id=1, source_target_pairs={{0,4},{4,0},{8,12},{12,8},{1,5},{5,1},{9,13},{13,9},{2,6},{6,2},{1... | collective-permute-start | bytes 1376264 | tf_op jit(solution)/shard_map/ppermute | solution.py:21
  35.0 22.6 %collective-permute-start.3 = (bf16[8,56,512]{2,1,0:T(8,128)(2,1)S(1)}, bf16[8,56,512]{2,1,0:T(8,128)(2,1)S(1)}, u32[]{:S(2)}, u32[]{:S(2)}) collective-permute-start(bf16[8,56,512]{2,1,0:T(8,128)(2,1)S(1)} %pad_maximum_fusion.4), channel_id=1, source_target_pairs={{0,8},{4,12},{8,0},{12,4},{1,9},{5,13},{9,1},{13,5},{2,10},{6,14},... | collective-permute-start | bytes 1376264 | tf_op jit(solution)/shard_map/ppermute | solution.py:21
  37.9 22.3 %collective-permute-start.4 = (bf16[8,56,512]{2,1,0:T(8,128)(2,1)S(1)}, bf16[8,56,512]{2,1,0:T(8,128)(2,1)S(1)}, u32[]{:S(2)}, u32[]{:S(2)}) collective-permute-start(bf16[8,56,512]{2,1,0:T(8,128)(2,1)S(1)} %pad_maximum_fusion.4), channel_id=1, source_target_pairs={{0,12},{4,8},{8,4},{12,0},{1,13},{5,9},{9,5},{13,1},{2,14},{6,10},... | collective-permute-start | bytes 1376264 | tf_op jit(solution)/shard_map/ppermute | solution.py:21
  43.8 17.1 %collective-permute-start.5 = (bf16[256,512]{1,0:T(8,128)(2,1)S(1)}, bf16[256,512]{1,0:T(8,128)(2,1)S(1)}, u32[]{:S(2)}, u32[]{:S(2)}) collective-permute-start(bf16[256,512]{1,0:T(8,128)(2,1)S(1)} %bitcast.107), channel_id=1, source_target_pairs={{0,2},{2,0},{1,3},{3,1},{4,6},{6,4},{5,7},{7,5},{8,10},{10,8},{9,1... | collective-permute-start | bytes 786440 | tf_op jit(solution)/shard_map/ppermute | solution.py:21
  44.4 16.6 %collective-permute-start.6 = (bf16[256,512]{1,0:T(8,128)(2,1)S(1)}, bf16[256,512]{1,0:T(8,128)(2,1)S(1)}, u32[]{:S(2)}, u32[]{:S(2)}) collective-permute-start(bf16[256,512]{1,0:T(8,128)(2,1)S(1)} %bitcast.108), channel_id=1, source_target_pairs={{0,130},{2,128},{128,2},{130,0},{1,131},{3,129},{129,3},{131,1},{4... | collective-permute-start | bytes 786440 | tf_op jit(solution)/shard_map/ppermute | solution.py:21
  47.1 14.3 %collective-permute-start = (bf16[256,512]{1,0:T(8,128)(2,1)S(1)}, bf16[256,512]{1,0:T(8,128)(2,1)S(1)}, u32[]{:S(2)}, u32[]{:S(2)}) collective-permute-start(bf16[256,512]{1,0:T(8,128)(2,1)S(1)} %bitcast.109), channel_id=1, source_target_pairs={{0,128},{128,0},{1,129},{129,1},{2,130},{130,2},{3,131},{131,3},{4... | collective-permute-start | bytes 786440 | tf_op jit(solution)/shard_map/ppermute | solution.py:21
  61.9 1.9 %collective-permute-start.7 = (bf16[256,896]{1,0:T(8,128)(2,1)S(1)}, bf16[256,896]{1,0:T(8,128)(2,1)S(1)}, u32[]{:S(2)}, u32[]{:S(2)}) collective-permute-start(bf16[256,896]{1,0:T(8,128)(2,1)S(1)} %fusion.10), channel_id=1, source_target_pairs={{0,1},{1,0},{2,3},{3,2},{4,5},{5,4},{6,7},{7,6},{8,9},{9,8},{10,11... | collective-permute-start | bytes 1376264 | tf_op jit(solution)/shard_map/ppermute | solution.py:21
  62.5 10.0 %copy-start.2 = (s32[32,8]{0,1:T(8,128)S(1)}, s32[32,8]{0,1:T(8,128)}, u32[]{:S(2)}) copy-start(s32[32,8]{0,1:T(8,128)} %param.18) | copy-start | bytes 3076
  65.1 16.4 %copy-start.4 = (s32[256]{0:T(256)S(1)}, s32[256]{0:T(256)}, u32[]{:S(2)}) copy-start(s32[256]{0:T(256)} %param.20) | copy-start | bytes 3076
  65.1 22.3 %all-to-all-start.2 = ((bf16[8,32,896]{2,1,0:T(8,128)(2,1)}), bf16[8,32,896]{2,1,0:T(8,128)(2,1)S(1)}, u32[]{:S(2)}, u32[]{:S(2)}) async-start(bf16[8,32,896]{2,1,0:T(8,128)(2,1)} %bitcast.15), calls=%async_computation.2 | async-start | bytes 917504 | tf_op jit(solution)/shard_map/all_to_all | solution.py:25
  72.5 9.0 %collective-permute-start.11 = (s32[32,8]{0,1:T(8,128)S(1)}, s32[32,8]{0,1:T(8,128)S(1)}, u32[]{:S(2)}, u32[]{:S(2)}) collective-permute-start(s32[32,8]{0,1:T(8,128)S(1)} %copy-done.2), channel_id=1, source_target_pairs={{0,0},{1,128},{128,1},{129,129},{2,2},{3,130},{130,3},{131,131},{4... | collective-permute-start | bytes 3080 | tf_op jit(solution)/shard_map/ppermute | solution.py:116
  75.6 19.4 %copy-start.1 = (f32[3584]{0:T(1024)S(1)}, f32[3584]{0:T(1024)}, u32[]{:S(2)}) copy-start(f32[3584]{0:T(1024)} %param.17) | copy-start | bytes 43012
  75.6 19.4 %copy-start.3 = (f32[32,8]{0,1:T(8,128)S(1)}, f32[32,8]{0,1:T(8,128)}, u32[]{:S(2)}) copy-start(f32[32,8]{0,1:T(8,128)} %param.19) | copy-start | bytes 3076
  75.6 57.9 %collective-permute-start.16 = (bf16[256,896]{1,0:T(8,128)(2,1)}, bf16[256,896]{1,0:T(8,128)(2,1)S(1)}, u32[]{:S(2)}, u32[]{:S(2)}) collective-permute-start(bf16[256,896]{1,0:T(8,128)(2,1)} %get-tuple-element.13), channel_id=1, source_target_pairs={{0,1},{1,0},{2,3},{3,2},{4,5},{5,4},{6,7},{7,6},{8,9},{9,8},{10,11... | collective-permute-start | bytes 1376264 | tf_op jit(solution)/shard_map/ppermute | solution.py:21
  79.7 57.6 %collective-permute-start.18 = (bf16[256,896]{1,0:T(8,128)(2,1)}, bf16[256,896]{1,0:T(8,128)(2,1)S(1)}, u32[]{:S(2)}, u32[]{:S(2)}) collective-permute-start(bf16[256,896]{1,0:T(8,128)(2,1)} %get-tuple-element.14), channel_id=1, source_target_pairs={{0,2},{1,3},{2,0},{3,1},{4,6},{5,7},{6,4},{7,5},{8,10},{9,11},{10,... | collective-permute-start | bytes 1376264 | tf_op jit(solution)/shard_map/ppermute | solution.py:21
  80.0 57.7 %collective-permute-start.20 = (bf16[256,896]{1,0:T(8,128)(2,1)}, bf16[256,896]{1,0:T(8,128)(2,1)}, u32[]{:S(2)}, u32[]{:S(2)}) collective-permute-start(bf16[256,896]{1,0:T(8,128)(2,1)} %get-tuple-element.12), channel_id=1, source_target_pairs={{0,3},{1,2},{2,1},{3,0},{4,7},{5,6},{6,5},{7,4},{8,11},{9,10},{10,... | collective-permute-start | bytes 1376264 | tf_op jit(solution)/shard_map/ppermute | solution.py:21
  89.0 24.8 %all-to-all-start.3 = ((bf16[64,4,896]{2,1,0:T(4,128)(2,1)}), bf16[64,4,896]{2,1,0:T(4,128)(2,1)S(1)}, u32[]{:S(2)}, u32[]{:S(2)}) async-start(bf16[64,4,896]{2,1,0:T(4,128)(2,1)} %copy.68), calls=%async_computation.3 | async-start | bytes 917504 | tf_op jit(solution)/shard_map/all_to_all | solution.py:25
  95.3 13.1 %collective-permute-start.8 = (bf16[32,896]{1,0:T(8,128)(2,1)S(1)}, bf16[32,896]{1,0:T(8,128)(2,1)S(1)}, u32[]{:S(2)}, u32[]{:S(2)}) collective-permute-start(bf16[32,896]{1,0:T(8,128)(2,1)S(1)} %reduce_sum.85), channel_id=1, source_target_pairs={{0,2},{2,0},{1,3},{3,1},{4,6},{6,4},{5,7},{7,5},{8,10},{10,8},{9,1... | collective-permute-start | bytes 172040 | tf_op jit(solution)/shard_map/ppermute | solution.py:21
  108.5 7.3 %collective-permute-start.9 = (bf16[32,1792]{1,0:T(8,128)(2,1)S(1)}, bf16[32,1792]{1,0:T(8,128)(2,1)}, u32[]{:S(2)}, u32[]{:S(2)}) collective-permute-start(bf16[32,1792]{1,0:T(8,128)(2,1)S(1)} %pad_maximum_fusion.6), channel_id=1, source_target_pairs={{0,128},{128,0},{1,129},{129,1},{2,130},{130,2},{3,131},{131,3},{4... | collective-permute-start | bytes 344072 | tf_op jit(solution)/shard_map/ppermute | solution.py:21
  113.9 10.2 %collective-permute-start.13 = (bf16[2,128,896]{2,1,0:T(8,128)(2,1)S(1)}, bf16[2,128,896]{2,1,0:T(8,128)(2,1)S(1)}, u32[]{:S(2)}, u32[]{:S(2)}) collective-permute-start(bf16[2,128,896]{2,1,0:T(8,128)(2,1)S(1)} %reshape.237), channel_id=1, source_target_pairs={{0,2},{2,0},{1,3},{3,1},{4,6},{6,4},{5,7},{7,5},{8,10},{10,8},{9,1... | collective-permute-start | bytes 1376264 | tf_op jit(solution)/shard_map/ppermute | solution.py:21
  115.8 9.0 %collective-permute-start.12 = (bf16[2,128,896]{2,1,0:T(8,128)(2,1)S(1)}, bf16[2,128,896]{2,1,0:T(8,128)(2,1)S(1)}, u32[]{:S(2)}, u32[]{:S(2)}) collective-permute-start(bf16[2,128,896]{2,1,0:T(8,128)(2,1)S(1)} %reshape.237), channel_id=1, source_target_pairs={{0,1},{1,0},{2,3},{3,2},{4,5},{5,4},{6,7},{7,6},{8,9},{9,8},{10,11... | collective-permute-start | bytes 1376264 | tf_op jit(solution)/shard_map/ppermute | solution.py:21
  124.1 1.8 %collective-permute-start.14 = (bf16[2,128,896]{2,1,0:T(8,128)(2,1)S(1)}, bf16[2,128,896]{2,1,0:T(8,128)(2,1)S(1)}, u32[]{:S(2)}, u32[]{:S(2)}) collective-permute-start(bf16[2,128,896]{2,1,0:T(8,128)(2,1)S(1)} %collective-permute-done.13), channel_id=1, source_target_pairs={{0,1},{1,0},{2,3},{3,2},{4,5},{5,4},{6,7},{7,6},{8,9},{9,8},{10,11... | collective-permute-start | bytes 1376264 | tf_op jit(solution)/shard_map/ppermute | solution.py:21
  126.0 2.4 %copy-start.7 = (bf16[1,3584,256]{2,1,0:T(8,128)(2,1)S(1)}, bf16[1,3584,256]{2,1,0:T(8,128)(2,1)}, u32[]{:S(2)}) copy-start(bf16[1,3584,256]{2,1,0:T(8,128)(2,1)} %param.22) | copy-start | bytes 5505028
  126.4 1.7 copy-start.6
  131.0 6.0 %collective-permute-start.15 = (bf16[256,256]{1,0:T(8,128)(2,1)S(1)}, bf16[256,256]{1,0:T(8,128)(2,1)S(1)}, u32[]{:S(2)}, u32[]{:S(2)}) collective-permute-start(bf16[256,256]{1,0:T(8,128)(2,1)S(1)} %fusion.15), channel_id=1, source_target_pairs={{0,1},{1,0},{2,3},{3,2},{4,5},{5,4},{6,7},{7,6},{8,9},{9,8},{10,11... | collective-permute-start | bytes 393224 | tf_op jit(solution)/shard_map/ppermute | solution.py:21
  131.2 5.8 %collective-permute-start.17 = (bf16[256,256]{1,0:T(8,128)(2,1)S(1)}, bf16[256,256]{1,0:T(8,128)(2,1)S(1)}, u32[]{:S(2)}, u32[]{:S(2)}) collective-permute-start(bf16[256,256]{1,0:T(8,128)(2,1)S(1)} %fusion.15), channel_id=1, source_target_pairs={{0,2},{2,0},{1,3},{3,1},{4,6},{6,4},{5,7},{7,5},{8,10},{10,8},{9,1... | collective-permute-start | bytes 393224 | tf_op jit(solution)/shard_map/ppermute | solution.py:21
  133.5 15.7 %collective-permute-start.10 = (bf16[32,3584]{1,0:T(8,128)(2,1)}, bf16[32,3584]{1,0:T(8,128)(2,1)S(1)}, u32[]{:S(2)}, u32[]{:S(2)}) collective-permute-start(bf16[32,3584]{1,0:T(8,128)(2,1)} %pad_maximum_fusion.5), channel_id=1, source_target_pairs={{0,1},{1,0},{2,3},{3,2},{4,5},{5,4},{6,7},{7,6},{8,9},{9,8},{10,11... | collective-permute-start | bytes 688136 | tf_op jit(solution)/shard_map/ppermute | solution.py:21
  137.0 1.3 collective-permute-start.19
  140.6 27.6 %all-to-all-start.4 = ((bf16[64,4,896]{2,1,0:T(4,128)(2,1)}), bf16[64,4,896]{2,1,0:T(4,128)(2,1)S(1)}, u32[]{:S(2)}, u32[]{:S(2)}) async-start(bf16[64,4,896]{2,1,0:T(4,128)(2,1)} %reshape.238), calls=%async_computation.4 | async-start | bytes 917504 | tf_op jit(solution)/shard_map/all_to_all | solution.py:25

commit v3 on v2

--- a/solution.py
+++ b/solution.py
@@ -99,7 +99,14 @@
     proj_other = flip(proj_leaving, "xl")
     proj_mine = lax.dynamic_slice_in_dim(proj, xl * half, half, 0)
     over_y = jnp.concatenate([proj_mine, proj_other], axis=0)
-    over_y = jnp.stack([over_y] + [flip(over_y, "y", s) for s in range(1, n_y)])
+    over_y = [over_y] + [flip(over_y, "y", s) for s in range(1, n_y)]
+    values = values.reshape(rows_here, n_z, depth).transpose(1, 0, 2)
+    values = exchange(values, "z").reshape(n_z * rows_here, depth)
+    from_xh = flip(values, "xh")
+    from_both = flip(values, ("xh", "xl"), 3)
+    over_y[1], values_late = lax.optimization_barrier((over_y[1], values))
+    from_xl = flip(values_late, "xl")
+    over_y = jnp.stack(over_y)
     over_y = over_y.reshape(n_y, 2, half, cols, depth)
     over_y = jnp.stack(
         [lax.dynamic_index_in_dim(over_y, y ^ s, 0, keepdims=False) for s in range(n_y)], axis=2
@@ -107,19 +114,6 @@
     proj_own = over_y[0].reshape(quarter, depth)
     proj_oth = over_y[1].reshape(quarter, depth)
 
-    down = []
-    for s in range(n_tensor):
-        piece = lax.dynamic_slice_in_dim(w_down[0], (tensor_at ^ s) * quarter, quarter, 1)
-        down.append(flip(piece, TENSOR, s) if s else piece)
-
-    swap = [(i, (i % 2) * 2 + i // 2) for i in range(4)]
-    routes_sent = lax.ppermute(routes, ("xh", "core"), swap)
-
-    values = values.reshape(rows_here, n_z, depth).transpose(1, 0, 2)
-    values = exchange(values, "z").reshape(n_z * rows_here, depth)
-    from_xl = flip(values, "xl")
-    from_xh = flip(values, "xh")
-    from_both = flip(values, ("xh", "xl"), 3)
     here = xh == core
     keep_own, send_own = pair(here, values, from_xh)
     keep_oth, send_oth = pair(here, from_xl, from_both)
@@ -127,51 +121,80 @@
     partial_got = flip(partial_send, "core")
     partial = dot_t(keep_own, proj_own) + dot_t(keep_oth, proj_oth) + partial_got.astype(f32)
     partial = partial.astype(bf16).reshape(n_z, rows_here, quarter)
+    w_down, partial, routes_late = lax.optimization_barrier((w_down, partial, routes))
     partial = exchange(partial, "z")
+    swap = [(i, (i % 2) * 2 + i // 2) for i in range(4)]
+    routes_sent = lax.ppermute(routes_late, ("xh", "core"), swap)
+
+    down = []
+    for s in range(n_tensor):
+        piece = lax.dynamic_slice_in_dim(w_down[0], (tensor_at ^ s) * quarter, quarter, 1)
+        down.append(flip(piece, TENSOR, s) if s else piece)
+
     part_rows = jnp.sum(partial.astype(f32), axis=0).astype(bf16)
 
     _, slots_sent = placing(routes_sent, expert_home, owners)
     outgoing = jnp.einsum(
         "roc,rd->ocd", slots_sent.astype(bf16), part_rows, preferred_element_type=f32
     ).astype(bf16)
+    outgoing, w_gate, w_up = lax.optimization_barrier((outgoing, w_gate, w_up))
     incoming = exchange(outgoing, DP).reshape(2, -1, quarter)
 
+    def folded(weight, side):
+        weight = weight.reshape(2, 2, quarter, -1)
+        gains = norm_gain.reshape(2, 2, quarter, 1)
+        weight = lax.dynamic_index_in_dim(weight, side, 1, keepdims=False)
+        gains = lax.dynamic_index_in_dim(gains, side, 1, keepdims=False)
+        return (weight.astype(f32) * gains).astype(bf16)
+
+    halves = [[folded(w, side) for w in (w_gate, w_up)] for side in (xl, 1 - xl)]
+    halves, incoming = lax.optimization_barrier((halves, incoming))
     in_xl = flip(incoming, "xl")
     in_core = flip(incoming, "core")
     in_both = flip(in_xl, "core")
-    own_xl = jnp.concatenate(pair(core == 0, incoming, in_core), axis=1)
-    oth_xl = jnp.concatenate(pair(core == 0, in_xl, in_both), axis=1)
-    xl_zero, xl_one = pair(xl == 0, own_xl, oth_xl)
-    stacked = [xl_zero[0], xl_one[0], xl_zero[1], xl_one[1]]
-    stacked_f = [piece.astype(f32) for piece in stacked]
-    mean_square = sum(jnp.sum(p * p, axis=1, keepdims=True) for p in stacked_f) / width
-    scale = lax.rsqrt(mean_square + norm_eps)
-    gate_out, up_out = 0.0, 0.0
-    for q in range(n_tensor):
-        span = slice(q * quarter, (q + 1) * quarter)
-        normed = (stacked_f[q] * scale * norm_gain[span]).astype(bf16)
-        gate_out += jnp.dot(normed, w_gate[0, span], preferred_element_type=f32)
-        up_out += jnp.dot(normed, w_up[0, span], preferred_element_type=f32)
-    hidden = (jax.nn.silu(gate_out) * up_out).astype(bf16)
+
+    def from_half(pieces, weights):
+        squares, gate_out, up_out = 0.0, 0.0, 0.0
+        for i in (0, 1):
+            rows = pieces[i].astype(f32)
+            squares += jnp.sum(rows * rows, axis=1, keepdims=True)
+            gate_out += jnp.dot(pieces[i], weights[0][i], preferred_element_type=f32)
+            up_out += jnp.dot(pieces[i], weights[1][i], preferred_element_type=f32)
+        return squares, gate_out, up_out
+
+    def hidden_of(own_half, other_half):
+        squares, gate_out, up_out = (
+            one + two
+            for one, two in zip(from_half(own_half, halves[0]), from_half(other_half, halves[1]))
+        )
+        scale = lax.rsqrt(squares / width + norm_eps)
+        return (jax.nn.silu(gate_out * scale) * (up_out * scale)).astype(bf16)
+
+    hidden = jnp.concatenate(
+        pair(core == 0, hidden_of(incoming, in_xl), hidden_of(in_core, in_both)), axis=0
+    )
     hid_xl = flip(hidden, "xl")
     hid_core = flip(hidden, "core")
+    result = jnp.dot(hidden, down[0], preferred_element_type=f32)
+    result += jnp.dot(hid_core, down[1], preferred_element_type=f32)
+    result, hid_xl = lax.optimization_barrier((result, hid_xl))
     hid_both = flip(hid_xl, "core")
-    result = 0.0
-    for piece, weight in zip((hidden, hid_core, hid_xl, hid_both), down):
-        result += jnp.dot(piece, weight, preferred_element_type=f32)
-    returned = exchange(result.astype(bf16).reshape(owners, MOST, quarter), DP)
-
-    on_owner, slot_map = placing(routes, expert_home, owners)
-    share_weight = jnp.sum(jnp.where(on_owner, route_weight[:, :, None], 0.0), axis=1)
-    combine_weight = slot_map.astype(f32) * share_weight[:, :, None]
-    experts_out = jnp.einsum("roc,ocd->rd", combine_weight, returned.astype(f32)).astype(bf16)
-
+    result += jnp.dot(hid_xl, down[2], preferred_element_type=f32)
+    result += jnp.dot(hid_both, down[3], preferred_element_type=f32)
     row_xl = flip(part_rows, "xl")
     lower, upper = pair(xl == 0, part_rows, row_xl)
     mine = jnp.concatenate([lower, upper], axis=1)
     row_xh = flip(mine, "xh")
     lower, upper = pair(xh == 0, mine, row_xh)
     whole = jnp.concatenate([lower, upper], axis=1)
+    whole, result = lax.optimization_barrier((whole, result))
+    returned = exchange(result.astype(bf16).reshape(owners, MOST, quarter), DP)
+
+    on_owner, slot_map = placing(routes, expert_home, owners)
+    share_weight = jnp.sum(jnp.where(on_owner, route_weight[:, :, None], 0.0), axis=1)
+    combine_weight = slot_map.astype(f32) * share_weight[:, :, None]
+    experts_out = jnp.einsum("roc,ocd->rd", combine_weight, returned.astype(f32)).astype(bf16)
+
     attended = jnp.where(here, whole, flip(whole, "core"))
     return (attended, experts_out)
 

time: 170 us -> 169 us (level)
  waiting for transfers between devices: 75.5 us -> 65.8 us
  matrix products: 20.5 us -> 28.2 us
    ppermute x20, waiting for transfers between devices: 38.3 us -> 32.5 us  [flip(): return lax.ppermute(value, axis, [(i, i ^ mask) for i in range(count)])]
    dot_general x12 -> x20, matrix products: 6.12 us -> 11.1 us  [the longest x8 3.91 us: from_half(): gate_out += jnp.dot(pieces[i], weights[0][i], preferred_element_type=f32)]
    all_to_all x5, waiting for transfers between devices: 37.2 us -> 33.3 us  [exchange(): return lax.all_to_all(value, axis, split_axis=0, concat_axis=0, tiled=True)]
    convert_element_type x0 -> x1, other arithmetic: none -> 3.58 us  [folded(): return (weight.astype(f32) * gains).astype(bf16)]
    dot_general x4, matrix products: 2.69 us -> 5.44 us  [dot_t(): lax.dot_general(left, right, (((1,), (1,)), ((), ())), preferred_element_...]
  transfers between devices with their start and end apart: 26 -> 26, of which waited for: 14 -> 13; matrix products, arithmetic and copies ran while one was open for 18% -> 22% of each run, Pallas kernels for 0% -> 0%
where the time goes in v3:
time: 169 us; the launch traced here: 168 us
  waiting for transfers between devices  65.8 us (39%)
  starting transfers between devices  56 us (33%)
  matrix products  28.2 us (17%)
  local copies, waits for them, and re-layouts  8.57 us (5%)
  other arithmetic  7.85 us (5%)
    all_to_all x5, starting transfers between devices, exchange(): return lax.all_to_all(value, axis, split_axis=0, concat_axis=0, tiled=True)  36.7 us
    all_to_all x5, waiting for transfers between devices, exchange(): return lax.all_to_all(value, axis, split_axis=0, concat_axis=0, tiled=True)  33.3 us
    ppermute x20, waiting for transfers between devices, flip(): return lax.ppermute(value, axis, [(i, i ^ mask) for i in range(count)])  32.5 us
    ppermute x20, starting transfers between devices, flip(): return lax.ppermute(value, axis, [(i, i ^ mask) for i in range(count)])  18.7 us
    dot_general x4, matrix products, dot_t(): lax.dot_general(left, right, (((1,), (1,)), ((), ())), preferred_element_...  5.44 us
    dot_general x1, matrix products, attention(): jnp.einsum('rhj,rjc->rhc', weights, latent_cache[:, :, :LATENT], preferre...  4.02 us
    dot_general x8, matrix products, from_half(): gate_out += jnp.dot(pieces[i], weights[0][i], preferred_element_type=f32)  3.91 us
    convert_element_type x1, other arithmetic, folded(): return (weight.astype(f32) * gains).astype(bf16)  3.58 us
  transfers between devices with their start and end apart: 26, of which 13 were waited for; matrix products, arithmetic and copies ran while one was open for 22% of the time, Pallas kernels for 0%

profile of v3, /device:TPU:32, one launch (start us, length us, event | category | flops | bytes accessed | tf_op | source)
XLA Modules:
  0.0 167.6 jit_solution(8787091083202271354)
XLA Ops:
  0.7 1.3 copy.88
  1.9 0.9 copy.70
  2.8 8.6 %all-to-all-start = ((bf16[8,56,512]{2,1,0:T(8,128)(2,1)}), bf16[8,56,512]{2,1,0:T(8,128)(2,1)S(1)}, u32[]{:S(2)}, u32[]{:S(2)}) async-start(bf16[8,56,512]{2,1,0:T(8,128)(2,1)} %copy.70), calls=%async_computation | async-start | bytes 917504 | tf_op jit(solution)/shard_map/all_to_all | solution.py:25
  11.5 3.2 %fusion.15 = f32[32,32,128]{2,1,0:T(8,128)S(1)} fusion(bf16[32,32,576]{2,1,0:T(8,128)(2,1)S(1)} %copy-done, bf16[32,128,576]{1,2,0:T(8,128)(2,1)} %param.13, pred[32,128]{1,0:T(8,128)(4,1)S(1)} %iota_compare_fusion.6), kind=kOutput, calls=%fused_computation.24 | convolution fusion | flops 151257088 | bytes 6426624 | tf_op jit(solution)/shard_map/rhc,rjc->rhj/dot_general | solution.py:38
  15.1 4.0 %fusion.7 = bf16[32,32,512]{2,1,0:T(8,128)(2,1)S(1)} fusion(bf16[32,128,576]{1,2,0:T(8,128)(2,1)} %param.13, f32[32,32]{1,0:T(8,128)S(1)} %fusion.112, f32[32,32,128]{2,1,0:T(8,128)S(1)} %fusion.15), kind=kOutput, calls=%fused_computation.13 | convolution fusion | flops 135136384 | bytes 6307840 | tf_op jit(solution)/shard_map/rhj,rjc->rhc/dot_general | solution.py:48
  19.1 3.3 %fusion.16 = bf16[32,4,8,128]{3,2,1,0:T(8,128)(2,1)S(1)} fusion(bf16[32,512,128]{2,1,0:T(8,128)(2,1)} %param.15, bf16[32,32,512]{2,1,0:T(8,128)(2,1)S(1)} %fusion.7), kind=kOutput, calls=%fused_computation.26 | convolution fusion | flops 134348800 | bytes 5505024 | tf_op jit(solution)/shard_map/rhc,hcv->rhv/dot_general | solution.py:51
  22.4 3.6 %all-to-all-done = bf16[8,56,512]{2,1,0:T(8,128)(2,1)S(1)} async-done(((bf16[8,56,512]{2,1,0:T(8,128)(2,1)}), bf16[8,56,512]{2,1,0:T(8,128)(2,1)S(1)}, u32[]{:S(2)}, u32[]{:S(2)}) %all-to-all-start) | async-done | bytes 458784 | tf_op jit(solution)/shard_map/all_to_all | solution.py:25
  26.1 1.6 collective-permute-start.1
  27.7 0.8 copy.74
  28.5 4.8 %all-to-all-start.1 = ((bf16[8,32,512]{2,1,0:T(8,128)(2,1)}), bf16[8,32,512]{2,1,0:T(8,128)(2,1)S(1)}, u32[]{:S(2)}, u32[]{:S(2)}) async-start(bf16[8,32,512]{2,1,0:T(8,128)(2,1)} %copy.74), calls=%async_computation.1 | async-start | bytes 524288 | tf_op jit(solution)/shard_map/all_to_all | solution.py:25
  33.3 1.7 collective-permute-start.2
  35.0 2.2 %collective-permute-start.4 = (bf16[8,56,512]{2,1,0:T(8,128)(2,1)S(1)}, bf16[8,56,512]{2,1,0:T(8,128)(2,1)S(1)}, u32[]{:S(2)}, u32[]{:S(2)}) collective-permute-start(bf16[8,56,512]{2,1,0:T(8,128)(2,1)S(1)} %pad_maximum_fusion.2), channel_id=1, source_target_pairs={{0,12},{4,8},{8,4},{12,0},{1,13},{5,9},{9,5},{13,1},{2,14},{6,10},... | collective-permute-start | bytes 1376264 | tf_op jit(solution)/shard_map/ppermute | solution.py:21
  37.2 0.7 collective-permute-start.3
  37.9 5.9 %all-to-all-done.1 = bf16[8,32,512]{2,1,0:T(8,128)(2,1)S(1)} async-done(((bf16[8,32,512]{2,1,0:T(8,128)(2,1)}), bf16[8,32,512]{2,1,0:T(8,128)(2,1)S(1)}, u32[]{:S(2)}, u32[]{:S(2)}) %all-to-all-start.1) | async-done | bytes 262176 | tf_op jit(solution)/shard_map/all_to_all | solution.py:25
  43.8 2.1 %collective-permute-start.6 = (bf16[256,512]{1,0:T(8,128)(2,1)S(1)}, bf16[256,512]{1,0:T(8,128)(2,1)S(1)}, u32[]{:S(2)}, u32[]{:S(2)}) collective-permute-start(bf16[256,512]{1,0:T(8,128)(2,1)S(1)} %bitcast.188), channel_id=1, source_target_pairs={{0,130},{2,128},{128,2},{130,0},{1,131},{3,129},{129,3},{131,1},{4... | collective-permute-start | bytes 786440 | tf_op jit(solution)/shard_map/ppermute | solution.py:21
  46.9 1.0 collective-permute-start.5
  47.9 8.1 %collective-permute-done.4 = bf16[8,56,512]{2,1,0:T(8,128)(2,1)S(1)} collective-permute-done((bf16[8,56,512]{2,1,0:T(8,128)(2,1)S(1)}, bf16[8,56,512]{2,1,0:T(8,128)(2,1)S(1)}, u32[]{:S(2)}, u32[]{:S(2)}) %collective-permute-start.4) | collective-permute-done | bytes 458784 | tf_op jit(solution)/shard_map/ppermute | solution.py:21
  56.0 1.5 collective-permute-done.3
  58.9 1.2 fusion.13
  60.3 1.5 fusion.74
  62.4 2.3 %fusion.12 = bf16[256,896]{1,0:T(8,128)(2,1)} fusion(f32[256,896]{1,0:T(8,128)S(1)} %fusion.74, bf16[896,512]{1,0:T(8,128)(2,1)S(1)} %bitcast.187, bf16[256,896]{1,0:T(8,128)(2,1)} %collective-permute-done.7, bf16[256,512]{1,0:T(8,128)(2,1)S(1)} %bitcast.192, bf16[256,512]{1,0:T(8,128)(2,1)S(1)} %copy-done.6, pred[]{:T(512)S(6)} %eq.44), kind=kOutput, calls=%fused_computation.19 | convolution fusion | flops 235929600 | bytes 3276801 | tf_op jit(solution)/shard_map/dot_general | solution.py:29
  64.7 7.4 %all-to-all-start.2 = ((bf16[8,32,896]{2,1,0:T(8,128)(2,1)}), bf16[8,32,896]{2,1,0:T(8,128)(2,1)S(1)}, u32[]{:S(2)}, u32[]{:S(2)}) async-start(bf16[8,32,896]{2,1,0:T(8,128)(2,1)} %bitcast.15), calls=%async_computation.2 | async-start | bytes 917504 | tf_op jit(solution)/shard_map/all_to_all | solution.py:25
  72.2 0.7 collective-permute-start.10
  72.9 2.4 %dynamic-slice_bitcast_fusion.1 = (bf16[256,896]{1,0:T(8,128)(2,1)}, bf16[256,896]{1,0:T(8,128)(2,1)}, bf16[256,896]{1,0:T(8,128)(2,1)}) fusion(bf16[1,256,3584]{2,1,0:T(8,128)(2,1)} %param.23, s32[]{:T(128)S(6)} %select_n.151, s32[]{:T(128)S(6)} %select_n.152, s32[]{:T(128)S(6)} %select_n.150), kind=kLoop, calls=%fused_computation.77 | loop fusion | bytes 2752524 | tf_op jit(solution)/shard_map/dynamic_slice | solution.py:131
  75.3 4.1 %collective-permute-start.15 = (bf16[256,896]{1,0:T(8,128)(2,1)}, bf16[256,896]{1,0:T(8,128)(2,1)}, u32[]{:S(2)}, u32[]{:S(2)}) collective-permute-start(bf16[256,896]{1,0:T(8,128)(2,1)} %get-tuple-element.52), channel_id=1, source_target_pairs={{0,1},{1,0},{2,3},{3,2},{4,5},{5,4},{6,7},{7,6},{8,9},{9,8},{10,11... | collective-permute-start | bytes 1376264 | tf_op jit(solution)/shard_map/ppermute | solution.py:21
  79.6 1.1 collective-permute-start.19
  80.8 1.2 select_reduce_fusion
  82.4 4.5 %all-to-all-done.2 = bf16[8,32,896]{2,1,0:T(8,128)(2,1)S(1)} async-done(((bf16[8,32,896]{2,1,0:T(8,128)(2,1)}), bf16[8,32,896]{2,1,0:T(8,128)(2,1)S(1)}, u32[]{:S(2)}, u32[]{:S(2)}) %all-to-all-start.2) | async-done | bytes 458784 | tf_op jit(solution)/shard_map/all_to_all | solution.py:25
  88.0 1.2 copy.78
  89.2 7.9 %all-to-all-start.3 = ((bf16[64,4,896]{2,1,0:T(4,128)(2,1)}), bf16[64,4,896]{2,1,0:T(4,128)(2,1)S(1)}, u32[]{:S(2)}, u32[]{:S(2)}) async-start(bf16[64,4,896]{2,1,0:T(4,128)(2,1)} %copy.78), calls=%async_computation.3 | async-start | bytes 917504 | tf_op jit(solution)/shard_map/all_to_all | solution.py:25
  97.1 10.6 %collective-permute-done.8 = bf16[32,896]{1,0:T(8,128)(2,1)S(1)} collective-permute-done((bf16[32,896]{1,0:T(8,128)(2,1)S(1)}, bf16[32,896]{1,0:T(8,128)(2,1)S(1)}, u32[]{:S(2)}, u32[]{:S(2)}) %collective-permute-start.8) | collective-permute-done | bytes 57376 | tf_op jit(solution)/shard_map/ppermute | solution.py:21
  107.9 3.6 %fusion.4 = (bf16[2,896,256]{2,1,0:T(8,128)(2,1)S(1)}, bf16[2,896,256]{2,1,0:T(8,128)(2,1)}, bf16[2,896,256]{2,1,0:T(8,128)(2,1)}, bf16[2,896,256]{2,1,0:T(8,128)(2,1)}) fusion(f32[2,896]{1,0:T(2,128)S(1)} %get-tuple-element.75, bf16[2,2,896,256]{3,2,1,0:T(8,128)(2,1)} %bitcast.195, s32[]{:T(128)S(6)} %select_n.146, f32[2,896]{1,0:T(2,128)S(1)} %get-tuple-element.76, ...), kind=kLoop, calls=%fused_computation.8 | loop fusion | flops 5505024 | bytes 7354376 | tf_op jit(solution)/shard_map/convert_element_type | solution.py:148
  111.5 2.9 %collective-permute-done.9 = bf16[32,1792]{1,0:T(8,128)(2,1)S(1)} collective-permute-done((bf16[32,1792]{1,0:T(8,128)(2,1)S(1)}, bf16[32,1792]{1,0:T(8,128)(2,1)S(1)}, u32[]{:S(2)}, u32[]{:S(2)}) %collective-permute-start.9) | collective-permute-done | bytes 114720 | tf_op jit(solution)/shard_map/ppermute | solution.py:21
  114.5 1.1 all-to-all-done.3
  115.7 0.7 collective-permute-start.11
  116.4 1.2 fusion.51
  117.6 1.2 convolution_add_fusion.10
  119.6 6.1 %collective-permute-done.11 = bf16[2,128,896]{2,1,0:T(8,128)(2,1)S(1)} collective-permute-done((bf16[2,128,896]{2,1,0:T(8,128)(2,1)S(1)}, bf16[2,128,896]{2,1,0:T(8,128)(2,1)S(1)}, u32[]{:S(2)}, u32[]{:S(2)}) %collective-permute-start.11) | collective-permute-done | bytes 458784 | tf_op jit(solution)/shard_map/ppermute | solution.py:21
  130.6 1.3 fusion.27
  132.0 1.3 convolution_add_fusion.2
  133.3 2.2 %collective-permute-done.16 = bf16[256,256]{1,0:T(8,128)(2,1)S(1)} collective-permute-done((bf16[256,256]{1,0:T(8,128)(2,1)S(1)}, bf16[256,256]{1,0:T(8,128)(2,1)S(1)}, u32[]{:S(2)}, u32[]{:S(2)}) %collective-permute-start.16) | collective-permute-done | bytes 131104 | tf_op jit(solution)/shard_map/ppermute | solution.py:21
  135.5 1.3 fusion.113
  136.9 1.3 add_add_fusion
  139.0 0.9 reshape.165
  139.9 8.0 %all-to-all-start.4 = ((bf16[64,4,896]{2,1,0:T(4,128)(2,1)}), bf16[64,4,896]{2,1,0:T(4,128)(2,1)S(1)}, u32[]{:S(2)}, u32[]{:S(2)}) async-start(bf16[64,4,896]{2,1,0:T(4,128)(2,1)} %reshape.165), calls=%async_computation.4 | async-start | bytes 917504 | tf_op jit(solution)/shard_map/all_to_all | solution.py:25
  147.9 0.7 broadcast_select_fusion
  148.6 18.1 %all-to-all-done.4 = bf16[64,4,896]{2,1,0:T(4,128)(2,1)S(1)} async-done(((bf16[64,4,896]{2,1,0:T(4,128)(2,1)}), bf16[64,4,896]{2,1,0:T(4,128)(2,1)S(1)}, u32[]{:S(2)}, u32[]{:S(2)}) %all-to-all-start.4) | async-done | bytes 458784 | tf_op jit(solution)/shard_map/all_to_all | solution.py:25
  166.7 0.9 fusion.25
  (106 shorter events, 12.0 us)
Async XLA Ops:
  0.6 10.9 %copy-start = (bf16[32,32,576]{2,1,0:T(8,128)(2,1)S(1)}, bf16[32,32,576]{2,1,0:T(8,128)(2,1)}, u32[]{:S(2)}) copy-start(bf16[32,32,576]{2,1,0:T(8,128)(2,1)} %param.12) | copy-start | bytes 3538948
  0.6 10.8 %copy-start.12 = (s32[32]{0:T(128)S(1)}, s32[32]{0:T(128)}, u32[]{:S(2)}) copy-start(s32[32]{0:T(128)} %param.14) | copy-start | bytes 388
  2.8 23.2 %all-to-all-start = ((bf16[8,56,512]{2,1,0:T(8,128)(2,1)}), bf16[8,56,512]{2,1,0:T(8,128)(2,1)S(1)}, u32[]{:S(2)}, u32[]{:S(2)}) async-start(bf16[8,56,512]{2,1,0:T(8,128)(2,1)} %copy.70), calls=%async_computation | async-start | bytes 917504 | tf_op jit(solution)/shard_map/all_to_all | solution.py:25
  26.1 7.2 %collective-permute-start.1 = (bf16[4,56,512]{2,1,0:T(8,128)(2,1)S(1)}, bf16[4,56,512]{2,1,0:T(8,128)(2,1)S(1)}, u32[]{:S(2)}, u32[]{:S(2)}) collective-permute-start(bf16[4,56,512]{2,1,0:T(8,128)(2,1)S(1)} %get-tuple-element.64), channel_id=1, source_target_pairs={{0,2},{2,0},{1,3},{3,1},{4,6},{6,4},{5,7},{7,5},{8,10},{10,8},{9,1... | collective-permute-start | bytes 688136 | tf_op jit(solution)/shard_map/ppermute | solution.py:21
  28.5 15.3 %all-to-all-start.1 = ((bf16[8,32,512]{2,1,0:T(8,128)(2,1)}), bf16[8,32,512]{2,1,0:T(8,128)(2,1)S(1)}, u32[]{:S(2)}, u32[]{:S(2)}) async-start(bf16[8,32,512]{2,1,0:T(8,128)(2,1)} %copy.74), calls=%async_computation.1 | async-start | bytes 524288 | tf_op jit(solution)/shard_map/all_to_all | solution.py:25
  33.3 13.5 %collective-permute-start.2 = (bf16[8,56,512]{2,1,0:T(8,128)(2,1)S(1)}, bf16[8,56,512]{2,1,0:T(8,128)(2,1)S(1)}, u32[]{:S(2)}, u32[]{:S(2)}) collective-permute-start(bf16[8,56,512]{2,1,0:T(8,128)(2,1)S(1)} %pad_maximum_fusion.2), channel_id=1, source_target_pairs={{0,4},{4,0},{8,12},{12,8},{1,5},{5,1},{9,13},{13,9},{2,6},{6,2},{1... | collective-permute-start | bytes 1376264 | tf_op jit(solution)/shard_map/ppermute | solution.py:21
  35.0 21.0 %collective-permute-start.4 = (bf16[8,56,512]{2,1,0:T(8,128)(2,1)S(1)}, bf16[8,56,512]{2,1,0:T(8,128)(2,1)S(1)}, u32[]{:S(2)}, u32[]{:S(2)}) collective-permute-start(bf16[8,56,512]{2,1,0:T(8,128)(2,1)S(1)} %pad_maximum_fusion.2), channel_id=1, source_target_pairs={{0,12},{4,8},{8,4},{12,0},{1,13},{5,9},{9,5},{13,1},{2,14},{6,10},... | collective-permute-start | bytes 1376264 | tf_op jit(solution)/shard_map/ppermute | solution.py:21
  37.2 20.4 %collective-permute-start.3 = (bf16[8,56,512]{2,1,0:T(8,128)(2,1)S(1)}, bf16[8,56,512]{2,1,0:T(8,128)(2,1)S(1)}, u32[]{:S(2)}, u32[]{:S(2)}) collective-permute-start(bf16[8,56,512]{2,1,0:T(8,128)(2,1)S(1)} %pad_maximum_fusion.2), channel_id=1, source_target_pairs={{0,8},{4,12},{8,0},{12,4},{1,9},{5,13},{9,1},{13,5},{2,10},{6,14},... | collective-permute-start | bytes 1376264 | tf_op jit(solution)/shard_map/ppermute | solution.py:21
  43.8 14.6 %collective-permute-start.6 = (bf16[256,512]{1,0:T(8,128)(2,1)S(1)}, bf16[256,512]{1,0:T(8,128)(2,1)S(1)}, u32[]{:S(2)}, u32[]{:S(2)}) collective-permute-start(bf16[256,512]{1,0:T(8,128)(2,1)S(1)} %bitcast.188), channel_id=1, source_target_pairs={{0,130},{2,128},{128,2},{130,0},{1,131},{3,129},{129,3},{131,1},{4... | collective-permute-start | bytes 786440 | tf_op jit(solution)/shard_map/ppermute | solution.py:21
  45.9 13.0 %collective-permute-start = (bf16[256,512]{1,0:T(8,128)(2,1)S(1)}, bf16[256,512]{1,0:T(8,128)(2,1)S(1)}, u32[]{:S(2)}, u32[]{:S(2)}) collective-permute-start(bf16[256,512]{1,0:T(8,128)(2,1)S(1)} %bitcast.189), channel_id=1, source_target_pairs={{0,128},{128,0},{1,129},{129,1},{2,130},{130,2},{3,131},{131,3},{4... | collective-permute-start | bytes 786440 | tf_op jit(solution)/shard_map/ppermute | solution.py:21
  46.9 11.5 %collective-permute-start.5 = (bf16[256,512]{1,0:T(8,128)(2,1)S(1)}, bf16[256,512]{1,0:T(8,128)(2,1)S(1)}, u32[]{:S(2)}, u32[]{:S(2)}) collective-permute-start(bf16[256,512]{1,0:T(8,128)(2,1)S(1)} %bitcast.190), channel_id=1, source_target_pairs={{0,2},{2,0},{1,3},{3,1},{4,6},{6,4},{5,7},{7,5},{8,10},{10,8},{9,1... | collective-permute-start | bytes 786440 | tf_op jit(solution)/shard_map/ppermute | solution.py:21
  58.4 1.8 %copy-start.3 = (bf16[256,512]{1,0:T(8,128)(2,1)}, bf16[256,512]{1,0:T(8,128)(2,1)S(1)}, u32[]{:S(2)}) copy-start(bf16[256,512]{1,0:T(8,128)(2,1)S(1)} %collective-permute-done.6) | copy-start | bytes 786436
  58.4 1.8 %copy-start.4 = (bf16[256,512]{1,0:T(8,128)(2,1)}, bf16[256,512]{1,0:T(8,128)(2,1)S(1)}, u32[]{:S(2)}) copy-start(bf16[256,512]{1,0:T(8,128)(2,1)S(1)} %collective-permute-done.5) | copy-start | bytes 786436
  58.9 1.4 copy-start.8
  58.9 1.3 copy-start.5
  60.2 2.2 %collective-permute-start.7 = (bf16[256,896]{1,0:T(8,128)(2,1)}, bf16[256,896]{1,0:T(8,128)(2,1)}, u32[]{:S(2)}, u32[]{:S(2)}) collective-permute-start(bf16[256,896]{1,0:T(8,128)(2,1)} %fusion.13), channel_id=1, source_target_pairs={{0,1},{1,0},{2,3},{3,2},{4,5},{5,4},{6,7},{7,6},{8,9},{9,8},{10,11... | collective-permute-start | bytes 1376264 | tf_op jit(solution)/shard_map/ppermute | solution.py:21
  60.3 2.1 %copy-start.6 = (bf16[256,512]{1,0:T(8,128)(2,1)S(1)}, bf16[256,512]{1,0:T(8,128)(2,1)}, u32[]{:S(2)}) copy-start(bf16[256,512]{1,0:T(8,128)(2,1)} %copy-done.5) | copy-start | bytes 786436
  61.8 10.3 %copy-start.10 = (s32[32,8]{0,1:T(8,128)S(1)}, s32[32,8]{0,1:T(8,128)}, u32[]{:S(2)}) copy-start(s32[32,8]{0,1:T(8,128)} %param.18) | copy-start | bytes 3076
  61.8 10.3 %copy-start.9 = (f32[32,8]{0,1:T(8,128)S(1)}, f32[32,8]{0,1:T(8,128)}, u32[]{:S(2)}) copy-start(f32[32,8]{0,1:T(8,128)} %param.19) | copy-start | bytes 3076
  64.7 16.2 %copy-start.11 = (s32[256]{0:T(256)S(1)}, s32[256]{0:T(256)}, u32[]{:S(2)}) copy-start(s32[256]{0:T(256)} %param.20) | copy-start | bytes 3076
  64.7 22.3 %all-to-all-start.2 = ((bf16[8,32,896]{2,1,0:T(8,128)(2,1)}), bf16[8,32,896]{2,1,0:T(8,128)(2,1)S(1)}, u32[]{:S(2)}, u32[]{:S(2)}) async-start(bf16[8,32,896]{2,1,0:T(8,128)(2,1)} %bitcast.15), calls=%async_computation.2 | async-start | bytes 917504 | tf_op jit(solution)/shard_map/all_to_all | solution.py:25
  72.2 8.5 %collective-permute-start.10 = (s32[32,8]{0,1:T(8,128)S(1)}, s32[32,8]{0,1:T(8,128)S(1)}, u32[]{:S(2)}, u32[]{:S(2)}) collective-permute-start(s32[32,8]{0,1:T(8,128)S(1)} %copy-done.10), channel_id=1, source_target_pairs={{0,0},{1,128},{128,1},{129,129},{2,2},{3,130},{130,3},{131,131},{4... | collective-permute-start | bytes 3080 | tf_op jit(solution)/shard_map/ppermute | solution.py:127
  75.3 56.6 %collective-permute-start.15 = (bf16[256,896]{1,0:T(8,128)(2,1)}, bf16[256,896]{1,0:T(8,128)(2,1)}, u32[]{:S(2)}, u32[]{:S(2)}) collective-permute-start(bf16[256,896]{1,0:T(8,128)(2,1)} %get-tuple-element.52), channel_id=1, source_target_pairs={{0,1},{1,0},{2,3},{3,2},{4,5},{5,4},{6,7},{7,6},{8,9},{9,8},{10,11... | collective-permute-start | bytes 1376264 | tf_op jit(solution)/shard_map/ppermute | solution.py:21
  79.4 56.1 %collective-permute-start.17 = (bf16[256,896]{1,0:T(8,128)(2,1)}, bf16[256,896]{1,0:T(8,128)(2,1)}, u32[]{:S(2)}, u32[]{:S(2)}) collective-permute-start(bf16[256,896]{1,0:T(8,128)(2,1)} %get-tuple-element.50), channel_id=1, source_target_pairs={{0,2},{1,3},{2,0},{3,1},{4,6},{5,7},{6,4},{7,5},{8,10},{9,11},{10,... | collective-permute-start | bytes 1376264 | tf_op jit(solution)/shard_map/ppermute | solution.py:21
  79.6 57.2 %collective-permute-start.19 = (bf16[256,896]{1,0:T(8,128)(2,1)}, bf16[256,896]{1,0:T(8,128)(2,1)}, u32[]{:S(2)}, u32[]{:S(2)}) collective-permute-start(bf16[256,896]{1,0:T(8,128)(2,1)} %get-tuple-element.51), channel_id=1, source_target_pairs={{0,3},{1,2},{2,1},{3,0},{4,7},{5,6},{6,5},{7,4},{8,11},{9,10},{10,... | collective-permute-start | bytes 1376264 | tf_op jit(solution)/shard_map/ppermute | solution.py:21
  87.0 20.7 %collective-permute-start.8 = (bf16[32,896]{1,0:T(8,128)(2,1)S(1)}, bf16[32,896]{1,0:T(8,128)(2,1)S(1)}, u32[]{:S(2)}, u32[]{:S(2)}) collective-permute-start(bf16[32,896]{1,0:T(8,128)(2,1)S(1)} %reduce_sum.121), channel_id=1, source_target_pairs={{0,2},{2,0},{1,3},{3,1},{4,6},{6,4},{5,7},{7,5},{8,10},{10,8},{9,1... | collective-permute-start | bytes 172040 | tf_op jit(solution)/shard_map/ppermute | solution.py:21
  89.2 26.4 %all-to-all-start.3 = ((bf16[64,4,896]{2,1,0:T(4,128)(2,1)}), bf16[64,4,896]{2,1,0:T(4,128)(2,1)S(1)}, u32[]{:S(2)}, u32[]{:S(2)}) async-start(bf16[64,4,896]{2,1,0:T(4,128)(2,1)} %copy.78), calls=%async_computation.3 | async-start | bytes 917504 | tf_op jit(solution)/shard_map/all_to_all | solution.py:25
  107.8 6.6 %collective-permute-start.9 = (bf16[32,1792]{1,0:T(8,128)(2,1)S(1)}, bf16[32,1792]{1,0:T(8,128)(2,1)S(1)}, u32[]{:S(2)}, u32[]{:S(2)}) collective-permute-start(bf16[32,1792]{1,0:T(8,128)(2,1)S(1)} %pad_maximum_fusion.5), channel_id=1, source_target_pairs={{0,128},{128,0},{1,129},{129,1},{2,130},{130,2},{3,131},{131,3},{4... | collective-permute-start | bytes 344072 | tf_op jit(solution)/shard_map/ppermute | solution.py:21
  115.7 3.2 %copy-start.2 = (bf16[2,896,256]{2,1,0:T(8,128)(2,1)S(1)}, bf16[2,896,256]{2,1,0:T(8,128)(2,1)}, u32[]{:S(2)}) copy-start(bf16[2,896,256]{2,1,0:T(8,128)(2,1)} %get-tuple-element.33) | copy-start | bytes 2752516
  115.7 10.0 %collective-permute-start.11 = (bf16[2,128,896]{2,1,0:T(8,128)(2,1)S(1)}, bf16[2,128,896]{2,1,0:T(8,128)(2,1)S(1)}, u32[]{:S(2)}, u32[]{:S(2)}) collective-permute-start(bf16[2,128,896]{2,1,0:T(8,128)(2,1)S(1)} %reshape.164), channel_id=1, source_target_pairs={{0,2},{2,0},{1,3},{3,1},{4,6},{6,4},{5,7},{7,5},{8,10},{10,8},{9,1... | collective-permute-start | bytes 1376264 | tf_op jit(solution)/shard_map/ppermute | solution.py:21
  116.4 9.5 %collective-permute-start.12 = (bf16[2,128,896]{2,1,0:T(8,128)(2,1)S(1)}, bf16[2,128,896]{2,1,0:T(8,128)(2,1)S(1)}, u32[]{:S(2)}, u32[]{:S(2)}) collective-permute-start(bf16[2,128,896]{2,1,0:T(8,128)(2,1)S(1)} %reshape.164), channel_id=1, source_target_pairs={{0,1},{1,0},{2,3},{3,2},{4,5},{5,4},{6,7},{7,6},{8,9},{9,8},{10,11... | collective-permute-start | bytes 1376264 | tf_op jit(solution)/shard_map/ppermute | solution.py:21
  119.2 7.1 %copy-start.1 = (bf16[2,896,256]{2,1,0:T(8,128)(2,1)S(1)}, bf16[2,896,256]{2,1,0:T(8,128)(2,1)}, u32[]{:S(2)}) copy-start(bf16[2,896,256]{2,1,0:T(8,128)(2,1)} %get-tuple-element.31) | copy-start | bytes 2752516
  125.7 2.5 %collective-permute-start.13 = (bf16[2,128,896]{2,1,0:T(8,128)(2,1)S(1)}, bf16[2,128,896]{2,1,0:T(8,128)(2,1)S(1)}, u32[]{:S(2)}, u32[]{:S(2)}) collective-permute-start(bf16[2,128,896]{2,1,0:T(8,128)(2,1)S(1)} %collective-permute-done.11), channel_id=1, source_target_pairs={{0,1},{1,0},{2,3},{3,2},{4,5},{5,4},{6,7},{7,6},{8,9},{9,8},{10,11... | collective-permute-start | bytes 1376264 | tf_op jit(solution)/shard_map/ppermute | solution.py:21
  126.6 1.2 copy-start.7
  129.4 2.5 %collective-permute-start.14 = (bf16[256,256]{1,0:T(8,128)(2,1)S(1)}, bf16[256,256]{1,0:T(8,128)(2,1)S(1)}, u32[]{:S(2)}, u32[]{:S(2)}) collective-permute-start(bf16[256,256]{1,0:T(8,128)(2,1)S(1)} %pad_maximum_fusion.4), channel_id=1, source_target_pairs={{0,1},{1,0},{2,3},{3,2},{4,5},{5,4},{6,7},{7,6},{8,9},{9,8},{10,11... | collective-permute-start | bytes 393224 | tf_op jit(solution)/shard_map/ppermute | solution.py:21
  130.0 5.5 %collective-permute-start.16 = (bf16[256,256]{1,0:T(8,128)(2,1)S(1)}, bf16[256,256]{1,0:T(8,128)(2,1)S(1)}, u32[]{:S(2)}, u32[]{:S(2)}) collective-permute-start(bf16[256,256]{1,0:T(8,128)(2,1)S(1)} %pad_maximum_fusion.4), channel_id=1, source_target_pairs={{0,2},{2,0},{1,3},{3,1},{4,6},{6,4},{5,7},{7,5},{8,10},{10,8},{9,1... | collective-permute-start | bytes 393224 | tf_op jit(solution)/shard_map/ppermute | solution.py:21
  135.5 1.3 collective-permute-start.18
  138.2 9.7 %collective-permute-start.20 = (bf16[32,3584]{1,0:T(8,128)(2,1)S(1)}, bf16[32,3584]{1,0:T(8,128)(2,1)S(1)}, u32[]{:S(2)}, u32[]{:S(2)}) collective-permute-start(bf16[32,3584]{1,0:T(8,128)(2,1)S(1)} %pad_maximum_fusion.3), channel_id=1, source_target_pairs={{0,1},{1,0},{2,3},{3,2},{4,5},{5,4},{6,7},{7,6},{8,9},{9,8},{10,11... | collective-permute-start | bytes 688136 | tf_op jit(solution)/shard_map/ppermute | solution.py:21
  139.9 26.8 %all-to-all-start.4 = ((bf16[64,4,896]{2,1,0:T(4,128)(2,1)}), bf16[64,4,896]{2,1,0:T(4,128)(2,1)S(1)}, u32[]{:S(2)}, u32[]{:S(2)}) async-start(bf16[64,4,896]{2,1,0:T(4,128)(2,1)} %reshape.165), calls=%async_computation.4 | async-start | bytes 917504 | tf_op jit(solution)/shard_map/all_to_all | solution.py:25

commit v4 on v3

--- a/solution.py
+++ b/solution.py
@@ -177,17 +177,16 @@
     hid_core = flip(hidden, "core")
     result = jnp.dot(hidden, down[0], preferred_element_type=f32)
     result += jnp.dot(hid_core, down[1], preferred_element_type=f32)
-    result, hid_xl = lax.optimization_barrier((result, hid_xl))
-    hid_both = flip(hid_xl, "core")
-    result += jnp.dot(hid_xl, down[2], preferred_element_type=f32)
-    result += jnp.dot(hid_both, down[3], preferred_element_type=f32)
     row_xl = flip(part_rows, "xl")
     lower, upper = pair(xl == 0, part_rows, row_xl)
     mine = jnp.concatenate([lower, upper], axis=1)
     row_xh = flip(mine, "xh")
     lower, upper = pair(xh == 0, mine, row_xh)
     whole = jnp.concatenate([lower, upper], axis=1)
-    whole, result = lax.optimization_barrier((whole, result))
+    result, hid_xl, whole = lax.optimization_barrier((result, hid_xl, whole))
+    hid_both = flip(hid_xl, "core")
+    result += jnp.dot(hid_xl, down[2], preferred_element_type=f32)
+    result += jnp.dot(hid_both, down[3], preferred_element_type=f32)
     returned = exchange(result.astype(bf16).reshape(owners, MOST, quarter), DP)
 
     on_owner, slot_map = placing(routes, expert_home, owners)

time: 169 us -> 166 us (0.982)
  matrix products: 28.2 us -> 25.4 us
    dot_general x4, matrix products: 5.44 us -> 2.67 us  [dot_t(): lax.dot_general(left, right, (((1,), (1,)), ((), ())), preferred_element_...]
where the time goes in v4:
time: 166 us; the launch traced here: 165 us
  waiting for transfers between devices  66.2 us (40%)
  starting transfers between devices  55.6 us (33%)
  matrix products  25.4 us (15%)
  local copies, waits for them, and re-layouts  8.49 us (5%)
  other arithmetic  7.83 us (5%)
    all_to_all x5, starting transfers between devices, exchange(): return lax.all_to_all(value, axis, split_axis=0, concat_axis=0, tiled=True)  36.4 us
    all_to_all x5, waiting for transfers between devices, exchange(): return lax.all_to_all(value, axis, split_axis=0, concat_axis=0, tiled=True)  33.2 us
    ppermute x20, waiting for transfers between devices, flip(): return lax.ppermute(value, axis, [(i, i ^ mask) for i in range(count)])  33 us
    ppermute x20, starting transfers between devices, flip(): return lax.ppermute(value, axis, [(i, i ^ mask) for i in range(count)])  18.6 us
    dot_general x1, matrix products, attention(): jnp.einsum('rhj,rjc->rhc', weights, latent_cache[:, :, :LATENT], preferre...  4.02 us
    dot_general x8, matrix products, from_half(): gate_out += jnp.dot(pieces[i], weights[0][i], preferred_element_type=f32)  3.91 us
    convert_element_type x1, other arithmetic, folded(): return (weight.astype(f32) * gains).astype(bf16)  3.55 us
  transfers between devices with their start and end apart: 26, of which 13 were waited for; matrix products, arithmetic and copies ran while one was open for 22% of the time, Pallas kernels for 0%

profile of v4, /device:TPU:32, one launch (start us, length us, event | category | flops | bytes accessed | tf_op | source)
XLA Modules:
  0.0 164.7 jit_solution(10992632648081511048)
XLA Ops:
  0.7 1.3 copy.88
  1.9 0.9 copy.70
  2.8 8.6 %all-to-all-start = ((bf16[8,56,512]{2,1,0:T(8,128)(2,1)}), bf16[8,56,512]{2,1,0:T(8,128)(2,1)S(1)}, u32[]{:S(2)}, u32[]{:S(2)}) async-start(bf16[8,56,512]{2,1,0:T(8,128)(2,1)} %copy.70), calls=%async_computation | async-start | bytes 917504 | tf_op jit(solution)/shard_map/all_to_all | solution.py:25
  11.5 3.2 %fusion.15 = f32[32,32,128]{2,1,0:T(8,128)S(1)} fusion(bf16[32,32,576]{2,1,0:T(8,128)(2,1)S(1)} %copy-done, bf16[32,128,576]{1,2,0:T(8,128)(2,1)} %param.13, pred[32,128]{1,0:T(8,128)(4,1)S(1)} %iota_compare_fusion.6), kind=kOutput, calls=%fused_computation.24 | convolution fusion | flops 151257088 | bytes 6426624 | tf_op jit(solution)/shard_map/rhc,rjc->rhj/dot_general | solution.py:38
  15.1 4.0 %fusion.7 = bf16[32,32,512]{2,1,0:T(8,128)(2,1)S(1)} fusion(bf16[32,128,576]{1,2,0:T(8,128)(2,1)} %param.13, f32[32,32]{1,0:T(8,128)S(1)} %fusion.112, f32[32,32,128]{2,1,0:T(8,128)S(1)} %fusion.15), kind=kOutput, calls=%fused_computation.13 | convolution fusion | flops 135136384 | bytes 6307840 | tf_op jit(solution)/shard_map/rhj,rjc->rhc/dot_general | solution.py:48
  19.1 3.3 %fusion.16 = bf16[32,4,8,128]{3,2,1,0:T(8,128)(2,1)S(1)} fusion(bf16[32,512,128]{2,1,0:T(8,128)(2,1)} %param.15, bf16[32,32,512]{2,1,0:T(8,128)(2,1)S(1)} %fusion.7), kind=kOutput, calls=%fused_computation.26 | convolution fusion | flops 134348800 | bytes 5505024 | tf_op jit(solution)/shard_map/rhc,hcv->rhv/dot_general | solution.py:51
  22.4 3.6 %all-to-all-done = bf16[8,56,512]{2,1,0:T(8,128)(2,1)S(1)} async-done(((bf16[8,56,512]{2,1,0:T(8,128)(2,1)}), bf16[8,56,512]{2,1,0:T(8,128)(2,1)S(1)}, u32[]{:S(2)}, u32[]{:S(2)}) %all-to-all-start) | async-done | bytes 458784 | tf_op jit(solution)/shard_map/all_to_all | solution.py:25
  26.1 1.6 collective-permute-start.1
  27.7 0.8 copy.74
  28.5 4.8 %all-to-all-start.1 = ((bf16[8,32,512]{2,1,0:T(8,128)(2,1)}), bf16[8,32,512]{2,1,0:T(8,128)(2,1)S(1)}, u32[]{:S(2)}, u32[]{:S(2)}) async-start(bf16[8,32,512]{2,1,0:T(8,128)(2,1)} %copy.74), calls=%async_computation.1 | async-start | bytes 524288 | tf_op jit(solution)/shard_map/all_to_all | solution.py:25
  33.3 1.7 %collective-permute-start.2 = (bf16[8,56,512]{2,1,0:T(8,128)(2,1)S(1)}, bf16[8,56,512]{2,1,0:T(8,128)(2,1)S(1)}, u32[]{:S(2)}, u32[]{:S(2)}) collective-permute-start(bf16[8,56,512]{2,1,0:T(8,128)(2,1)S(1)} %pad_maximum_fusion.2), channel_id=1, source_target_pairs={{0,4},{4,0},{8,12},{12,8},{1,5},{5,1},{9,13},{13,9},{2,6},{6,2},{1... | collective-permute-start | bytes 1376264 | tf_op jit(solution)/shard_map/ppermute | solution.py:21
  35.0 2.2 %collective-permute-start.4 = (bf16[8,56,512]{2,1,0:T(8,128)(2,1)S(1)}, bf16[8,56,512]{2,1,0:T(8,128)(2,1)S(1)}, u32[]{:S(2)}, u32[]{:S(2)}) collective-permute-start(bf16[8,56,512]{2,1,0:T(8,128)(2,1)S(1)} %pad_maximum_fusion.2), channel_id=1, source_target_pairs={{0,12},{4,8},{8,4},{12,0},{1,13},{5,9},{9,5},{13,1},{2,14},{6,10},... | collective-permute-start | bytes 1376264 | tf_op jit(solution)/shard_map/ppermute | solution.py:21
  37.2 0.7 collective-permute-start.3
  38.1 5.7 %all-to-all-done.1 = bf16[8,32,512]{2,1,0:T(8,128)(2,1)S(1)} async-done(((bf16[8,32,512]{2,1,0:T(8,128)(2,1)}), bf16[8,32,512]{2,1,0:T(8,128)(2,1)S(1)}, u32[]{:S(2)}, u32[]{:S(2)}) %all-to-all-start.1) | async-done | bytes 262176 | tf_op jit(solution)/shard_map/all_to_all | solution.py:25
  43.8 2.1 %collective-permute-start.6 = (bf16[256,512]{1,0:T(8,128)(2,1)S(1)}, bf16[256,512]{1,0:T(8,128)(2,1)S(1)}, u32[]{:S(2)}, u32[]{:S(2)}) collective-permute-start(bf16[256,512]{1,0:T(8,128)(2,1)S(1)} %bitcast.188), channel_id=1, source_target_pairs={{0,130},{2,128},{128,2},{130,0},{1,131},{3,129},{129,3},{131,1},{4... | collective-permute-start | bytes 786440 | tf_op jit(solution)/shard_map/ppermute | solution.py:21
  45.9 0.6 collective-permute-start
  46.9 1.0 collective-permute-start.5
  47.9 8.1 %collective-permute-done.4 = bf16[8,56,512]{2,1,0:T(8,128)(2,1)S(1)} collective-permute-done((bf16[8,56,512]{2,1,0:T(8,128)(2,1)S(1)}, bf16[8,56,512]{2,1,0:T(8,128)(2,1)S(1)}, u32[]{:S(2)}, u32[]{:S(2)}) %collective-permute-start.4) | collective-permute-done | bytes 458784 | tf_op jit(solution)/shard_map/ppermute | solution.py:21
  56.0 1.5 collective-permute-done.3
  59.9 1.3 collective-permute-done.7
  61.2 1.3 fusion.12
  62.5 7.4 %all-to-all-start.2 = ((bf16[8,32,896]{2,1,0:T(8,128)(2,1)}), bf16[8,32,896]{2,1,0:T(8,128)(2,1)S(1)}, u32[]{:S(2)}, u32[]{:S(2)}) async-start(bf16[8,32,896]{2,1,0:T(8,128)(2,1)} %bitcast.15), calls=%async_computation.2 | async-start | bytes 917504 | tf_op jit(solution)/shard_map/all_to_all | solution.py:25
  69.8 0.6 collective-permute-start.8
  70.5 2.4 %dynamic-slice_bitcast_fusion.1 = (bf16[256,896]{1,0:T(8,128)(2,1)}, bf16[256,896]{1,0:T(8,128)(2,1)}, bf16[256,896]{1,0:T(8,128)(2,1)}) fusion(bf16[1,256,3584]{2,1,0:T(8,128)(2,1)} %param.23, s32[]{:T(128)S(6)} %select_n.154, s32[]{:T(128)S(6)} %select_n.155, s32[]{:T(128)S(6)} %select_n.144), kind=kLoop, calls=%fused_computation.77 | loop fusion | bytes 2752524 | tf_op jit(solution)/shard_map/dynamic_slice | solution.py:131
  72.9 4.1 %collective-permute-start.13 = (bf16[256,896]{1,0:T(8,128)(2,1)}, bf16[256,896]{1,0:T(8,128)(2,1)}, u32[]{:S(2)}, u32[]{:S(2)}) collective-permute-start(bf16[256,896]{1,0:T(8,128)(2,1)} %get-tuple-element.50), channel_id=1, source_target_pairs={{0,1},{1,0},{2,3},{3,2},{4,5},{5,4},{6,7},{7,6},{8,9},{9,8},{10,11... | collective-permute-start | bytes 1376264 | tf_op jit(solution)/shard_map/ppermute | solution.py:21
  77.2 1.1 collective-permute-start.20
  78.4 1.2 select_reduce_fusion
  80.2 4.5 %all-to-all-done.2 = bf16[8,32,896]{2,1,0:T(8,128)(2,1)S(1)} async-done(((bf16[8,32,896]{2,1,0:T(8,128)(2,1)}), bf16[8,32,896]{2,1,0:T(8,128)(2,1)S(1)}, u32[]{:S(2)}, u32[]{:S(2)}) %all-to-all-start.2) | async-done | bytes 458784 | tf_op jit(solution)/shard_map/all_to_all | solution.py:25
  85.8 1.2 copy.78
  86.9 7.9 %all-to-all-start.3 = ((bf16[64,4,896]{2,1,0:T(4,128)(2,1)}), bf16[64,4,896]{2,1,0:T(4,128)(2,1)S(1)}, u32[]{:S(2)}, u32[]{:S(2)}) async-start(bf16[64,4,896]{2,1,0:T(4,128)(2,1)} %copy.78), calls=%async_computation.3 | async-start | bytes 917504 | tf_op jit(solution)/shard_map/all_to_all | solution.py:25
  94.9 10.4 %collective-permute-done.15 = bf16[32,896]{1,0:T(8,128)(2,1)S(1)} collective-permute-done((bf16[32,896]{1,0:T(8,128)(2,1)S(1)}, bf16[32,896]{1,0:T(8,128)(2,1)S(1)}, u32[]{:S(2)}, u32[]{:S(2)}) %collective-permute-start.15) | collective-permute-done | bytes 57376 | tf_op jit(solution)/shard_map/ppermute | solution.py:21
  105.4 3.6 %fusion.4 = (bf16[2,896,256]{2,1,0:T(8,128)(2,1)S(1)}, bf16[2,896,256]{2,1,0:T(8,128)(2,1)}, bf16[2,896,256]{2,1,0:T(8,128)(2,1)}, bf16[2,896,256]{2,1,0:T(8,128)(2,1)}) fusion(f32[2,896]{1,0:T(2,128)S(1)} %get-tuple-element.73, bf16[2,2,896,256]{3,2,1,0:T(8,128)(2,1)} %bitcast.195, s32[]{:T(128)S(6)} %select_n.140, f32[2,896]{1,0:T(2,128)S(1)} %get-tuple-element.74, ...), kind=kLoop, calls=%fused_computation.8 | loop fusion | flops 5505024 | bytes 7354376 | tf_op jit(solution)/shard_map/convert_element_type | solution.py:148
  109.0 3.0 %collective-permute-done.16 = bf16[32,1792]{1,0:T(8,128)(2,1)S(1)} collective-permute-done((bf16[32,1792]{1,0:T(8,128)(2,1)S(1)}, bf16[32,1792]{1,0:T(8,128)(2,1)S(1)}, u32[]{:S(2)}, u32[]{:S(2)}) %collective-permute-start.16) | collective-permute-done | bytes 114720 | tf_op jit(solution)/shard_map/ppermute | solution.py:21
  112.0 1.3 all-to-all-done.3
  113.5 0.7 collective-permute-start.9
  114.2 1.2 fusion.51
  115.4 1.2 convolution_add_fusion.10
  117.4 6.1 %collective-permute-done.9 = bf16[2,128,896]{2,1,0:T(8,128)(2,1)S(1)} collective-permute-done((bf16[2,128,896]{2,1,0:T(8,128)(2,1)S(1)}, bf16[2,128,896]{2,1,0:T(8,128)(2,1)S(1)}, u32[]{:S(2)}, u32[]{:S(2)}) %collective-permute-start.9) | collective-permute-done | bytes 458784 | tf_op jit(solution)/shard_map/ppermute | solution.py:21
  128.4 1.3 fusion.27
  129.7 1.3 convolution_add_fusion.2
  131.1 2.2 %collective-permute-done.14 = bf16[256,256]{1,0:T(8,128)(2,1)S(1)} collective-permute-done((bf16[256,256]{1,0:T(8,128)(2,1)S(1)}, bf16[256,256]{1,0:T(8,128)(2,1)S(1)}, u32[]{:S(2)}, u32[]{:S(2)}) %collective-permute-start.14) | collective-permute-done | bytes 131104 | tf_op jit(solution)/shard_map/ppermute | solution.py:21
  133.8 1.3 fusion.113
  135.1 1.3 add_convert_fusion
  136.5 0.9 reshape.165
  137.3 7.7 %all-to-all-start.4 = ((bf16[64,4,896]{2,1,0:T(4,128)(2,1)}), bf16[64,4,896]{2,1,0:T(4,128)(2,1)S(1)}, u32[]{:S(2)}, u32[]{:S(2)}) async-start(bf16[64,4,896]{2,1,0:T(4,128)(2,1)} %reshape.165), calls=%async_computation.4 | async-start | bytes 917504 | tf_op jit(solution)/shard_map/all_to_all | solution.py:25
  145.1 0.7 broadcast_select_fusion
  145.8 18.1 %all-to-all-done.4 = bf16[64,4,896]{2,1,0:T(4,128)(2,1)S(1)} async-done(((bf16[64,4,896]{2,1,0:T(4,128)(2,1)}), bf16[64,4,896]{2,1,0:T(4,128)(2,1)S(1)}, u32[]{:S(2)}, u32[]{:S(2)}) %all-to-all-start.4) | async-done | bytes 458784 | tf_op jit(solution)/shard_map/all_to_all | solution.py:25
  163.9 0.9 fusion.25
  (98 shorter events, 11.5 us)
Async XLA Ops:
  0.6 10.9 %copy-start = (bf16[32,32,576]{2,1,0:T(8,128)(2,1)S(1)}, bf16[32,32,576]{2,1,0:T(8,128)(2,1)}, u32[]{:S(2)}) copy-start(bf16[32,32,576]{2,1,0:T(8,128)(2,1)} %param.12) | copy-start | bytes 3538948
  0.6 10.8 %copy-start.8 = (s32[32]{0:T(128)S(1)}, s32[32]{0:T(128)}, u32[]{:S(2)}) copy-start(s32[32]{0:T(128)} %param.14) | copy-start | bytes 388
  2.8 23.2 %all-to-all-start = ((bf16[8,56,512]{2,1,0:T(8,128)(2,1)}), bf16[8,56,512]{2,1,0:T(8,128)(2,1)S(1)}, u32[]{:S(2)}, u32[]{:S(2)}) async-start(bf16[8,56,512]{2,1,0:T(8,128)(2,1)} %copy.70), calls=%async_computation | async-start | bytes 917504 | tf_op jit(solution)/shard_map/all_to_all | solution.py:25
  22.4 15.5 %copy-start.4 = (f32[3584]{0:T(1024)S(1)}, f32[3584]{0:T(1024)}, u32[]{:S(2)}) copy-start(f32[3584]{0:T(1024)} %param.17) | copy-start | bytes 43012
  22.4 15.5 %copy-start.6 = (s32[32,8]{0,1:T(8,128)S(1)}, s32[32,8]{0,1:T(8,128)}, u32[]{:S(2)}) copy-start(s32[32,8]{0,1:T(8,128)} %param.18) | copy-start | bytes 3076
  22.4 15.6 %copy-start.5 = (f32[32,8]{0,1:T(8,128)S(1)}, f32[32,8]{0,1:T(8,128)}, u32[]{:S(2)}) copy-start(f32[32,8]{0,1:T(8,128)} %param.19) | copy-start | bytes 3076
  26.1 7.2 %collective-permute-start.1 = (bf16[4,56,512]{2,1,0:T(8,128)(2,1)S(1)}, bf16[4,56,512]{2,1,0:T(8,128)(2,1)S(1)}, u32[]{:S(2)}, u32[]{:S(2)}) collective-permute-start(bf16[4,56,512]{2,1,0:T(8,128)(2,1)S(1)} %get-tuple-element.62), channel_id=1, source_target_pairs={{0,2},{2,0},{1,3},{3,1},{4,6},{6,4},{5,7},{7,5},{8,10},{10,8},{9,1... | collective-permute-start | bytes 688136 | tf_op jit(solution)/shard_map/ppermute | solution.py:21
  28.5 15.3 %all-to-all-start.1 = ((bf16[8,32,512]{2,1,0:T(8,128)(2,1)}), bf16[8,32,512]{2,1,0:T(8,128)(2,1)S(1)}, u32[]{:S(2)}, u32[]{:S(2)}) async-start(bf16[8,32,512]{2,1,0:T(8,128)(2,1)} %copy.74), calls=%async_computation.1 | async-start | bytes 524288 | tf_op jit(solution)/shard_map/all_to_all | solution.py:25
  33.3 13.5 %collective-permute-start.2 = (bf16[8,56,512]{2,1,0:T(8,128)(2,1)S(1)}, bf16[8,56,512]{2,1,0:T(8,128)(2,1)S(1)}, u32[]{:S(2)}, u32[]{:S(2)}) collective-permute-start(bf16[8,56,512]{2,1,0:T(8,128)(2,1)S(1)} %pad_maximum_fusion.2), channel_id=1, source_target_pairs={{0,4},{4,0},{8,12},{12,8},{1,5},{5,1},{9,13},{13,9},{2,6},{6,2},{1... | collective-permute-start | bytes 1376264 | tf_op jit(solution)/shard_map/ppermute | solution.py:21
  35.0 21.0 %collective-permute-start.4 = (bf16[8,56,512]{2,1,0:T(8,128)(2,1)S(1)}, bf16[8,56,512]{2,1,0:T(8,128)(2,1)S(1)}, u32[]{:S(2)}, u32[]{:S(2)}) collective-permute-start(bf16[8,56,512]{2,1,0:T(8,128)(2,1)S(1)} %pad_maximum_fusion.2), channel_id=1, source_target_pairs={{0,12},{4,8},{8,4},{12,0},{1,13},{5,9},{9,5},{13,1},{2,14},{6,10},... | collective-permute-start | bytes 1376264 | tf_op jit(solution)/shard_map/ppermute | solution.py:21
  37.2 20.4 %collective-permute-start.3 = (bf16[8,56,512]{2,1,0:T(8,128)(2,1)S(1)}, bf16[8,56,512]{2,1,0:T(8,128)(2,1)S(1)}, u32[]{:S(2)}, u32[]{:S(2)}) collective-permute-start(bf16[8,56,512]{2,1,0:T(8,128)(2,1)S(1)} %pad_maximum_fusion.2), channel_id=1, source_target_pairs={{0,8},{4,12},{8,0},{12,4},{1,9},{5,13},{9,1},{13,5},{2,10},{6,14},... | collective-permute-start | bytes 1376264 | tf_op jit(solution)/shard_map/ppermute | solution.py:21
  43.8 14.5 %collective-permute-start.6 = (bf16[256,512]{1,0:T(8,128)(2,1)S(1)}, bf16[256,512]{1,0:T(8,128)(2,1)S(1)}, u32[]{:S(2)}, u32[]{:S(2)}) collective-permute-start(bf16[256,512]{1,0:T(8,128)(2,1)S(1)} %bitcast.188), channel_id=1, source_target_pairs={{0,130},{2,128},{128,2},{130,0},{1,131},{3,129},{129,3},{131,1},{4... | collective-permute-start | bytes 786440 | tf_op jit(solution)/shard_map/ppermute | solution.py:21
  45.9 12.9 %collective-permute-start = (bf16[256,512]{1,0:T(8,128)(2,1)S(1)}, bf16[256,512]{1,0:T(8,128)(2,1)S(1)}, u32[]{:S(2)}, u32[]{:S(2)}) collective-permute-start(bf16[256,512]{1,0:T(8,128)(2,1)S(1)} %bitcast.189), channel_id=1, source_target_pairs={{0,128},{128,0},{1,129},{129,1},{2,130},{130,2},{3,131},{131,3},{4... | collective-permute-start | bytes 786440 | tf_op jit(solution)/shard_map/ppermute | solution.py:21
  46.9 11.5 %collective-permute-start.5 = (bf16[256,512]{1,0:T(8,128)(2,1)S(1)}, bf16[256,512]{1,0:T(8,128)(2,1)S(1)}, u32[]{:S(2)}, u32[]{:S(2)}) collective-permute-start(bf16[256,512]{1,0:T(8,128)(2,1)S(1)} %bitcast.190), channel_id=1, source_target_pairs={{0,2},{2,0},{1,3},{3,1},{4,6},{6,4},{5,7},{7,5},{8,10},{10,8},{9,1... | collective-permute-start | bytes 786440 | tf_op jit(solution)/shard_map/ppermute | solution.py:21
  59.3 1.9 %collective-permute-start.7 = (bf16[256,896]{1,0:T(8,128)(2,1)S(1)}, bf16[256,896]{1,0:T(8,128)(2,1)S(1)}, u32[]{:S(2)}, u32[]{:S(2)}) collective-permute-start(bf16[256,896]{1,0:T(8,128)(2,1)S(1)} %fusion.13), channel_id=1, source_target_pairs={{0,1},{1,0},{2,3},{3,2},{4,5},{5,4},{6,7},{7,6},{8,9},{9,8},{10,11... | collective-permute-start | bytes 1376264 | tf_op jit(solution)/shard_map/ppermute | solution.py:21
  62.5 16.0 %copy-start.7 = (s32[256]{0:T(256)S(1)}, s32[256]{0:T(256)}, u32[]{:S(2)}) copy-start(s32[256]{0:T(256)} %param.20) | copy-start | bytes 3076
  62.5 22.3 %all-to-all-start.2 = ((bf16[8,32,896]{2,1,0:T(8,128)(2,1)}), bf16[8,32,896]{2,1,0:T(8,128)(2,1)S(1)}, u32[]{:S(2)}, u32[]{:S(2)}) async-start(bf16[8,32,896]{2,1,0:T(8,128)(2,1)} %bitcast.15), calls=%async_computation.2 | async-start | bytes 917504 | tf_op jit(solution)/shard_map/all_to_all | solution.py:25
  69.8 8.5 %collective-permute-start.8 = (s32[32,8]{0,1:T(8,128)S(1)}, s32[32,8]{0,1:T(8,128)S(1)}, u32[]{:S(2)}, u32[]{:S(2)}) collective-permute-start(s32[32,8]{0,1:T(8,128)S(1)} %copy-done.6), channel_id=1, source_target_pairs={{0,0},{1,128},{128,1},{129,129},{2,2},{3,130},{130,3},{131,131},{4... | collective-permute-start | bytes 3080 | tf_op jit(solution)/shard_map/ppermute | solution.py:127
  72.9 56.8 %collective-permute-start.13 = (bf16[256,896]{1,0:T(8,128)(2,1)}, bf16[256,896]{1,0:T(8,128)(2,1)}, u32[]{:S(2)}, u32[]{:S(2)}) collective-permute-start(bf16[256,896]{1,0:T(8,128)(2,1)} %get-tuple-element.50), channel_id=1, source_target_pairs={{0,1},{1,0},{2,3},{3,2},{4,5},{5,4},{6,7},{7,6},{8,9},{9,8},{10,11... | collective-permute-start | bytes 1376264 | tf_op jit(solution)/shard_map/ppermute | solution.py:21
  77.0 56.8 %collective-permute-start.18 = (bf16[256,896]{1,0:T(8,128)(2,1)}, bf16[256,896]{1,0:T(8,128)(2,1)}, u32[]{:S(2)}, u32[]{:S(2)}) collective-permute-start(bf16[256,896]{1,0:T(8,128)(2,1)} %get-tuple-element.48), channel_id=1, source_target_pairs={{0,2},{1,3},{2,0},{3,1},{4,6},{5,7},{6,4},{7,5},{8,10},{9,11},{10,... | collective-permute-start | bytes 1376264 | tf_op jit(solution)/shard_map/ppermute | solution.py:21
  77.2 57.9 %collective-permute-start.20 = (bf16[256,896]{1,0:T(8,128)(2,1)}, bf16[256,896]{1,0:T(8,128)(2,1)}, u32[]{:S(2)}, u32[]{:S(2)}) collective-permute-start(bf16[256,896]{1,0:T(8,128)(2,1)} %get-tuple-element.49), channel_id=1, source_target_pairs={{0,3},{1,2},{2,1},{3,0},{4,7},{5,6},{6,5},{7,4},{8,11},{9,10},{10,... | collective-permute-start | bytes 1376264 | tf_op jit(solution)/shard_map/ppermute | solution.py:21
  84.8 20.5 %collective-permute-start.15 = (bf16[32,896]{1,0:T(8,128)(2,1)S(1)}, bf16[32,896]{1,0:T(8,128)(2,1)S(1)}, u32[]{:S(2)}, u32[]{:S(2)}) collective-permute-start(bf16[32,896]{1,0:T(8,128)(2,1)S(1)} %reduce_sum.122), channel_id=1, source_target_pairs={{0,2},{2,0},{1,3},{3,1},{4,6},{6,4},{5,7},{7,5},{8,10},{10,8},{9,1... | collective-permute-start | bytes 172040 | tf_op jit(solution)/shard_map/ppermute | solution.py:21
  86.9 26.4 %all-to-all-start.3 = ((bf16[64,4,896]{2,1,0:T(4,128)(2,1)}), bf16[64,4,896]{2,1,0:T(4,128)(2,1)S(1)}, u32[]{:S(2)}, u32[]{:S(2)}) async-start(bf16[64,4,896]{2,1,0:T(4,128)(2,1)} %copy.78), calls=%async_computation.3 | async-start | bytes 917504 | tf_op jit(solution)/shard_map/all_to_all | solution.py:25
  105.3 6.6 %collective-permute-start.16 = (bf16[32,1792]{1,0:T(8,128)(2,1)S(1)}, bf16[32,1792]{1,0:T(8,128)(2,1)S(1)}, u32[]{:S(2)}, u32[]{:S(2)}) collective-permute-start(bf16[32,1792]{1,0:T(8,128)(2,1)S(1)} %pad_maximum_fusion.5), channel_id=1, source_target_pairs={{0,128},{128,0},{1,129},{129,1},{2,130},{130,2},{3,131},{131,3},{4... | collective-permute-start | bytes 344072 | tf_op jit(solution)/shard_map/ppermute | solution.py:21
  113.5 3.2 %copy-start.2 = (bf16[2,896,256]{2,1,0:T(8,128)(2,1)S(1)}, bf16[2,896,256]{2,1,0:T(8,128)(2,1)}, u32[]{:S(2)}) copy-start(bf16[2,896,256]{2,1,0:T(8,128)(2,1)} %get-tuple-element.32) | copy-start | bytes 2752516
  113.5 10.0 %collective-permute-start.9 = (bf16[2,128,896]{2,1,0:T(8,128)(2,1)S(1)}, bf16[2,128,896]{2,1,0:T(8,128)(2,1)S(1)}, u32[]{:S(2)}, u32[]{:S(2)}) collective-permute-start(bf16[2,128,896]{2,1,0:T(8,128)(2,1)S(1)} %reshape.164), channel_id=1, source_target_pairs={{0,2},{2,0},{1,3},{3,1},{4,6},{6,4},{5,7},{7,5},{8,10},{10,8},{9,1... | collective-permute-start | bytes 1376264 | tf_op jit(solution)/shard_map/ppermute | solution.py:21
  114.2 9.5 %collective-permute-start.10 = (bf16[2,128,896]{2,1,0:T(8,128)(2,1)S(1)}, bf16[2,128,896]{2,1,0:T(8,128)(2,1)S(1)}, u32[]{:S(2)}, u32[]{:S(2)}) collective-permute-start(bf16[2,128,896]{2,1,0:T(8,128)(2,1)S(1)} %reshape.164), channel_id=1, source_target_pairs={{0,1},{1,0},{2,3},{3,2},{4,5},{5,4},{6,7},{7,6},{8,9},{9,8},{10,11... | collective-permute-start | bytes 1376264 | tf_op jit(solution)/shard_map/ppermute | solution.py:21
  116.9 7.1 %copy-start.1 = (bf16[2,896,256]{2,1,0:T(8,128)(2,1)S(1)}, bf16[2,896,256]{2,1,0:T(8,128)(2,1)}, u32[]{:S(2)}) copy-start(bf16[2,896,256]{2,1,0:T(8,128)(2,1)} %get-tuple-element.30) | copy-start | bytes 2752516
  123.5 2.5 %collective-permute-start.11 = (bf16[2,128,896]{2,1,0:T(8,128)(2,1)S(1)}, bf16[2,128,896]{2,1,0:T(8,128)(2,1)S(1)}, u32[]{:S(2)}, u32[]{:S(2)}) collective-permute-start(bf16[2,128,896]{2,1,0:T(8,128)(2,1)S(1)} %collective-permute-done.9), channel_id=1, source_target_pairs={{0,1},{1,0},{2,3},{3,2},{4,5},{5,4},{6,7},{7,6},{8,9},{9,8},{10,11... | collective-permute-start | bytes 1376264 | tf_op jit(solution)/shard_map/ppermute | solution.py:21
  124.3 1.2 copy-start.3
  127.2 2.5 %collective-permute-start.12 = (bf16[256,256]{1,0:T(8,128)(2,1)S(1)}, bf16[256,256]{1,0:T(8,128)(2,1)S(1)}, u32[]{:S(2)}, u32[]{:S(2)}) collective-permute-start(bf16[256,256]{1,0:T(8,128)(2,1)S(1)} %pad_maximum_fusion.4), channel_id=1, source_target_pairs={{0,1},{1,0},{2,3},{3,2},{4,5},{5,4},{6,7},{7,6},{8,9},{9,8},{10,11... | collective-permute-start | bytes 393224 | tf_op jit(solution)/shard_map/ppermute | solution.py:21
  127.8 5.5 %collective-permute-start.14 = (bf16[256,256]{1,0:T(8,128)(2,1)S(1)}, bf16[256,256]{1,0:T(8,128)(2,1)S(1)}, u32[]{:S(2)}, u32[]{:S(2)}) collective-permute-start(bf16[256,256]{1,0:T(8,128)(2,1)S(1)} %pad_maximum_fusion.4), channel_id=1, source_target_pairs={{0,2},{2,0},{1,3},{3,1},{4,6},{6,4},{5,7},{7,5},{8,10},{10,8},{9,1... | collective-permute-start | bytes 393224 | tf_op jit(solution)/shard_map/ppermute | solution.py:21
  133.3 11.8 %collective-permute-start.17 = (bf16[32,3584]{1,0:T(8,128)(2,1)S(1)}, bf16[32,3584]{1,0:T(8,128)(2,1)S(1)}, u32[]{:S(2)}, u32[]{:S(2)}) collective-permute-start(bf16[32,3584]{1,0:T(8,128)(2,1)S(1)} %pad_maximum_fusion.3), channel_id=1, source_target_pairs={{0,1},{1,0},{2,3},{3,2},{4,5},{5,4},{6,7},{7,6},{8,9},{9,8},{10,11... | collective-permute-start | bytes 688136 | tf_op jit(solution)/shard_map/ppermute | solution.py:21
  133.3 1.8 %collective-permute-start.19 = (bf16[256,256]{1,0:T(8,128)(2,1)S(1)}, bf16[256,256]{1,0:T(8,128)(2,1)S(1)}, u32[]{:S(2)}, u32[]{:S(2)}) collective-permute-start(bf16[256,256]{1,0:T(8,128)(2,1)S(1)} %collective-permute-done.14), channel_id=1, source_target_pairs={{0,1},{1,0},{2,3},{3,2},{4,5},{5,4},{6,7},{7,6},{8,9},{9,8},{10,11... | collective-permute-start | bytes 393224 | tf_op jit(solution)/shard_map/ppermute | solution.py:21
  137.3 26.5 %all-to-all-start.4 = ((bf16[64,4,896]{2,1,0:T(4,128)(2,1)}), bf16[64,4,896]{2,1,0:T(4,128)(2,1)S(1)}, u32[]{:S(2)}, u32[]{:S(2)}) async-start(bf16[64,4,896]{2,1,0:T(4,128)(2,1)} %reshape.165), calls=%async_computation.4 | async-start | bytes 917504 | tf_op jit(solution)/shard_map/all_to_all | solution.py:25

commit v5 on v4

--- a/solution.py
+++ b/solution.py
@@ -134,9 +134,11 @@
     part_rows = jnp.sum(partial.astype(f32), axis=0).astype(bf16)
 
     _, slots_sent = placing(routes_sent, expert_home, owners)
-    outgoing = jnp.einsum(
-        "roc,rd->ocd", slots_sent.astype(bf16), part_rows, preferred_element_type=f32
+    slots_sent = slots_sent.astype(bf16).reshape(rows_here, owners * MOST)
+    outgoing = lax.dot_general(
+        slots_sent, part_rows, (((0,), (0,)), ((), ())), preferred_element_type=f32
     ).astype(bf16)
+    outgoing = outgoing.reshape(owners, MOST, quarter)
     outgoing, w_gate, w_up = lax.optimization_barrier((outgoing, w_gate, w_up))
     incoming = exchange(outgoing, DP).reshape(2, -1, quarter)
 

time: 166 us -> 166 us (level)
  no operation moved by 1% of the time
where the time goes in v5:
time: 166 us; the launch traced here: 165 us
  waiting for transfers between devices  65.9 us (40%)
  starting transfers between devices  55.9 us (34%)
  matrix products  25.4 us (15%)
  local copies, waits for them, and re-layouts  8.59 us (5%)
  other arithmetic  7.83 us (5%)
    all_to_all x5, starting transfers between devices, exchange(): return lax.all_to_all(value, axis, split_axis=0, concat_axis=0, tiled=True)  36.7 us
    ppermute x20, waiting for transfers between devices, flip(): return lax.ppermute(value, axis, [(i, i ^ mask) for i in range(count)])  33.2 us
    all_to_all x5, waiting for transfers between devices, exchange(): return lax.all_to_all(value, axis, split_axis=0, concat_axis=0, tiled=True)  32.8 us
    ppermute x20, starting transfers between devices, flip(): return lax.ppermute(value, axis, [(i, i ^ mask) for i in range(count)])  18.6 us
    dot_general x1, matrix products, attention(): jnp.einsum('rhj,rjc->rhc', weights, latent_cache[:, :, :LATENT], preferre...  4.02 us
    dot_general x8, matrix products, from_half(): gate_out += jnp.dot(pieces[i], weights[0][i], preferred_element_type=f32)  3.91 us
    convert_element_type x1, other arithmetic, folded(): return (weight.astype(f32) * gains).astype(bf16)  3.55 us
  transfers between devices with their start and end apart: 26, of which 13 were waited for; matrix products, arithmetic and copies ran while one was open for 22% of the time, Pallas kernels for 0%

profile of v5, /device:TPU:32, one launch (start us, length us, event | category | flops | bytes accessed | tf_op | source)
XLA Modules:
  0.0 164.9 jit_solution(9761232495966029357)
XLA Ops:
  0.7 1.3 copy.93
  1.9 0.9 copy.74
  2.8 8.6 %all-to-all-start = ((bf16[8,56,512]{2,1,0:T(8,128)(2,1)}), bf16[8,56,512]{2,1,0:T(8,128)(2,1)S(1)}, u32[]{:S(2)}, u32[]{:S(2)}) async-start(bf16[8,56,512]{2,1,0:T(8,128)(2,1)} %copy.74), calls=%async_computation | async-start | bytes 917504 | tf_op jit(solution)/shard_map/all_to_all | solution.py:25
  11.5 3.2 %fusion.15 = f32[32,32,128]{2,1,0:T(8,128)S(1)} fusion(bf16[32,32,576]{2,1,0:T(8,128)(2,1)S(1)} %copy-done, bf16[32,128,576]{1,2,0:T(8,128)(2,1)} %param.13, pred[32,128]{1,0:T(8,128)(4,1)S(1)} %iota_compare_fusion.5), kind=kOutput, calls=%fused_computation.24 | convolution fusion | flops 151257088 | bytes 6426624 | tf_op jit(solution)/shard_map/rhc,rjc->rhj/dot_general | solution.py:38
  15.1 4.0 %fusion.7 = bf16[32,32,512]{2,1,0:T(8,128)(2,1)S(1)} fusion(bf16[32,128,576]{1,2,0:T(8,128)(2,1)} %param.13, f32[32,32]{1,0:T(8,128)S(1)} %fusion.110, f32[32,32,128]{2,1,0:T(8,128)S(1)} %fusion.15), kind=kOutput, calls=%fused_computation.13 | convolution fusion | flops 135136384 | bytes 6307840 | tf_op jit(solution)/shard_map/rhj,rjc->rhc/dot_general | solution.py:48
  19.1 3.3 %fusion.16 = bf16[32,4,8,128]{3,2,1,0:T(8,128)(2,1)S(1)} fusion(bf16[32,512,128]{2,1,0:T(8,128)(2,1)} %param.15, bf16[32,32,512]{2,1,0:T(8,128)(2,1)S(1)} %fusion.7), kind=kOutput, calls=%fused_computation.26 | convolution fusion | flops 134348800 | bytes 5505024 | tf_op jit(solution)/shard_map/rhc,hcv->rhv/dot_general | solution.py:51
  22.4 3.6 %all-to-all-done = bf16[8,56,512]{2,1,0:T(8,128)(2,1)S(1)} async-done(((bf16[8,56,512]{2,1,0:T(8,128)(2,1)}), bf16[8,56,512]{2,1,0:T(8,128)(2,1)S(1)}, u32[]{:S(2)}, u32[]{:S(2)}) %all-to-all-start) | async-done | bytes 458784 | tf_op jit(solution)/shard_map/all_to_all | solution.py:25
  26.1 1.6 collective-permute-start.1
  27.7 0.8 copy.78
  28.5 4.8 %all-to-all-start.1 = ((bf16[8,32,512]{2,1,0:T(8,128)(2,1)}), bf16[8,32,512]{2,1,0:T(8,128)(2,1)S(1)}, u32[]{:S(2)}, u32[]{:S(2)}) async-start(bf16[8,32,512]{2,1,0:T(8,128)(2,1)} %copy.78), calls=%async_computation.1 | async-start | bytes 524288 | tf_op jit(solution)/shard_map/all_to_all | solution.py:25
  33.3 1.7 %collective-permute-start.2 = (bf16[8,56,512]{2,1,0:T(8,128)(2,1)S(1)}, bf16[8,56,512]{2,1,0:T(8,128)(2,1)S(1)}, u32[]{:S(2)}, u32[]{:S(2)}) collective-permute-start(bf16[8,56,512]{2,1,0:T(8,128)(2,1)S(1)} %pad_maximum_fusion.2), channel_id=1, source_target_pairs={{0,4},{4,0},{8,12},{12,8},{1,5},{5,1},{9,13},{13,9},{2,6},{6,2},{1... | collective-permute-start | bytes 1376264 | tf_op jit(solution)/shard_map/ppermute | solution.py:21
  35.0 2.2 %collective-permute-start.4 = (bf16[8,56,512]{2,1,0:T(8,128)(2,1)S(1)}, bf16[8,56,512]{2,1,0:T(8,128)(2,1)S(1)}, u32[]{:S(2)}, u32[]{:S(2)}) collective-permute-start(bf16[8,56,512]{2,1,0:T(8,128)(2,1)S(1)} %pad_maximum_fusion.2), channel_id=1, source_target_pairs={{0,12},{4,8},{8,4},{12,0},{1,13},{5,9},{9,5},{13,1},{2,14},{6,10},... | collective-permute-start | bytes 1376264 | tf_op jit(solution)/shard_map/ppermute | solution.py:21
  37.2 0.7 collective-permute-start.3
  38.2 5.6 %all-to-all-done.1 = bf16[8,32,512]{2,1,0:T(8,128)(2,1)S(1)} async-done(((bf16[8,32,512]{2,1,0:T(8,128)(2,1)}), bf16[8,32,512]{2,1,0:T(8,128)(2,1)S(1)}, u32[]{:S(2)}, u32[]{:S(2)}) %all-to-all-start.1) | async-done | bytes 262176 | tf_op jit(solution)/shard_map/all_to_all | solution.py:25
  43.8 2.1 %collective-permute-start.6 = (bf16[256,512]{1,0:T(8,128)(2,1)S(1)}, bf16[256,512]{1,0:T(8,128)(2,1)S(1)}, u32[]{:S(2)}, u32[]{:S(2)}) collective-permute-start(bf16[256,512]{1,0:T(8,128)(2,1)S(1)} %bitcast.188), channel_id=1, source_target_pairs={{0,130},{2,128},{128,2},{130,0},{1,131},{3,129},{129,3},{131,1},{4... | collective-permute-start | bytes 786440 | tf_op jit(solution)/shard_map/ppermute | solution.py:21
  45.9 0.6 collective-permute-start
  46.9 1.0 collective-permute-start.5
  47.9 8.1 %collective-permute-done.4 = bf16[8,56,512]{2,1,0:T(8,128)(2,1)S(1)} collective-permute-done((bf16[8,56,512]{2,1,0:T(8,128)(2,1)S(1)}, bf16[8,56,512]{2,1,0:T(8,128)(2,1)S(1)}, u32[]{:S(2)}, u32[]{:S(2)}) %collective-permute-start.4) | collective-permute-done | bytes 458784 | tf_op jit(solution)/shard_map/ppermute | solution.py:21
  56.0 1.5 collective-permute-done.3
  59.9 1.3 collective-permute-done.7
  61.2 1.3 fusion.12
  62.5 7.4 %all-to-all-start.2 = ((bf16[8,32,896]{2,1,0:T(8,128)(2,1)}), bf16[8,32,896]{2,1,0:T(8,128)(2,1)S(1)}, u32[]{:S(2)}, u32[]{:S(2)}) async-start(bf16[8,32,896]{2,1,0:T(8,128)(2,1)} %bitcast.15), calls=%async_computation.2 | async-start | bytes 917504 | tf_op jit(solution)/shard_map/all_to_all | solution.py:25
  69.8 0.6 collective-permute-start.8
  70.5 2.4 %dynamic-slice_bitcast_fusion.1 = (bf16[256,896]{1,0:T(8,128)(2,1)}, bf16[256,896]{1,0:T(8,128)(2,1)}, bf16[256,896]{1,0:T(8,128)(2,1)}) fusion(bf16[1,256,3584]{2,1,0:T(8,128)(2,1)} %param.23, s32[]{:T(128)S(6)} %select_n.154, s32[]{:T(128)S(6)} %select_n.155, s32[]{:T(128)S(6)} %select_n.144), kind=kLoop, calls=%fused_computation.77 | loop fusion | bytes 2752524 | tf_op jit(solution)/shard_map/dynamic_slice | solution.py:131
  72.9 4.1 %collective-permute-start.13 = (bf16[256,896]{1,0:T(8,128)(2,1)}, bf16[256,896]{1,0:T(8,128)(2,1)}, u32[]{:S(2)}, u32[]{:S(2)}) collective-permute-start(bf16[256,896]{1,0:T(8,128)(2,1)} %get-tuple-element.50), channel_id=1, source_target_pairs={{0,1},{1,0},{2,3},{3,2},{4,5},{5,4},{6,7},{7,6},{8,9},{9,8},{10,11... | collective-permute-start | bytes 1376264 | tf_op jit(solution)/shard_map/ppermute | solution.py:21
  77.2 1.1 collective-permute-start.20
  78.4 1.2 select_reduce_fusion
  80.4 4.3 %all-to-all-done.2 = bf16[8,32,896]{2,1,0:T(8,128)(2,1)S(1)} async-done(((bf16[8,32,896]{2,1,0:T(8,128)(2,1)}), bf16[8,32,896]{2,1,0:T(8,128)(2,1)S(1)}, u32[]{:S(2)}, u32[]{:S(2)}) %all-to-all-start.2) | async-done | bytes 458784 | tf_op jit(solution)/shard_map/all_to_all | solution.py:25
  85.9 0.9 reshape.168
  86.8 7.9 %all-to-all-start.3 = ((bf16[64,4,896]{2,1,0:T(4,128)(2,1)}), bf16[64,4,896]{2,1,0:T(4,128)(2,1)S(1)}, u32[]{:S(2)}, u32[]{:S(2)}) async-start(bf16[64,4,896]{2,1,0:T(4,128)(2,1)} %reshape.168), calls=%async_computation.3 | async-start | bytes 917504 | tf_op jit(solution)/shard_map/all_to_all | solution.py:25
  94.7 10.6 %collective-permute-done.15 = bf16[32,896]{1,0:T(8,128)(2,1)S(1)} collective-permute-done((bf16[32,896]{1,0:T(8,128)(2,1)S(1)}, bf16[32,896]{1,0:T(8,128)(2,1)S(1)}, u32[]{:S(2)}, u32[]{:S(2)}) %collective-permute-start.15) | collective-permute-done | bytes 57376 | tf_op jit(solution)/shard_map/ppermute | solution.py:21
  105.4 3.6 %fusion.4 = (bf16[2,896,256]{2,1,0:T(8,128)(2,1)S(1)}, bf16[2,896,256]{2,1,0:T(8,128)(2,1)}, bf16[2,896,256]{2,1,0:T(8,128)(2,1)}, bf16[2,896,256]{2,1,0:T(8,128)(2,1)}) fusion(f32[2,896]{1,0:T(2,128)S(1)} %get-tuple-element.73, bf16[2,2,896,256]{3,2,1,0:T(8,128)(2,1)} %bitcast.195, s32[]{:T(128)S(6)} %select_n.140, f32[2,896]{1,0:T(2,128)S(1)} %get-tuple-element.74, ...), kind=kLoop, calls=%fused_computation.8 | loop fusion | flops 5505024 | bytes 7354376 | tf_op jit(solution)/shard_map/convert_element_type | solution.py:150
  109.0 3.0 %collective-permute-done.16 = bf16[32,1792]{1,0:T(8,128)(2,1)S(1)} collective-permute-done((bf16[32,1792]{1,0:T(8,128)(2,1)S(1)}, bf16[32,1792]{1,0:T(8,128)(2,1)S(1)}, u32[]{:S(2)}, u32[]{:S(2)}) %collective-permute-start.16) | collective-permute-done | bytes 114720 | tf_op jit(solution)/shard_map/ppermute | solution.py:21
  112.0 1.2 all-to-all-done.3
  113.3 0.7 collective-permute-start.9
  114.0 1.2 fusion.51
  115.2 1.2 convolution_add_fusion.10
  117.2 6.1 %collective-permute-done.9 = bf16[2,128,896]{2,1,0:T(8,128)(2,1)S(1)} collective-permute-done((bf16[2,128,896]{2,1,0:T(8,128)(2,1)S(1)}, bf16[2,128,896]{2,1,0:T(8,128)(2,1)S(1)}, u32[]{:S(2)}, u32[]{:S(2)}) %collective-permute-start.9) | collective-permute-done | bytes 458784 | tf_op jit(solution)/shard_map/ppermute | solution.py:21
  128.2 1.3 fusion.27
  129.6 1.3 convolution_add_fusion.2
  130.9 2.2 %collective-permute-done.14 = bf16[256,256]{1,0:T(8,128)(2,1)S(1)} collective-permute-done((bf16[256,256]{1,0:T(8,128)(2,1)S(1)}, bf16[256,256]{1,0:T(8,128)(2,1)S(1)}, u32[]{:S(2)}, u32[]{:S(2)}) %collective-permute-start.14) | collective-permute-done | bytes 131104 | tf_op jit(solution)/shard_map/ppermute | solution.py:21
  133.6 1.3 fusion.111
  135.0 1.3 add_convert_fusion
  136.3 0.9 reshape.173
  137.2 8.0 %all-to-all-start.4 = ((bf16[64,4,896]{2,1,0:T(4,128)(2,1)}), bf16[64,4,896]{2,1,0:T(4,128)(2,1)S(1)}, u32[]{:S(2)}, u32[]{:S(2)}) async-start(bf16[64,4,896]{2,1,0:T(4,128)(2,1)} %reshape.173), calls=%async_computation.4 | async-start | bytes 917504 | tf_op jit(solution)/shard_map/all_to_all | solution.py:25
  145.2 0.7 broadcast_select_fusion
  145.9 18.1 %all-to-all-done.4 = bf16[64,4,896]{2,1,0:T(4,128)(2,1)S(1)} async-done(((bf16[64,4,896]{2,1,0:T(4,128)(2,1)}), bf16[64,4,896]{2,1,0:T(4,128)(2,1)S(1)}, u32[]{:S(2)}, u32[]{:S(2)}) %all-to-all-start.4) | async-done | bytes 458784 | tf_op jit(solution)/shard_map/all_to_all | solution.py:25
  164.0 0.9 fusion.25
  (104 shorter events, 11.9 us)
Async XLA Ops:
  0.6 10.9 %copy-start = (bf16[32,32,576]{2,1,0:T(8,128)(2,1)S(1)}, bf16[32,32,576]{2,1,0:T(8,128)(2,1)}, u32[]{:S(2)}) copy-start(bf16[32,32,576]{2,1,0:T(8,128)(2,1)} %param.12) | copy-start | bytes 3538948
  0.6 10.8 %copy-start.8 = (s32[32]{0:T(128)S(1)}, s32[32]{0:T(128)}, u32[]{:S(2)}) copy-start(s32[32]{0:T(128)} %param.14) | copy-start | bytes 388
  2.8 23.2 %all-to-all-start = ((bf16[8,56,512]{2,1,0:T(8,128)(2,1)}), bf16[8,56,512]{2,1,0:T(8,128)(2,1)S(1)}, u32[]{:S(2)}, u32[]{:S(2)}) async-start(bf16[8,56,512]{2,1,0:T(8,128)(2,1)} %copy.74), calls=%async_computation | async-start | bytes 917504 | tf_op jit(solution)/shard_map/all_to_all | solution.py:25
  22.4 15.5 %copy-start.4 = (f32[3584]{0:T(1024)S(1)}, f32[3584]{0:T(1024)}, u32[]{:S(2)}) copy-start(f32[3584]{0:T(1024)} %param.17) | copy-start | bytes 43012
  22.4 15.5 %copy-start.6 = (s32[32,8]{0,1:T(8,128)S(1)}, s32[32,8]{0,1:T(8,128)}, u32[]{:S(2)}) copy-start(s32[32,8]{0,1:T(8,128)} %param.18) | copy-start | bytes 3076
  22.4 15.7 %copy-start.5 = (f32[32,8]{0,1:T(8,128)S(1)}, f32[32,8]{0,1:T(8,128)}, u32[]{:S(2)}) copy-start(f32[32,8]{0,1:T(8,128)} %param.19) | copy-start | bytes 3076
  26.1 7.2 %collective-permute-start.1 = (bf16[4,56,512]{2,1,0:T(8,128)(2,1)S(1)}, bf16[4,56,512]{2,1,0:T(8,128)(2,1)S(1)}, u32[]{:S(2)}, u32[]{:S(2)}) collective-permute-start(bf16[4,56,512]{2,1,0:T(8,128)(2,1)S(1)} %get-tuple-element.62), channel_id=1, source_target_pairs={{0,2},{2,0},{1,3},{3,1},{4,6},{6,4},{5,7},{7,5},{8,10},{10,8},{9,1... | collective-permute-start | bytes 688136 | tf_op jit(solution)/shard_map/ppermute | solution.py:21
  28.5 15.3 %all-to-all-start.1 = ((bf16[8,32,512]{2,1,0:T(8,128)(2,1)}), bf16[8,32,512]{2,1,0:T(8,128)(2,1)S(1)}, u32[]{:S(2)}, u32[]{:S(2)}) async-start(bf16[8,32,512]{2,1,0:T(8,128)(2,1)} %copy.78), calls=%async_computation.1 | async-start | bytes 524288 | tf_op jit(solution)/shard_map/all_to_all | solution.py:25
  33.3 13.5 %collective-permute-start.2 = (bf16[8,56,512]{2,1,0:T(8,128)(2,1)S(1)}, bf16[8,56,512]{2,1,0:T(8,128)(2,1)S(1)}, u32[]{:S(2)}, u32[]{:S(2)}) collective-permute-start(bf16[8,56,512]{2,1,0:T(8,128)(2,1)S(1)} %pad_maximum_fusion.2), channel_id=1, source_target_pairs={{0,4},{4,0},{8,12},{12,8},{1,5},{5,1},{9,13},{13,9},{2,6},{6,2},{1... | collective-permute-start | bytes 1376264 | tf_op jit(solution)/shard_map/ppermute | solution.py:21
  35.0 21.0 %collective-permute-start.4 = (bf16[8,56,512]{2,1,0:T(8,128)(2,1)S(1)}, bf16[8,56,512]{2,1,0:T(8,128)(2,1)S(1)}, u32[]{:S(2)}, u32[]{:S(2)}) collective-permute-start(bf16[8,56,512]{2,1,0:T(8,128)(2,1)S(1)} %pad_maximum_fusion.2), channel_id=1, source_target_pairs={{0,12},{4,8},{8,4},{12,0},{1,13},{5,9},{9,5},{13,1},{2,14},{6,10},... | collective-permute-start | bytes 1376264 | tf_op jit(solution)/shard_map/ppermute | solution.py:21
  37.2 20.4 %collective-permute-start.3 = (bf16[8,56,512]{2,1,0:T(8,128)(2,1)S(1)}, bf16[8,56,512]{2,1,0:T(8,128)(2,1)S(1)}, u32[]{:S(2)}, u32[]{:S(2)}) collective-permute-start(bf16[8,56,512]{2,1,0:T(8,128)(2,1)S(1)} %pad_maximum_fusion.2), channel_id=1, source_target_pairs={{0,8},{4,12},{8,0},{12,4},{1,9},{5,13},{9,1},{13,5},{2,10},{6,14},... | collective-permute-start | bytes 1376264 | tf_op jit(solution)/shard_map/ppermute | solution.py:21
  43.8 14.5 %collective-permute-start.6 = (bf16[256,512]{1,0:T(8,128)(2,1)S(1)}, bf16[256,512]{1,0:T(8,128)(2,1)S(1)}, u32[]{:S(2)}, u32[]{:S(2)}) collective-permute-start(bf16[256,512]{1,0:T(8,128)(2,1)S(1)} %bitcast.188), channel_id=1, source_target_pairs={{0,130},{2,128},{128,2},{130,0},{1,131},{3,129},{129,3},{131,1},{4... | collective-permute-start | bytes 786440 | tf_op jit(solution)/shard_map/ppermute | solution.py:21
  45.9 12.9 %collective-permute-start = (bf16[256,512]{1,0:T(8,128)(2,1)S(1)}, bf16[256,512]{1,0:T(8,128)(2,1)S(1)}, u32[]{:S(2)}, u32[]{:S(2)}) collective-permute-start(bf16[256,512]{1,0:T(8,128)(2,1)S(1)} %bitcast.189), channel_id=1, source_target_pairs={{0,128},{128,0},{1,129},{129,1},{2,130},{130,2},{3,131},{131,3},{4... | collective-permute-start | bytes 786440 | tf_op jit(solution)/shard_map/ppermute | solution.py:21
  46.9 11.5 %collective-permute-start.5 = (bf16[256,512]{1,0:T(8,128)(2,1)S(1)}, bf16[256,512]{1,0:T(8,128)(2,1)S(1)}, u32[]{:S(2)}, u32[]{:S(2)}) collective-permute-start(bf16[256,512]{1,0:T(8,128)(2,1)S(1)} %bitcast.190), channel_id=1, source_target_pairs={{0,2},{2,0},{1,3},{3,1},{4,6},{6,4},{5,7},{7,5},{8,10},{10,8},{9,1... | collective-permute-start | bytes 786440 | tf_op jit(solution)/shard_map/ppermute | solution.py:21
  59.3 1.9 %collective-permute-start.7 = (bf16[256,896]{1,0:T(8,128)(2,1)S(1)}, bf16[256,896]{1,0:T(8,128)(2,1)S(1)}, u32[]{:S(2)}, u32[]{:S(2)}) collective-permute-start(bf16[256,896]{1,0:T(8,128)(2,1)S(1)} %fusion.13), channel_id=1, source_target_pairs={{0,1},{1,0},{2,3},{3,2},{4,5},{5,4},{6,7},{7,6},{8,9},{9,8},{10,11... | collective-permute-start | bytes 1376264 | tf_op jit(solution)/shard_map/ppermute | solution.py:21
  62.5 16.0 %copy-start.7 = (s32[256]{0:T(256)S(1)}, s32[256]{0:T(256)}, u32[]{:S(2)}) copy-start(s32[256]{0:T(256)} %param.20) | copy-start | bytes 3076
  62.5 22.3 %all-to-all-start.2 = ((bf16[8,32,896]{2,1,0:T(8,128)(2,1)}), bf16[8,32,896]{2,1,0:T(8,128)(2,1)S(1)}, u32[]{:S(2)}, u32[]{:S(2)}) async-start(bf16[8,32,896]{2,1,0:T(8,128)(2,1)} %bitcast.15), calls=%async_computation.2 | async-start | bytes 917504 | tf_op jit(solution)/shard_map/all_to_all | solution.py:25
  69.8 8.5 %collective-permute-start.8 = (s32[32,8]{0,1:T(8,128)S(1)}, s32[32,8]{0,1:T(8,128)S(1)}, u32[]{:S(2)}, u32[]{:S(2)}) collective-permute-start(s32[32,8]{0,1:T(8,128)S(1)} %copy-done.6), channel_id=1, source_target_pairs={{0,0},{1,128},{128,1},{129,129},{2,2},{3,130},{130,3},{131,131},{4... | collective-permute-start | bytes 3080 | tf_op jit(solution)/shard_map/ppermute | solution.py:127
  72.9 56.6 %collective-permute-start.13 = (bf16[256,896]{1,0:T(8,128)(2,1)}, bf16[256,896]{1,0:T(8,128)(2,1)}, u32[]{:S(2)}, u32[]{:S(2)}) collective-permute-start(bf16[256,896]{1,0:T(8,128)(2,1)} %get-tuple-element.50), channel_id=1, source_target_pairs={{0,1},{1,0},{2,3},{3,2},{4,5},{5,4},{6,7},{7,6},{8,9},{9,8},{10,11... | collective-permute-start | bytes 1376264 | tf_op jit(solution)/shard_map/ppermute | solution.py:21
  77.0 56.6 %collective-permute-start.18 = (bf16[256,896]{1,0:T(8,128)(2,1)}, bf16[256,896]{1,0:T(8,128)(2,1)}, u32[]{:S(2)}, u32[]{:S(2)}) collective-permute-start(bf16[256,896]{1,0:T(8,128)(2,1)} %get-tuple-element.48), channel_id=1, source_target_pairs={{0,2},{1,3},{2,0},{3,1},{4,6},{5,7},{6,4},{7,5},{8,10},{9,11},{10,... | collective-permute-start | bytes 1376264 | tf_op jit(solution)/shard_map/ppermute | solution.py:21
  77.2 57.7 %collective-permute-start.20 = (bf16[256,896]{1,0:T(8,128)(2,1)}, bf16[256,896]{1,0:T(8,128)(2,1)}, u32[]{:S(2)}, u32[]{:S(2)}) collective-permute-start(bf16[256,896]{1,0:T(8,128)(2,1)} %get-tuple-element.49), channel_id=1, source_target_pairs={{0,3},{1,2},{2,1},{3,0},{4,7},{5,6},{6,5},{7,4},{8,11},{9,10},{10,... | collective-permute-start | bytes 1376264 | tf_op jit(solution)/shard_map/ppermute | solution.py:21
  84.8 20.5 %collective-permute-start.15 = (bf16[32,896]{1,0:T(8,128)(2,1)S(1)}, bf16[32,896]{1,0:T(8,128)(2,1)S(1)}, u32[]{:S(2)}, u32[]{:S(2)}) collective-permute-start(bf16[32,896]{1,0:T(8,128)(2,1)S(1)} %reduce_sum.122), channel_id=1, source_target_pairs={{0,2},{2,0},{1,3},{3,1},{4,6},{6,4},{5,7},{7,5},{8,10},{10,8},{9,1... | collective-permute-start | bytes 172040 | tf_op jit(solution)/shard_map/ppermute | solution.py:21
  86.8 26.4 %all-to-all-start.3 = ((bf16[64,4,896]{2,1,0:T(4,128)(2,1)}), bf16[64,4,896]{2,1,0:T(4,128)(2,1)S(1)}, u32[]{:S(2)}, u32[]{:S(2)}) async-start(bf16[64,4,896]{2,1,0:T(4,128)(2,1)} %reshape.168), calls=%async_computation.3 | async-start | bytes 917504 | tf_op jit(solution)/shard_map/all_to_all | solution.py:25
  105.3 6.6 %collective-permute-start.16 = (bf16[32,1792]{1,0:T(8,128)(2,1)S(1)}, bf16[32,1792]{1,0:T(8,128)(2,1)S(1)}, u32[]{:S(2)}, u32[]{:S(2)}) collective-permute-start(bf16[32,1792]{1,0:T(8,128)(2,1)S(1)} %pad_maximum_fusion.5), channel_id=1, source_target_pairs={{0,128},{128,0},{1,129},{129,1},{2,130},{130,2},{3,131},{131,3},{4... | collective-permute-start | bytes 344072 | tf_op jit(solution)/shard_map/ppermute | solution.py:21
  113.3 3.2 %copy-start.2 = (bf16[2,896,256]{2,1,0:T(8,128)(2,1)S(1)}, bf16[2,896,256]{2,1,0:T(8,128)(2,1)}, u32[]{:S(2)}) copy-start(bf16[2,896,256]{2,1,0:T(8,128)(2,1)} %get-tuple-element.32) | copy-start | bytes 2752516
  113.3 10.0 %collective-permute-start.9 = (bf16[2,128,896]{2,1,0:T(8,128)(2,1)S(1)}, bf16[2,128,896]{2,1,0:T(8,128)(2,1)S(1)}, u32[]{:S(2)}, u32[]{:S(2)}) collective-permute-start(bf16[2,128,896]{2,1,0:T(8,128)(2,1)S(1)} %reshape.172), channel_id=1, source_target_pairs={{0,2},{2,0},{1,3},{3,1},{4,6},{6,4},{5,7},{7,5},{8,10},{10,8},{9,1... | collective-permute-start | bytes 1376264 | tf_op jit(solution)/shard_map/ppermute | solution.py:21
  114.0 9.5 %collective-permute-start.10 = (bf16[2,128,896]{2,1,0:T(8,128)(2,1)S(1)}, bf16[2,128,896]{2,1,0:T(8,128)(2,1)S(1)}, u32[]{:S(2)}, u32[]{:S(2)}) collective-permute-start(bf16[2,128,896]{2,1,0:T(8,128)(2,1)S(1)} %reshape.172), channel_id=1, source_target_pairs={{0,1},{1,0},{2,3},{3,2},{4,5},{5,4},{6,7},{7,6},{8,9},{9,8},{10,11... | collective-permute-start | bytes 1376264 | tf_op jit(solution)/shard_map/ppermute | solution.py:21
  116.8 7.1 %copy-start.1 = (bf16[2,896,256]{2,1,0:T(8,128)(2,1)S(1)}, bf16[2,896,256]{2,1,0:T(8,128)(2,1)}, u32[]{:S(2)}) copy-start(bf16[2,896,256]{2,1,0:T(8,128)(2,1)} %get-tuple-element.30) | copy-start | bytes 2752516
  123.3 2.5 %collective-permute-start.11 = (bf16[2,128,896]{2,1,0:T(8,128)(2,1)S(1)}, bf16[2,128,896]{2,1,0:T(8,128)(2,1)S(1)}, u32[]{:S(2)}, u32[]{:S(2)}) collective-permute-start(bf16[2,128,896]{2,1,0:T(8,128)(2,1)S(1)} %collective-permute-done.9), channel_id=1, source_target_pairs={{0,1},{1,0},{2,3},{3,2},{4,5},{5,4},{6,7},{7,6},{8,9},{9,8},{10,11... | collective-permute-start | bytes 1376264 | tf_op jit(solution)/shard_map/ppermute | solution.py:21
  124.1 1.2 copy-start.3
  127.0 2.5 %collective-permute-start.12 = (bf16[256,256]{1,0:T(8,128)(2,1)S(1)}, bf16[256,256]{1,0:T(8,128)(2,1)S(1)}, u32[]{:S(2)}, u32[]{:S(2)}) collective-permute-start(bf16[256,256]{1,0:T(8,128)(2,1)S(1)} %pad_maximum_fusion.4), channel_id=1, source_target_pairs={{0,1},{1,0},{2,3},{3,2},{4,5},{5,4},{6,7},{7,6},{8,9},{9,8},{10,11... | collective-permute-start | bytes 393224 | tf_op jit(solution)/shard_map/ppermute | solution.py:21
  127.6 5.5 %collective-permute-start.14 = (bf16[256,256]{1,0:T(8,128)(2,1)S(1)}, bf16[256,256]{1,0:T(8,128)(2,1)S(1)}, u32[]{:S(2)}, u32[]{:S(2)}) collective-permute-start(bf16[256,256]{1,0:T(8,128)(2,1)S(1)} %pad_maximum_fusion.4), channel_id=1, source_target_pairs={{0,2},{2,0},{1,3},{3,1},{4,6},{6,4},{5,7},{7,5},{8,10},{10,8},{9,1... | collective-permute-start | bytes 393224 | tf_op jit(solution)/shard_map/ppermute | solution.py:21
  133.1 12.1 %collective-permute-start.17 = (bf16[32,3584]{1,0:T(8,128)(2,1)S(1)}, bf16[32,3584]{1,0:T(8,128)(2,1)S(1)}, u32[]{:S(2)}, u32[]{:S(2)}) collective-permute-start(bf16[32,3584]{1,0:T(8,128)(2,1)S(1)} %pad_maximum_fusion.3), channel_id=1, source_target_pairs={{0,1},{1,0},{2,3},{3,2},{4,5},{5,4},{6,7},{7,6},{8,9},{9,8},{10,11... | collective-permute-start | bytes 688136 | tf_op jit(solution)/shard_map/ppermute | solution.py:21
  133.1 1.8 %collective-permute-start.19 = (bf16[256,256]{1,0:T(8,128)(2,1)S(1)}, bf16[256,256]{1,0:T(8,128)(2,1)S(1)}, u32[]{:S(2)}, u32[]{:S(2)}) collective-permute-start(bf16[256,256]{1,0:T(8,128)(2,1)S(1)} %collective-permute-done.14), channel_id=1, source_target_pairs={{0,1},{1,0},{2,3},{3,2},{4,5},{5,4},{6,7},{7,6},{8,9},{9,8},{10,11... | collective-permute-start | bytes 393224 | tf_op jit(solution)/shard_map/ppermute | solution.py:21
  137.2 26.8 %all-to-all-start.4 = ((bf16[64,4,896]{2,1,0:T(4,128)(2,1)}), bf16[64,4,896]{2,1,0:T(4,128)(2,1)S(1)}, u32[]{:S(2)}, u32[]{:S(2)}) async-start(bf16[64,4,896]{2,1,0:T(4,128)(2,1)} %reshape.173), calls=%async_computation.4 | async-start | bytes 917504 | tf_op jit(solution)/shard_map/all_to_all | solution.py:25
